TPU v7x, 32 devices: a whole 2x2x4 slice. The times are simulated.
32 devices in a mesh: groups: 2 (over y), fsdp: 8 (over z, x), tp: 2 (over core).
Axes of the slice: x: 2, y: 2, z: 4, core: 2. Of those that a mesh axis runs over, the one named last changes fastest.
Arguments:
- tokens: bfloat16 [64, 8192], P(('groups', 'fsdp'), 'tp'), parts along dimension 0, may hold values from -6 to 6
- lengths: int32 [16], P(('groups', 'fsdp')), parts along dimension 0, may hold values from 1 to 4, as said below
- norm_gain: bfloat16 [8192], replicated, may hold values from 0.099609375 to 1.8984375
- gate_codes: bfloat16 [8192, 16384], P('fsdp', 'tp'), may hold values from -4 to 4
- gate_scales: bfloat16 [64, 128], P('fsdp', 'tp'), may hold values from 0.004486084 to 0.029907227
- up_codes: bfloat16 [8192, 16384], P('fsdp', 'tp'), may hold values from -4 to 4
- up_scales: bfloat16 [64, 128], P('fsdp', 'tp'), may hold values from 0.004486084 to 0.029907227
- down_codes: bfloat16 [8192, 16384], P('fsdp', 'tp'), may hold values from -4 to 4
- down_scales: bfloat16 [64, 128], P('fsdp', 'tp'), may hold values from 0.0029907227 to 0.021972656
- value_head: float32 [8192], P('tp'), may hold values from -0.0625 to 0.0625
Outputs:
- layer_out: bfloat16 [64, 8192], P(('groups', 'fsdp'), 'tp'), parts along dimension 0
- values: float32 [64], P(('groups', 'fsdp')), parts along dimension 0
There are 2 independent parts, one for each index of `groups`. A program takes and returns all parts, laid end to end along the dimension named above; an argument that names none is the same for every part. Nothing has to cross between parts.
Inputs may be any that keep to these rules, and one draw needn't show every extreme that they name: `lengths`: some index of fsdp has all 4 rows live.
All inputs are finite; a program needn't handle non-finite values.
Results may differ from a plain program's by a relative error of at most 0.0094.
Values may be sent and summed in bfloat16 or wider, within the bound.
No kernel may reach another device: no remote copies, remote signals or barrier semaphores. Data moves between devices by JAX's collectives and lax.ppermute only.
A program may use at most 384 MiB of HBM per device.

v0:
```python
import jax
import jax.numpy as jnp
from jax import lax
from jax.sharding import PartitionSpec as P


def dequantize(codes, scales):
    tile_rows = codes.shape[0] // scales.shape[0]
    tile_cols = codes.shape[1] // scales.shape[1]
    blocks = codes.astype(jnp.float32).reshape(
        scales.shape[0], tile_rows, scales.shape[1], tile_cols
    )
    scaled = blocks * scales.astype(jnp.float32)[:, None, :, None]
    return scaled.reshape(codes.shape).astype(jnp.bfloat16)


def rms_normed(rows_in, norm_gain):
    resid = rows_in.astype(jnp.float32)
    mean_sq = jnp.mean(resid * resid, axis=-1, keepdims=True)
    return (resid * lax.rsqrt(mean_sq + 1e-05) * norm_gain.astype(jnp.float32)).astype(jnp.bfloat16)


def gated_hidden(normed, gate_local, gate_scl, up_local, up_scl):
    gate_act = jnp.dot(normed, dequantize(gate_local, gate_scl), preferred_element_type=jnp.float32)
    up_act = jnp.dot(normed, dequantize(up_local, up_scl), preferred_element_type=jnp.float32)
    return (jax.nn.silu(gate_act) * up_act).astype(jnp.bfloat16)


def body(
    tokens,
    lengths,
    norm_gain,
    gate_codes,
    gate_scales,
    up_codes,
    up_scales,
    down_codes,
    down_scales,
    value_head,
):
    feature_rows = lax.all_gather(tokens, "tp", axis=1, tiled=True)
    all_rows = lax.all_gather(feature_rows, "fsdp", axis=0, tiled=True)
    normed = rms_normed(all_rows, norm_gain)
    gate_local, gate_scl, up_local, up_scl, down_local, down_scl = (
        lax.all_to_all(gate_codes, "fsdp", split_axis=1, concat_axis=0, tiled=True),
        lax.all_to_all(gate_scales, "fsdp", split_axis=1, concat_axis=0, tiled=True),
        lax.all_to_all(up_codes, "fsdp", split_axis=1, concat_axis=0, tiled=True),
        lax.all_to_all(up_scales, "fsdp", split_axis=1, concat_axis=0, tiled=True),
        lax.all_to_all(down_codes, "fsdp", split_axis=1, concat_axis=0, tiled=True),
        lax.all_to_all(down_scales, "fsdp", split_axis=1, concat_axis=0, tiled=True),
    )
    hidden = gated_hidden(normed, gate_local, gate_scl, up_local, up_scl)
    down_weight = dequantize(down_local, down_scl)
    group_sum = lax.psum_scatter(
        lax.dot_general(
            hidden, down_weight, (((1,), (1,)), ((), ())), preferred_element_type=jnp.float32
        ),
        "fsdp",
        scatter_dimension=0,
        tiled=True,
    )
    branch = lax.psum_scatter(group_sum, "tp", scatter_dimension=1, tiled=True)
    layer_out = (tokens.astype(jnp.float32) + branch).astype(jnp.bfloat16)
    head_part = jnp.dot(layer_out.astype(jnp.float32), value_head, precision=lax.Precision.HIGHEST)
    head_total = lax.psum(head_part, "tp")
    live = jnp.arange(tokens.shape[0]) < lengths[0]
    values = jnp.where(live, head_total, jnp.float32(0.0))
    return (layer_out, values)


def solution(mesh):
    placed = (
        P(("groups", "fsdp"), "tp"),
        P(("groups", "fsdp")),
        P(),
        P("fsdp", "tp"),
        P("fsdp", "tp"),
        P("fsdp", "tp"),
        P("fsdp", "tp"),
        P("fsdp", "tp"),
        P("fsdp", "tp"),
        P("tp"),
    )
    return jax.shard_map(
        body,
        mesh=mesh,
        in_specs=placed,
        out_specs=(P(("groups", "fsdp"), "tp"), P(("groups", "fsdp"))),
        check_vma=False,
    )
```

profile of v0, /device:TPU:0, one launch (start us, length us, event | category | flops | bytes accessed | tf_op | source)
XLA Modules:
  0.0 1585.7 jit_solution(5458929770839927547)
XLA Ops:
  8.6 7.3 all-to-all-start.1
  35.6 22.4 %copy.30 = bf16[1024,8192]{0,1:T(8,128)(2,1)} copy(bf16[1024,8192]{1,0:T(8,128)(2,1)} %param.13) | data formatting | bytes 33554432 | tf_op args[3]
  58.0 5.9 all-to-all-start
  63.9 22.4 %copy.35 = bf16[1024,8192]{0,1:T(8,128)(2,1)} copy(bf16[1024,8192]{1,0:T(8,128)(2,1)} %param.15) | data formatting | bytes 33554432 | tf_op args[5]
  86.3 337.9 %all-to-all-done = bf16[1024,8,1024]{0,2,1:T(8,128)(2,1)} async-done(((bf16[1024,8,1024]{0,2,1:T(8,128)(2,1)}), bf16[1024,8,1024]{0,2,1:T(8,128)(2,1)}, u32[]{:S(2)}, u32[]{:S(2)}) %all-to-all-start) | async-done | bytes 16777248 | tf_op jit(solution)/shard_map/all_to_all | solution.py:45
  429.9 22.4 %copy.40 = bf16[1024,8192]{0,1:T(8,128)(2,1)} copy(bf16[1024,8192]{1,0:T(8,128)(2,1)} %param.17) | data formatting | bytes 33554432 | tf_op args[7]
  452.4 338.6 %all-to-all-done.2 = bf16[1024,8,1024]{0,2,1:T(8,128)(2,1)} async-done(((bf16[1024,8,1024]{0,2,1:T(8,128)(2,1)}), bf16[1024,8,1024]{0,2,1:T(8,128)(2,1)}, u32[]{:S(2)}, u32[]{:S(2)}) %all-to-all-start.2) | async-done | bytes 16777248 | tf_op jit(solution)/shard_map/all_to_all | solution.py:47
  798.8 381.1 %all-gather = bf16[8,4,8192]{2,1,0:T(4,128)(2,1)S(1)} all-gather(bf16[1,4,8192]{2,1,0:T(4,128)(2,1)S(1)} %bitcast.69), channel_id=1, replica_groups=mesh['groups'=2,'fsdp'=8,'tp'=2] {'fsdp'}, dimensions={0}, use_global_device_ids=true | all-gather | bytes 589824 | tf_op jit(solution)/shard_map/all_gather | solution.py:42
  1182.3 18.6 %convert_bitcast_fusion.2 = f32[8,1024,1024]{1,2,0:T(8,128)} fusion(bf16[1024,8,1024]{0,2,1:T(8,128)(2,1)} %all-to-all-done), kind=kLoop, calls=%fused_computation.8 | loop fusion | flops 8388608 | bytes 50331648 | tf_op jit(solution)/shard_map/convert_element_type | solution.py:10
  1200.9 31.9 %copy.31 = f32[8,1024,1024]{2,1,0:T(8,128)} copy(f32[8,1024,1024]{1,2,0:T(8,128)} %convert_bitcast_fusion.2) | data formatting | bytes 67108864 | tf_op jit(solution)/shard_map/convert_element_type | solution.py:10
  1232.8 18.6 %convert_bitcast_fusion.1 = f32[8,1024,1024]{1,2,0:T(8,128)} fusion(bf16[1024,8,1024]{0,2,1:T(8,128)(2,1)} %all-to-all-done.2), kind=kLoop, calls=%fused_computation.7 | loop fusion | flops 8388608 | bytes 50331648 | tf_op jit(solution)/shard_map/convert_element_type | solution.py:10
  1251.3 31.9 %copy.36 = f32[8,1024,1024]{2,1,0:T(8,128)} copy(f32[8,1024,1024]{1,2,0:T(8,128)} %convert_bitcast_fusion.1) | data formatting | bytes 67108864 | tf_op jit(solution)/shard_map/convert_element_type | solution.py:10
  1283.2 18.6 %convert_bitcast_fusion = f32[8,1024,1024]{1,2,0:T(8,128)} fusion(bf16[1024,8,1024]{0,2,1:T(8,128)(2,1)} %all-to-all-done.4), kind=kLoop, calls=%fused_computation.6 | loop fusion | flops 8388608 | bytes 50331648 | tf_op jit(solution)/shard_map/convert_element_type | solution.py:10
  1301.8 31.9 %copy.41 = f32[8,1024,1024]{2,1,0:T(8,128)} copy(f32[8,1024,1024]{1,2,0:T(8,128)} %convert_bitcast_fusion) | data formatting | bytes 67108864 | tf_op jit(solution)/shard_map/convert_element_type | solution.py:10
  1333.7 11.1 mul.64
  1344.7 29.1 %fusion.2 = bf16[8192,1024]{1,0:T(8,128)(2,1)} fusion(f32[1024,8,8,128]{3,2,1,0:T(8,128)} %bitcast.61, f32[8,1024,1024]{2,1,0:T(8,128)} %copy.31), kind=kLoop, calls=%fused_computation.5 | loop fusion | flops 16777216 | bytes 83886080 | tf_op jit(solution)/shard_map/convert_element_type | solution.py:14
  1373.8 11.2 mul.68
  1385.0 29.2 %fusion.1 = bf16[8192,1024]{1,0:T(8,128)(2,1)} fusion(f32[1024,8,8,128]{3,2,1,0:T(8,128)} %bitcast.62, f32[8,1024,1024]{2,1,0:T(8,128)} %copy.36), kind=kLoop, calls=%fused_computation.3 | loop fusion | flops 16777216 | bytes 83886080 | tf_op jit(solution)/shard_map/convert_element_type | solution.py:14
  1414.2 9.0 fusion.4
  1427.9 11.1 mul.72
  1439.0 29.1 %fusion = bf16[8192,1024]{1,0:T(8,128)(2,1)} fusion(f32[1024,8,8,128]{3,2,1,0:T(8,128)} %bitcast.63, f32[8,1024,1024]{2,1,0:T(8,128)} %copy.41), kind=kLoop, calls=%fused_computation.1 | loop fusion | flops 16777216 | bytes 83886080 | tf_op jit(solution)/shard_map/convert_element_type | solution.py:14
  1468.2 11.8 fusion.5
  1481.2 76.0 %all-reduce.3.cloned.1.call-done = f32[32,8192]{1,0:T(8,128)} async-done(((f32[32,8192]{1,0:T(8,128)}), f32[32,8192]{1,0:T(8,128)}) %all-reduce.3.cloned.1.call-update) | async-done | bytes 1048592
  1560.9 11.8 reduce-scatter.4.cloned.1.call-done
  (59 shorter events, 51.4 us)
Async XLA Ops:
  7.2 1567.8 %copy-start = (f32[4096]{0:T(1024)S(1)}, f32[4096]{0:T(1024)}, u32[]{:S(2)}) copy-start(f32[4096]{0:T(1024)} %param.19) | copy-start | bytes 49156
  8.6 13.8 all-to-all-start.1
  22.4 9.9 all-to-all-start.3
  32.2 25.7 %all-to-all-start.5 = ((bf16[8,8,8]{0,2,1:T(8,128)(2,1)}), bf16[8,8,8]{0,2,1:T(8,128)(2,1)S(1)}, u32[]{:S(2)}, u32[]{:S(2)}) async-start(bf16[8,8,8]{0,2,1:T(8,128)(2,1)} %bitcast.16), calls=%async_computation.5 | async-start | bytes 32768 | tf_op jit(solution)/shard_map/all_to_all | solution.py:50
  58.0 366.2 %all-to-all-start = ((bf16[1024,8,1024]{0,2,1:T(8,128)(2,1)}), bf16[1024,8,1024]{0,2,1:T(8,128)(2,1)}, u32[]{:S(2)}, u32[]{:S(2)}) async-start(bf16[1024,8,1024]{0,2,1:T(8,128)(2,1)} %bitcast.65), calls=%async_computation | async-start | bytes 33554432 | tf_op jit(solution)/shard_map/all_to_all | solution.py:45
  424.2 366.7 %all-to-all-start.2 = ((bf16[1024,8,1024]{0,2,1:T(8,128)(2,1)}), bf16[1024,8,1024]{0,2,1:T(8,128)(2,1)}, u32[]{:S(2)}, u32[]{:S(2)}) async-start(bf16[1024,8,1024]{0,2,1:T(8,128)(2,1)} %bitcast.66), calls=%async_computation.2 | async-start | bytes 33554432 | tf_op jit(solution)/shard_map/all_to_all | solution.py:47
  791.0 5.9 copy-start.6
  791.0 389.0 %copy-start.9 = (bf16[8192]{0:T(1024)(128)(2,1)S(1)}, bf16[8192]{0:T(1024)(128)(2,1)}, u32[]{:S(2)}) copy-start(bf16[8192]{0:T(1024)(128)(2,1)} %param.12) | copy-start | bytes 49156
  791.0 492.2 %all-to-all-start.4 = ((bf16[1024,8,1024]{0,2,1:T(8,128)(2,1)}), bf16[1024,8,1024]{0,2,1:T(8,128)(2,1)}, u32[]{:S(2)}, u32[]{:S(2)}) async-start(bf16[1024,8,1024]{0,2,1:T(8,128)(2,1)} %bitcast.64), calls=%async_computation.4 | async-start | bytes 33554432 | tf_op jit(solution)/shard_map/all_to_all | solution.py:49
  796.9 760.4 %all-reduce.3.cloned.1.call-start = ((), (), s32[]{:S(2)}) async-start(), calls=%async_computation.8 | async-start | bytes 2097152
  1180.0 20.9 %copy-start.2 = (f32[32,8192]{1,0:T(8,128)}, f32[32,8192]{1,0:T(8,128)S(1)}, u32[]{:S(2)}) copy-start(f32[32,8192]{1,0:T(8,128)S(1)} %reshape.81) | copy-start | bytes 3145732
  1385.0 29.2 %copy-start.3 = (f32[32,8192]{1,0:T(8,128)S(1)}, f32[32,8192]{1,0:T(8,128)}, u32[]{:S(2)}) copy-start(f32[32,8192]{1,0:T(8,128)} %copy-done.2) | copy-start | bytes 3145732
  1385.0 29.2 %copy-start.4 = (f32[8192]{0:T(1024)S(1)}, f32[8192]{0:T(1024)}, u32[]{:S(2)}) copy-start(f32[8192]{0:T(1024)} %convert_element_type.102) | copy-start | bytes 98308
  1385.0 29.2 %copy-start.10 = (f32[32]{0:T(128)S(1)}, f32[32]{0:T(128)}, u32[]{:S(2)}) copy-start(f32[32]{0:T(128)} %add_rsqrt_fusion) | copy-start | bytes 388
  1414.2 10.5 copy-start.1
  1424.8 3.1 copy-start.5
  1468.1 11.9 copy-start.11
  1468.2 106.8 %copy-start.7 = (bf16[4,4096]{1,0:T(4,128)(2,1)S(1)}, bf16[4,4096]{1,0:T(4,128)(2,1)}, u32[]{:S(2)}) copy-start(bf16[4,4096]{1,0:T(4,128)(2,1)} %param.10) | copy-start | bytes 98308
  1479.9 92.8 %reduce-scatter.4.cloned.1.call-start = ((), (), s32[]{:S(2)}) async-start(), calls=%async_computation.7 | async-start | bytes 6291456
  1575.0 3.9 copy-start.8
Sparse Core Ops, SparseCore 0:
  1480.1 77.1 all-reduce.2
  1561.1 11.6 reduce-scatter.3
where the time goes:
time: 1590 us
  waiting for transfers between devices  775 us (49%)
  blocking collectives  385 us (24%)
  local copies, waits for them, and re-layouts  209 us (13%)
  other arithmetic  145 us (9%)
  starting transfers between devices  31.5 us (2%)
  matrix products  24.1 us (2%)
    all_gather x1, blocking collectives, body(): all_rows = lax.all_gather(feature_rows, 'fsdp', axis=0, tiled=True)  381 us
    all_to_all x1, waiting for transfers between devices, body(): lax.all_to_all(up_codes, 'fsdp', split_axis=1, concat_axis=0, tiled=True)  339 us
    all_to_all x1, waiting for transfers between devices, body(): lax.all_to_all(gate_codes, 'fsdp', split_axis=1, concat_axis=0, tiled=True)  338 us
    convert_element_type x3, local copies, waits for them, and re-layouts, dequantize(): codes.astype(jnp.float32)  95.7 us
    unnamed x4, waiting for transfers between devices  87.9 us
    convert_element_type x3, other arithmetic, dequantize(): return scaled.reshape(codes.shape).astype(jnp.bfloat16)  87.4 us
    unnamed x34, local copies, waits for them, and re-layouts  79.4 us
    convert_element_type x3, other arithmetic, dequantize(): codes.astype(jnp.float32)  55.7 us
  transfers between devices with their start and end apart: 8, of which 6 were waited for; matrix products, arithmetic and copies ran while one was open for 11% of the time, Pallas kernels for 0%

commit v1 on v0

v1 whole, which is shorter than its diff:
```python
import functools

import jax
import jax.numpy as jnp
from jax import lax
from jax.experimental import pallas as pl
from jax.experimental.pallas import tpu as pltpu
from jax.sharding import PartitionSpec as P

TILE = 128
BF16, F32 = jnp.bfloat16, jnp.float32
VMEM_SPEC = pl.BlockSpec(memory_space=pltpu.VMEM)
SMEM_SPEC = pl.BlockSpec(memory_space=pltpu.SMEM)


def params(mib):
    return pltpu.CompilerParams(vmem_limit_bytes=mib << 20)


def dequantize(codes, scales):
    tile_rows = codes.shape[0] // scales.shape[0]
    tile_cols = codes.shape[1] // scales.shape[1]
    blocks = codes.astype(F32).reshape(scales.shape[0], tile_rows, scales.shape[1], tile_cols)
    scaled = blocks * scales.astype(F32)[:, None, :, None]
    return scaled.reshape(codes.shape).astype(BF16)


def rms_normed(rows_in, norm_gain):
    resid = rows_in.astype(F32)
    mean_sq = jnp.mean(resid * resid, axis=-1, keepdims=True)
    return (resid * lax.rsqrt(mean_sq + 1e-05) * norm_gain.astype(F32)).astype(BF16)


def body_any(tokens, lengths, norm_gain, gate_codes, gate_scales, up_codes, up_scales, down_codes, down_scales, value_head):
    rows = tokens.shape[0]
    feature_rows = lax.all_gather(tokens, "tp", axis=1, tiled=True)
    normed = rms_normed(feature_rows, norm_gain)
    x = lax.all_to_all(normed, "fsdp", split_axis=1, concat_axis=0, tiled=True)
    gate = jnp.dot(x, dequantize(gate_codes, gate_scales), preferred_element_type=F32)
    up = jnp.dot(x, dequantize(up_codes, up_scales), preferred_element_type=F32)
    gate = lax.psum_scatter(gate, "fsdp", scatter_dimension=1, tiled=True)
    up = lax.psum_scatter(up, "fsdp", scatter_dimension=1, tiled=True)
    hidden = (jax.nn.silu(gate) * up).astype(BF16)
    hidden = lax.all_gather(hidden, "fsdp", axis=1, tiled=True)
    part = lax.dot_general(
        hidden, dequantize(down_codes, down_scales), (((1,), (1,)), ((), ())), preferred_element_type=F32
    )
    part = lax.all_to_all(part, "fsdp", split_axis=0, concat_axis=1, tiled=True)
    branch = lax.psum_scatter(part, "tp", scatter_dimension=1, tiled=True)
    layer_out = (tokens.astype(F32) + branch).astype(BF16)
    head = jnp.dot(layer_out.astype(F32), value_head, precision=lax.Precision.HIGHEST)
    head = lax.psum(head, "tp")
    live = jnp.arange(rows) < lengths[0]
    return layer_out, jnp.where(live, head, F32(0.0))


def norm_kernel(tok_ref, gain_ref, out_ref):
    n, _, width = out_ref.shape
    resid = tok_ref[...].astype(F32)
    mean_sq = jnp.mean(resid * resid, axis=-1, keepdims=True)
    inv = lax.rsqrt(mean_sq + 1e-05)
    gain = gain_ref[...].astype(F32)
    for c in range(n):
        cols = slice(c * width, (c + 1) * width)
        out_ref[c] = (resid[:, cols] * inv * gain[:, cols]).astype(BF16)


def gate_up_weights_kernel(g_ref, scl_ref, gate_ref, up_ref, out_ref):
    k, blocks, per = pl.program_id(0), out_ref.shape[0], out_ref.shape[2] // (2 * TILE)
    base = g_ref[0] * (blocks * per)
    rows = pl.ds(pl.multiple_of(k * TILE, TILE), TILE)
    for m, ref in enumerate((gate_ref, up_ref)):
        for b in range(blocks):
            for i in range(per):
                j = b * per + i
                scale = scl_ref[m, k, base + j]
                out_ref[b, rows, (m * per + i) * TILE : (m * per + i + 1) * TILE] = (
                    ref[:, j * TILE : (j + 1) * TILE].astype(F32) * scale
                ).astype(BF16)


def down_weights_kernel(g_ref, scl_ref, down_ref, out_ref):
    k, blocks, per = pl.program_id(0), out_ref.shape[0], out_ref.shape[2] // TILE
    base = g_ref[0] * (blocks * per)
    rows = pl.ds(pl.multiple_of(k * TILE, TILE), TILE)
    for b in range(blocks):
        for i in range(per):
            j = b * per + i
            scale = scl_ref[k, base + j]
            out_ref[b, rows, i * TILE : (i + 1) * TILE] = (
                down_ref[:, j * TILE : (j + 1) * TILE].astype(F32) * scale
            ).astype(BF16)


def gate_up_kernel(n, piece, me_ref, x_ref, w_ref, send_ref, keep_ref):
    me = me_ref[0]
    x = x_ref[...]
    for s in range(n // 2):
        for odd, ref in ((1, send_ref), (0, keep_ref)):
            block = piece * n + (me ^ (2 * s + odd))
            ref[s] = jnp.dot(x, w_ref[block], preferred_element_type=F32).astype(ref.dtype)


def pair_sum_kernel(keep_ref, got_ref, own_ref, *send_refs):
    own_ref[...] = keep_ref[0] + got_ref[0].astype(F32)
    for s, ref in enumerate(send_refs, 1):
        ref[...] = (keep_ref[s] + got_ref[s].astype(F32)).astype(BF16)


def hidden_kernel(own_ref, *refs):
    out_ref = refs[-1]
    total = own_ref[...]
    for ref in refs[:-1]:
        total = total + ref[...].astype(F32)
    half = out_ref.shape[-1]
    gate, up = total[:, :half], total[:, half:]
    out_ref[...] = (gate / (1.0 + jnp.exp(-gate)) * up).astype(BF16)


def down_kernel(n, piece, first, me_ref, *refs):
    near, far_ref = refs[: n // 2], refs[n // 2]
    w_ref, out_ref = refs[n // 2 + 1], refs[-1]
    me = me_ref[0]
    total = None if first else refs[n // 2 + 2][...]
    for s in range(n // 2):
        for odd in (0, 1):
            block = piece * n + (me ^ (2 * s + odd))
            h = far_ref[s] if odd else near[s][...]
            part = lax.dot_general(h, w_ref[block], (((1,), (1,)), ((), ())), preferred_element_type=F32)
            total = part if total is None else total + part
    out_ref[...] = total


def final_kernel(place_ref, tok_ref, branch_ref, head_ref, out_ref, values_ref):
    n, rows, width = branch_ref.shape
    half = out_ref.shape[1]
    total = jnp.zeros((rows, 1), F32)
    kept = []
    for c in range(n):
        cols = slice(c * width, (c + 1) * width)
        layer = (tok_ref[:, cols].astype(F32) + branch_ref[c].astype(F32)).astype(BF16)
        kept.append(layer)
        total = total + jnp.sum(layer.astype(F32) * head_ref[:, cols], axis=-1, keepdims=True)
    per = half // width
    for i in range(per):
        out_ref[:, i * width : (i + 1) * width] = jnp.where(place_ref[0] == 0, kept[i], kept[i + per])
    live = lax.broadcasted_iota(jnp.int32, (rows, 1), 0) < place_ref[1]
    values_ref[...] = jnp.broadcast_to(jnp.where(live, total, 0.0), values_ref.shape)


def body_split(pieces, n, tokens, lengths, norm_gain, gate_codes, gate_scales, up_codes, up_scales, down_codes, down_scales, value_head):
    rows, d_half = tokens.shape
    d, depth, ff_dev = 2 * d_half, gate_codes.shape[0], gate_codes.shape[1]
    group_cols = ff_dev // 2
    width = group_cols // (pieces * n)
    all_rows = 2 * n * rows
    half = n // 2
    me = lax.axis_index("fsdp").astype(jnp.int32).reshape(1)
    group = lax.axis_index("groups").astype(jnp.int32).reshape(1)
    core = lax.axis_index("tp").astype(jnp.int32)

    def swap(x, axis, bit):
        size = 2 if axis != "fsdp" else n
        return lax.ppermute(x, axis, [(i, i ^ bit) for i in range(size)])

    gu_scales = jnp.stack([gate_scales, up_scales]).astype(F32)
    w_gu = pl.pallas_call(
        gate_up_weights_kernel,
        grid_spec=pltpu.PrefetchScalarGridSpec(
            num_scalar_prefetch=1,
            grid=(depth // TILE,),
            in_specs=[
                SMEM_SPEC,
                pl.BlockSpec((TILE, group_cols), lambda k, g: (k, g[0])),
                pl.BlockSpec((TILE, group_cols), lambda k, g: (k, g[0])),
            ],
            out_specs=VMEM_SPEC,
        ),
        out_shape=pltpu.VMEM((pieces * n, depth, 2 * width), BF16),
        compiler_params=params(8),
        cost_estimate=pl.CostEstimate(flops=0, transcendentals=0, bytes_accessed=4 * depth * group_cols),
        name="gate_up_weights",
    )(group, gu_scales, gate_codes, up_codes)
    w_down = pl.pallas_call(
        down_weights_kernel,
        grid_spec=pltpu.PrefetchScalarGridSpec(
            num_scalar_prefetch=1,
            grid=(depth // TILE,),
            in_specs=[SMEM_SPEC, pl.BlockSpec((TILE, group_cols), lambda k, g: (k, g[0]))],
            out_specs=VMEM_SPEC,
        ),
        out_shape=pltpu.VMEM((pieces * n, depth, width), BF16),
        compiler_params=params(8),
        cost_estimate=pl.CostEstimate(flops=0, transcendentals=0, bytes_accessed=2 * depth * group_cols),
        name="down_weights",
    )(group, down_scales.astype(F32), down_codes)

    feature_rows = lax.all_gather(tokens, "tp", axis=1, tiled=True)
    head = lax.all_gather(value_head, "tp", axis=0, tiled=True)
    normed = pl.pallas_call(
        norm_kernel,
        out_shape=jax.ShapeDtypeStruct((n, rows, depth), BF16),
        name="norm",
    )(feature_rows, norm_gain.reshape(1, d))
    x_own = lax.all_to_all(normed, "fsdp", 0, 0, tiled=True).reshape(n * rows, depth)
    x = jnp.concatenate([x_own, swap(x_own, "groups", 1)], axis=0)

    branch = None
    for p in range(pieces):
        send, keep = pl.pallas_call(
            functools.partial(gate_up_kernel, n, p),
            in_specs=[SMEM_SPEC, VMEM_SPEC, VMEM_SPEC],
            out_specs=[VMEM_SPEC, VMEM_SPEC],
            out_shape=[
                jax.ShapeDtypeStruct((half, all_rows, 2 * width), BF16),
                jax.ShapeDtypeStruct((half, all_rows, 2 * width), F32),
            ],
            compiler_params=params(8),
            cost_estimate=pl.CostEstimate(
                flops=2 * all_rows * depth * 2 * width * n, transcendentals=0, bytes_accessed=4 * depth * width * n
            ),
            name=f"gate_up_{p}",
        )(me, x, pltpu.with_memory_space_constraint(w_gu, pltpu.VMEM))
        got = swap(send, "fsdp", 1)
        sums = pl.pallas_call(
            pair_sum_kernel,
            out_shape=[jax.ShapeDtypeStruct((all_rows, 2 * width), F32)]
            + [jax.ShapeDtypeStruct((all_rows, 2 * width), BF16)] * (half - 1),
            name=f"pair_sum_{p}",
        )(keep, got)
        got = [swap(sums[s], "fsdp", 2 * s) for s in range(1, half)]
        hidden = pl.pallas_call(
            hidden_kernel,
            out_shape=jax.ShapeDtypeStruct((all_rows, width), BF16),
            name=f"hidden_{p}",
        )(sums[0], *got)
        near = [hidden] + [swap(hidden, "fsdp", 2 * s) for s in range(1, half)]
        far = swap(jnp.stack(near), "fsdp", 1)
        before = [] if branch is None else [branch]
        branch = pl.pallas_call(
            functools.partial(down_kernel, n, p, branch is None),
            in_specs=[SMEM_SPEC] + [VMEM_SPEC] * (half + 2 + len(before)),
            out_specs=VMEM_SPEC,
            out_shape=jax.ShapeDtypeStruct((all_rows, depth), F32),
            compiler_params=params(8),
            cost_estimate=pl.CostEstimate(
                flops=2 * all_rows * depth * width * n, transcendentals=0, bytes_accessed=2 * depth * width * n
            ),
            name=f"down_{p}",
        )(me, *near, far, pltpu.with_memory_space_constraint(w_down, pltpu.VMEM), *before)

    branch = branch + swap(branch, "tp", 1)
    other = swap(branch[n * rows :].astype(BF16), "groups", 1)
    branch = (branch[: n * rows] + other.astype(F32)).astype(BF16)
    branch = lax.all_to_all(branch.reshape(n, rows, depth), "fsdp", 0, 0, tiled=True)
    place = jnp.stack([core, lengths[0]])
    layer_out, values = pl.pallas_call(
        final_kernel,
        in_specs=[SMEM_SPEC] + [VMEM_SPEC] * 3,
        out_specs=[VMEM_SPEC, VMEM_SPEC],
        out_shape=[jax.ShapeDtypeStruct((rows, d_half), BF16), jax.ShapeDtypeStruct((rows, TILE), F32)],
        name="final",
    )(place, feature_rows, branch, head.reshape(1, d))
    return layer_out, values[:, 0]


def solution(mesh):
    placed = (
        P(("groups", "fsdp"), "tp"),
        P(("groups", "fsdp")),
        P(),
        P("fsdp", "tp"),
        P("fsdp", "tp"),
        P("fsdp", "tp"),
        P("fsdp", "tp"),
        P("fsdp", "tp"),
        P("fsdp", "tp"),
        P("tp"),
    )
    n, pieces = mesh.shape["fsdp"], 2

    def body(*args):
        codes = args[3]
        fits = (
            n == 8
            and mesh.shape["groups"] == 2
            and mesh.shape["tp"] == 2
            and codes.shape[0] % TILE == 0
            and codes.shape[1] % (2 * pieces * n * TILE) == 0
        )
        if fits:
            return body_split(pieces, n, *args)
        return body_any(*args)

    return jax.shard_map(
        body,
        mesh=mesh,
        in_specs=placed,
        out_specs=(P(("groups", "fsdp"), "tp"), P(("groups", "fsdp"))),
        check_vma=False,
    )
```

time: 1590 us -> 124 us (0.08)
  waiting for transfers between devices: 775 us -> 17.8 us
  blocking collectives: 385 us -> 5.47 us
  local copies, waits for them, and re-layouts: 209 us -> 31.4 us
  other arithmetic: 145 us -> 2.91 us
  Pallas kernels: 0 us -> 26.9 us
  matrix products: 24.1 us -> 0 us
    all_to_all x6 -> x2, waiting for transfers between devices: 687 us -> 3.61 us  [the longest x1 3.61 us: body_split(): lax.all_to_all(branch.reshape(n, rows, depth), 'fsdp', 0, 0, tiled=True)]
    all_gather x2, blocking collectives: 383 us -> 5.47 us  [the longest x1 3.51 us: body_split(): feature_rows = lax.all_gather(tokens, 'tp', axis=1, tiled=True)]
    convert_element_type x11 -> x3, other arithmetic: 144 us -> 0.72 us  [the longest x1 0.7 us: body_split(): gu_scales = jnp.stack([gate_scales, up_scales]).astype(F32)]
    convert_element_type x7 -> x0, local copies, waits for them, and re-layouts: 96.6 us -> none  [the longest x3 95.7 us: dequantize(): codes.astype(jnp.float32)]
    unnamed x4 -> x0, waiting for transfers between devices: 87.9 us -> none
    unnamed x34 -> x39, local copies, waits for them, and re-layouts: 79.4 us -> 28 us
    mul x3 -> x0, local copies, waits for them, and re-layouts: 33.4 us -> none  [dequantize(): scaled = blocks * scales.astype(jnp.float32)[:, None, :, None]]
    ppermute x0 -> x19, starting transfers between devices: none -> 27.2 us  [swap(): return lax.ppermute(x, axis, [(i, i ^ bit) for i in range(size)])]
  transfers between devices with their start and end apart: 8 -> 21, of which waited for: 6 -> 6; matrix products, arithmetic and copies ran while one was open for 11% -> 2% of each run, Pallas kernels for 0% -> 17%
where the time goes in v1:
time: 124 us; the launch traced here: 123 us
  starting transfers between devices  37.5 us (30%)
  local copies, waits for them, and re-layouts  31.4 us (25%)
  Pallas kernels  26.9 us (22%)
  waiting for transfers between devices  17.8 us (14%)
  blocking collectives  5.47 us (4%)
  other arithmetic  2.91 us (2%)
  between operations  1.51 us (1%)
    unnamed x39, local copies, waits for them, and re-layouts  28 us
    ppermute x19, starting transfers between devices, swap(): return lax.ppermute(x, axis, [(i, i ^ bit) for i in range(size)])  27.2 us
    ppermute x19, waiting for transfers between devices, swap(): return lax.ppermute(x, axis, [(i, i ^ bit) for i in range(size)])  14.2 us
    pallas_call x1, Pallas kernels, body_split(): pl.pallas_call(gate_up_weights_kernel, grid_spec=pltpu.PrefetchScalarGrid...  7.77 us
    all_to_all x1, starting transfers between devices, body_split(): lax.all_to_all(normed, 'fsdp', 0, 0, tiled=True).reshape(n * rows, depth)  6.97 us
    pallas_call x2, Pallas kernels, body_split(): pl.pallas_call(pair_sum_kernel, out_shape=[jax.ShapeDtypeStruct((all_rows...  3.74 us
    all_to_all x1, waiting for transfers between devices, body_split(): lax.all_to_all(branch.reshape(n, rows, depth), 'fsdp', 0, 0, tiled=True)  3.61 us
    all_gather x1, blocking collectives, body_split(): feature_rows = lax.all_gather(tokens, 'tp', axis=1, tiled=True)  3.51 us
  transfers between devices with their start and end apart: 21, of which 6 were waited for; matrix products, arithmetic and copies ran while one was open for 2% of the time, Pallas kernels for 17%

profile of v1, /device:TPU:0, one launch (start us, length us, event | category | flops | bytes accessed | tf_op | source)
XLA Modules:
  0.0 123.4 jit_solution(5765446125328863835)
XLA Ops:
  0.6 3.5 %all_gather.6.tok_ref = bf16[4,8192]{1,0:T(4,128)(2,1)} all-gather(bf16[4,4096]{1,0:T(4,128)(2,1)} %param.10), channel_id=1, replica_groups=mesh['groups'=2,'fsdp'=8,'tp'=2] {'tp'}, dimensions={1}, use_global_device_ids=true | all-gather | bytes 98304 | tf_op jit(solution)/shard_map/all_gather | solution.py:198
  7.1 7.0 %all-to-all-start = ((bf16[8,4,1024]{2,1,0:T(4,128)(2,1)}), bf16[8,4,1024]{2,1,0:T(4,128)(2,1)S(1)}, u32[]{:S(2)}, u32[]{:S(2)}) async-start(bf16[8,4,1024]{2,1,0:T(4,128)(2,1)} %norm.1), calls=%async_computation | async-start | bytes 131072 | tf_op jit(solution)/shard_map/all_to_all | solution.py:205
  14.8 5.8 %copy-done.3 = bf16[1024,8192]{1,0:T(8,128)(2,1)S(1)} copy-done((bf16[1024,8192]{1,0:T(8,128)(2,1)S(1)}, bf16[1024,8192]{1,0:T(8,128)(2,1)}, u32[]{:S(2)}) %copy-start.3) | copy-done | bytes 16777240
  20.6 7.8 %gate_up_weights.1.w_ref = bf16[16,1024,512]{2,1,0:T(8,128)(2,1)S(1)} custom-call(s32[1]{0:T(128)} %bitcast.2.g_ref, f32[2,8,64]{2,1,0:T(8,128)S(1)} %maximum_convert_fusion.scl_ref, bf16[1024,8192]{1,0:T(8,128)(2,1)S(1)} %copy-done.3, bf16[1024,8192]{1,0:T(8,128)(2,1)} %up_ref.1), custom_call_target="tpu_custom_call" | custom-call | bytes 16777216 | tf_op jit(solution)/shard_map/gate_up_weights/pallas_call | solution.py:167
  28.4 5.8 %copy-done = bf16[16,1024,512]{2,1,0:T(8,128)(2,1)} copy-done((bf16[16,1024,512]{2,1,0:T(8,128)(2,1)}, bf16[16,1024,512]{2,1,0:T(8,128)(2,1)S(1)}, u32[]{:S(2)}) %copy-start) | copy-done | bytes 16777240
  35.7 2.7 %collective-permute-done = bf16[32,1024]{1,0:T(8,128)(2,1)S(1)} collective-permute-done((bf16[32,1024]{1,0:T(8,128)(2,1)S(1)}, bf16[32,1024]{1,0:T(8,128)(2,1)S(1)}, u32[]{:S(2)}, u32[]{:S(2)}) %collective-permute-start) | collective-permute-done | bytes 65568 | tf_op jit(solution)/shard_map/ppermute | solution.py:164
  38.5 5.8 %copy-done.1 = bf16[16,1024,512]{2,1,0:T(8,128)(2,1)S(1)} copy-done((bf16[16,1024,512]{2,1,0:T(8,128)(2,1)S(1)}, bf16[16,1024,512]{2,1,0:T(8,128)(2,1)}, u32[]{:S(2)}) %copy-start.1) | copy-done | bytes 16777240
  46.6 2.0 %collective-permute-start.9 = (bf16[4,64,512]{2,1,0:T(8,128)(2,1)S(1)}, bf16[4,64,512]{2,1,0:T(8,128)(2,1)S(1)}, u32[]{:S(2)}, u32[]{:S(2)}) collective-permute-start(bf16[4,64,512]{2,1,0:T(8,128)(2,1)S(1)} %get-tuple-element.23), channel_id=1, source_target_pairs={{0,2},{2,0},{4,6},{6,4},{8,10},{10,8},{12,14},{14,12},{1,3},{3,1},... | collective-permute-start | bytes 786440 | tf_op jit(solution)/shard_map/ppermute | solution.py:164
  51.0 4.5 %collective-permute-done.9.got_ref = bf16[4,64,512]{2,1,0:T(8,128)(2,1)S(1)} collective-permute-done((bf16[4,64,512]{2,1,0:T(8,128)(2,1)S(1)}, bf16[4,64,512]{2,1,0:T(8,128)(2,1)S(1)}, u32[]{:S(2)}, u32[]{:S(2)}) %collective-permute-start.9) | collective-permute-done | bytes 262176 | tf_op jit(solution)/shard_map/ppermute | solution.py:164
  56.2 1.9 %pair_sum_0.1 = (f32[64,512]{1,0:T(8,128)}, bf16[64,512]{1,0:T(8,128)(2,1)}, bf16[64,512]{1,0:T(8,128)(2,1)}, bf16[64,512]{1,0:T(8,128)(2,1)}) custom-call(f32[4,64,512]{2,1,0:T(8,128)} %copy-done.5, bf16[4,64,512]{2,1,0:T(8,128)(2,1)} %copy-done.9), custom_call_target="tpu_custom_call" | custom-call | tf_op jit(solution)/shard_map/pair_sum_0/pallas_call | solution.py:225
  58.1 2.1 %collective-permute-start.10 = (bf16[64,512]{1,0:T(8,128)(2,1)}, bf16[64,512]{1,0:T(8,128)(2,1)S(1)}, u32[]{:S(2)}, u32[]{:S(2)}) collective-permute-start(bf16[64,512]{1,0:T(8,128)(2,1)} %get-tuple-element.25), channel_id=1, source_target_pairs={{0,4},{2,6},{4,0},{6,2},{8,12},{10,14},{12,8},{14,10},{1,5},{3,7},... | collective-permute-start | bytes 196616 | tf_op jit(solution)/shard_map/ppermute | solution.py:164
  60.2 2.4 %collective-permute-start.11 = (bf16[64,512]{1,0:T(8,128)(2,1)}, bf16[64,512]{1,0:T(8,128)(2,1)S(1)}, u32[]{:S(2)}, u32[]{:S(2)}) collective-permute-start(bf16[64,512]{1,0:T(8,128)(2,1)} %get-tuple-element.26), channel_id=1, source_target_pairs={{0,8},{2,10},{4,12},{6,14},{8,0},{10,2},{12,4},{14,6},{1,9},{3,11}... | collective-permute-start | bytes 196616 | tf_op jit(solution)/shard_map/ppermute | solution.py:164
  66.2 3.3 %collective-permute-start.3 = (bf16[64,512]{1,0:T(8,128)(2,1)}, bf16[64,512]{1,0:T(8,128)(2,1)S(1)}, u32[]{:S(2)}, u32[]{:S(2)}) collective-permute-start(bf16[64,512]{1,0:T(8,128)(2,1)} %get-tuple-element.20), channel_id=1, source_target_pairs={{0,8},{2,10},{4,12},{6,14},{8,0},{10,2},{12,4},{14,6},{1,9},{3,11}... | collective-permute-start | bytes 196616 | tf_op jit(solution)/shard_map/ppermute | solution.py:164
  73.0 3.2 %collective-permute-start.14 = (bf16[64,256]{1,0:T(8,128)(2,1)}, bf16[64,256]{1,0:T(8,128)(2,1)S(1)}, u32[]{:S(2)}, u32[]{:S(2)}) collective-permute-start(bf16[64,256]{1,0:T(8,128)(2,1)} %hidden_0.1.refs_0_), channel_id=1, source_target_pairs={{0,8},{2,10},{4,12},{6,14},{8,0},{10,2},{12,4},{14,6},{1,9},{3,11}... | collective-permute-start | bytes 98312 | tf_op jit(solution)/shard_map/ppermute | solution.py:164
  79.1 3.8 %collective-permute-start.6 = (bf16[64,256]{1,0:T(8,128)(2,1)}, bf16[64,256]{1,0:T(8,128)(2,1)S(1)}, u32[]{:S(2)}, u32[]{:S(2)}) collective-permute-start(bf16[64,256]{1,0:T(8,128)(2,1)} %hidden_1.1.refs_0_), channel_id=1, source_target_pairs={{0,8},{2,10},{4,12},{6,14},{8,0},{10,2},{12,4},{14,6},{1,9},{3,11}... | collective-permute-start | bytes 98312 | tf_op jit(solution)/shard_map/ppermute | solution.py:164
  83.7 2.4 %collective-permute-start.16 = (bf16[4,64,256]{2,1,0:T(8,128)(2,1)S(1)}, bf16[4,64,256]{2,1,0:T(8,128)(2,1)S(1)}, u32[]{:S(2)}, u32[]{:S(2)}) collective-permute-start(bf16[4,64,256]{2,1,0:T(8,128)(2,1)S(1)} %pad_maximum_fusion.1), channel_id=1, source_target_pairs={{0,2},{2,0},{4,6},{6,4},{8,10},{10,8},{12,14},{14,12},{1,3},{3,1},... | collective-permute-start | bytes 393224 | tf_op jit(solution)/shard_map/ppermute | solution.py:164
  86.1 2.7 %collective-permute-done.7.refs_3_ = bf16[64,256]{1,0:T(8,128)(2,1)S(1)} collective-permute-done((bf16[64,256]{1,0:T(8,128)(2,1)}, bf16[64,256]{1,0:T(8,128)(2,1)S(1)}, u32[]{:S(2)}, u32[]{:S(2)}) %collective-permute-start.7) | collective-permute-done | bytes 32800 | tf_op jit(solution)/shard_map/ppermute | solution.py:164
  89.6 1.9 %collective-permute-start.8 = (bf16[4,64,256]{2,1,0:T(8,128)(2,1)S(1)}, bf16[4,64,256]{2,1,0:T(8,128)(2,1)S(1)}, u32[]{:S(2)}, u32[]{:S(2)}) collective-permute-start(bf16[4,64,256]{2,1,0:T(8,128)(2,1)S(1)} %pad_maximum_fusion), channel_id=1, source_target_pairs={{0,2},{2,0},{4,6},{6,4},{8,10},{10,8},{12,14},{14,12},{1,3},{3,1},... | collective-permute-start | bytes 393224 | tf_op jit(solution)/shard_map/ppermute | solution.py:164
  91.5 5.8 %copy-done.2 = bf16[1024,8192]{1,0:T(8,128)(2,1)S(1)} copy-done((bf16[1024,8192]{1,0:T(8,128)(2,1)S(1)}, bf16[1024,8192]{1,0:T(8,128)(2,1)}, u32[]{:S(2)}) %copy-start.2) | copy-done | bytes 16777240
  97.3 3.0 %down_weights.1.refs_5_ = bf16[16,1024,256]{2,1,0:T(8,128)(2,1)S(1)} custom-call(s32[1]{0:T(128)} %bitcast.2.g_ref, f32[8,64]{1,0:T(8,128)S(1)} %convert_element_type.14.scl_ref, bf16[1024,8192]{1,0:T(8,128)(2,1)S(1)} %copy-done.2), custom_call_target="tpu_custom_call" | custom-call | bytes 8388608 | tf_op jit(solution)/shard_map/down_weights/pallas_call | solution.py:184
  106.3 2.7 %collective-permute-done.18 = bf16[32,1024]{1,0:T(8,128)(2,1)S(1)} collective-permute-done((bf16[32,1024]{1,0:T(8,128)(2,1)S(1)}, bf16[32,1024]{1,0:T(8,128)(2,1)S(1)}, u32[]{:S(2)}, u32[]{:S(2)}) %collective-permute-start.18) | collective-permute-done | bytes 65568 | tf_op jit(solution)/shard_map/ppermute | solution.py:164
  109.7 3.3 %all-to-all-start.1 = ((bf16[8,4,1024]{2,1,0:T(4,128)(2,1)}), bf16[8,4,1024]{2,1,0:T(4,128)(2,1)S(1)}, u32[]{:S(2)}, u32[]{:S(2)}) async-start(bf16[8,4,1024]{2,1,0:T(4,128)(2,1)} %reshape.26), calls=%async_computation.1 | async-start | bytes 131072 | tf_op jit(solution)/shard_map/all_to_all | solution.py:255
  113.1 2.0 %all_gather.7 = f32[8192]{0:T(1024)} all-gather(f32[4096]{0:T(1024)S(1)} %copy-done.17), channel_id=1, replica_groups=mesh['groups'=2,'fsdp'=8,'tp'=2] {'tp'}, dimensions={0}, use_global_device_ids=true | all-gather | bytes 49152 | tf_op jit(solution)/shard_map/all_gather | solution.py:199
  116.3 3.6 %all-to-all-done.1.branch_ref = bf16[8,4,1024]{2,1,0:T(4,128)(2,1)S(1)} async-done(((bf16[8,4,1024]{2,1,0:T(4,128)(2,1)}), bf16[8,4,1024]{2,1,0:T(4,128)(2,1)S(1)}, u32[]{:S(2)}, u32[]{:S(2)}) %all-to-all-start.1) | async-done | bytes 65568 | tf_op jit(solution)/shard_map/all_to_all | solution.py:255
  (84 shorter events, 33.2 us)
Async XLA Ops:
  7.1 27.0 %all-to-all-start = ((bf16[8,4,1024]{2,1,0:T(4,128)(2,1)}), bf16[8,4,1024]{2,1,0:T(4,128)(2,1)S(1)}, u32[]{:S(2)}, u32[]{:S(2)}) async-start(bf16[8,4,1024]{2,1,0:T(4,128)(2,1)} %norm.1), calls=%async_computation | async-start | bytes 131072 | tf_op jit(solution)/shard_map/all_to_all | solution.py:205
  34.2 4.3 %collective-permute-start = (bf16[32,1024]{1,0:T(8,128)(2,1)S(1)}, bf16[32,1024]{1,0:T(8,128)(2,1)S(1)}, u32[]{:S(2)}, u32[]{:S(2)}) collective-permute-start(bf16[32,1024]{1,0:T(8,128)(2,1)S(1)} %reshape.24), channel_id=1, source_target_pairs={{0,16},{16,0},{1,17},{17,1},{2,18},{18,2},{3,19},{19,3},{4,20},{20... | collective-permute-start | bytes 196616 | tf_op jit(solution)/shard_map/ppermute | solution.py:164
  44.3 47.2 %copy-start.18 = (bf16[8,64]{1,0:T(8,128)(2,1)S(1)}, bf16[8,64]{1,0:T(8,128)(2,1)}, u32[]{:S(2)}) copy-start(bf16[8,64]{1,0:T(8,128)(2,1)} %param.18) | copy-start | bytes 3076
  46.6 8.9 %collective-permute-start.9 = (bf16[4,64,512]{2,1,0:T(8,128)(2,1)S(1)}, bf16[4,64,512]{2,1,0:T(8,128)(2,1)S(1)}, u32[]{:S(2)}, u32[]{:S(2)}) collective-permute-start(bf16[4,64,512]{2,1,0:T(8,128)(2,1)S(1)} %get-tuple-element.23), channel_id=1, source_target_pairs={{0,2},{2,0},{4,6},{6,4},{8,10},{10,8},{12,14},{14,12},{1,3},{3,1},... | collective-permute-start | bytes 786440 | tf_op jit(solution)/shard_map/ppermute | solution.py:164
  51.0 11.5 %collective-permute-start.1 = (bf16[4,64,512]{2,1,0:T(8,128)(2,1)S(1)}, bf16[4,64,512]{2,1,0:T(8,128)(2,1)S(1)}, u32[]{:S(2)}, u32[]{:S(2)}) collective-permute-start(bf16[4,64,512]{2,1,0:T(8,128)(2,1)S(1)} %get-tuple-element.17), channel_id=1, source_target_pairs={{0,2},{2,0},{4,6},{6,4},{8,10},{10,8},{12,14},{14,12},{1,3},{3,1},... | collective-permute-start | bytes 786440 | tf_op jit(solution)/shard_map/ppermute | solution.py:164
  58.1 11.4 %collective-permute-start.10 = (bf16[64,512]{1,0:T(8,128)(2,1)}, bf16[64,512]{1,0:T(8,128)(2,1)S(1)}, u32[]{:S(2)}, u32[]{:S(2)}) collective-permute-start(bf16[64,512]{1,0:T(8,128)(2,1)} %get-tuple-element.25), channel_id=1, source_target_pairs={{0,4},{2,6},{4,0},{6,2},{8,12},{10,14},{12,8},{14,10},{1,5},{3,7},... | collective-permute-start | bytes 196616 | tf_op jit(solution)/shard_map/ppermute | solution.py:164
  60.2 9.3 %collective-permute-start.11 = (bf16[64,512]{1,0:T(8,128)(2,1)}, bf16[64,512]{1,0:T(8,128)(2,1)S(1)}, u32[]{:S(2)}, u32[]{:S(2)}) collective-permute-start(bf16[64,512]{1,0:T(8,128)(2,1)} %get-tuple-element.26), channel_id=1, source_target_pairs={{0,8},{2,10},{4,12},{6,14},{8,0},{10,2},{12,4},{14,6},{1,9},{3,11}... | collective-permute-start | bytes 196616 | tf_op jit(solution)/shard_map/ppermute | solution.py:164
  62.5 7.0 %collective-permute-start.12 = (bf16[64,512]{1,0:T(8,128)(2,1)}, bf16[64,512]{1,0:T(8,128)(2,1)S(1)}, u32[]{:S(2)}, u32[]{:S(2)}) collective-permute-start(bf16[64,512]{1,0:T(8,128)(2,1)} %get-tuple-element.27), channel_id=1, source_target_pairs={{0,12},{2,14},{4,8},{6,10},{8,4},{10,6},{12,0},{14,2},{1,13},{3,15... | collective-permute-start | bytes 196616 | tf_op jit(solution)/shard_map/ppermute | solution.py:164
  65.1 11.1 %collective-permute-start.2 = (bf16[64,512]{1,0:T(8,128)(2,1)}, bf16[64,512]{1,0:T(8,128)(2,1)S(1)}, u32[]{:S(2)}, u32[]{:S(2)}) collective-permute-start(bf16[64,512]{1,0:T(8,128)(2,1)} %get-tuple-element.19), channel_id=1, source_target_pairs={{0,4},{2,6},{4,0},{6,2},{8,12},{10,14},{12,8},{14,10},{1,5},{3,7},... | collective-permute-start | bytes 196616 | tf_op jit(solution)/shard_map/ppermute | solution.py:164
  66.2 10.0 %collective-permute-start.3 = (bf16[64,512]{1,0:T(8,128)(2,1)}, bf16[64,512]{1,0:T(8,128)(2,1)S(1)}, u32[]{:S(2)}, u32[]{:S(2)}) collective-permute-start(bf16[64,512]{1,0:T(8,128)(2,1)} %get-tuple-element.20), channel_id=1, source_target_pairs={{0,8},{2,10},{4,12},{6,14},{8,0},{10,2},{12,4},{14,6},{1,9},{3,11}... | collective-permute-start | bytes 196616 | tf_op jit(solution)/shard_map/ppermute | solution.py:164
  69.5 6.8 %collective-permute-start.4 = (bf16[64,512]{1,0:T(8,128)(2,1)}, bf16[64,512]{1,0:T(8,128)(2,1)S(1)}, u32[]{:S(2)}, u32[]{:S(2)}) collective-permute-start(bf16[64,512]{1,0:T(8,128)(2,1)} %get-tuple-element.21), channel_id=1, source_target_pairs={{0,12},{2,14},{4,8},{6,10},{8,4},{10,6},{12,0},{14,2},{1,13},{3,15... | collective-permute-start | bytes 196616 | tf_op jit(solution)/shard_map/ppermute | solution.py:164
  71.8 28.5 %copy-start.6 = (bf16[64,256]{1,0:T(8,128)(2,1)S(1)}, bf16[64,256]{1,0:T(8,128)(2,1)}, u32[]{:S(2)}) copy-start(bf16[64,256]{1,0:T(8,128)(2,1)} %hidden_0.1.refs_0_) | copy-start | bytes 98308
  71.8 11.1 %collective-permute-start.13 = (bf16[64,256]{1,0:T(8,128)(2,1)}, bf16[64,256]{1,0:T(8,128)(2,1)S(1)}, u32[]{:S(2)}, u32[]{:S(2)}) collective-permute-start(bf16[64,256]{1,0:T(8,128)(2,1)} %hidden_0.1.refs_0_), channel_id=1, source_target_pairs={{0,4},{2,6},{4,0},{6,2},{8,12},{10,14},{12,8},{14,10},{1,5},{3,7},... | collective-permute-start | bytes 98312 | tf_op jit(solution)/shard_map/ppermute | solution.py:164
  73.0 10.0 %collective-permute-start.14 = (bf16[64,256]{1,0:T(8,128)(2,1)}, bf16[64,256]{1,0:T(8,128)(2,1)S(1)}, u32[]{:S(2)}, u32[]{:S(2)}) collective-permute-start(bf16[64,256]{1,0:T(8,128)(2,1)} %hidden_0.1.refs_0_), channel_id=1, source_target_pairs={{0,8},{2,10},{4,12},{6,14},{8,0},{10,2},{12,4},{14,6},{1,9},{3,11}... | collective-permute-start | bytes 98312 | tf_op jit(solution)/shard_map/ppermute | solution.py:164
  76.2 6.7 %collective-permute-start.15 = (bf16[64,256]{1,0:T(8,128)(2,1)}, bf16[64,256]{1,0:T(8,128)(2,1)S(1)}, u32[]{:S(2)}, u32[]{:S(2)}) collective-permute-start(bf16[64,256]{1,0:T(8,128)(2,1)} %hidden_0.1.refs_0_), channel_id=1, source_target_pairs={{0,12},{2,14},{4,8},{6,10},{8,4},{10,6},{12,0},{14,2},{1,13},{3,15... | collective-permute-start | bytes 98312 | tf_op jit(solution)/shard_map/ppermute | solution.py:164
  78.5 7.6 %collective-permute-start.5 = (bf16[64,256]{1,0:T(8,128)(2,1)}, bf16[64,256]{1,0:T(8,128)(2,1)S(1)}, u32[]{:S(2)}, u32[]{:S(2)}) collective-permute-start(bf16[64,256]{1,0:T(8,128)(2,1)} %hidden_1.1.refs_0_), channel_id=1, source_target_pairs={{0,4},{2,6},{4,0},{6,2},{8,12},{10,14},{12,8},{14,10},{1,5},{3,7},... | collective-permute-start | bytes 98312 | tf_op jit(solution)/shard_map/ppermute | solution.py:164
  79.1 7.0 %collective-permute-start.6 = (bf16[64,256]{1,0:T(8,128)(2,1)}, bf16[64,256]{1,0:T(8,128)(2,1)S(1)}, u32[]{:S(2)}, u32[]{:S(2)}) collective-permute-start(bf16[64,256]{1,0:T(8,128)(2,1)} %hidden_1.1.refs_0_), channel_id=1, source_target_pairs={{0,8},{2,10},{4,12},{6,14},{8,0},{10,2},{12,4},{14,6},{1,9},{3,11}... | collective-permute-start | bytes 98312 | tf_op jit(solution)/shard_map/ppermute | solution.py:164
  82.9 5.9 %collective-permute-start.7 = (bf16[64,256]{1,0:T(8,128)(2,1)}, bf16[64,256]{1,0:T(8,128)(2,1)S(1)}, u32[]{:S(2)}, u32[]{:S(2)}) collective-permute-start(bf16[64,256]{1,0:T(8,128)(2,1)} %hidden_1.1.refs_0_), channel_id=1, source_target_pairs={{0,12},{2,14},{4,8},{6,10},{8,4},{10,6},{12,0},{14,2},{1,13},{3,15... | collective-permute-start | bytes 98312 | tf_op jit(solution)/shard_map/ppermute | solution.py:164
  83.7 16.6 %collective-permute-start.16 = (bf16[4,64,256]{2,1,0:T(8,128)(2,1)S(1)}, bf16[4,64,256]{2,1,0:T(8,128)(2,1)S(1)}, u32[]{:S(2)}, u32[]{:S(2)}) collective-permute-start(bf16[4,64,256]{2,1,0:T(8,128)(2,1)S(1)} %pad_maximum_fusion.1), channel_id=1, source_target_pairs={{0,2},{2,0},{4,6},{6,4},{8,10},{10,8},{12,14},{14,12},{1,3},{3,1},... | collective-permute-start | bytes 393224 | tf_op jit(solution)/shard_map/ppermute | solution.py:164
  89.6 12.1 %collective-permute-start.8 = (bf16[4,64,256]{2,1,0:T(8,128)(2,1)S(1)}, bf16[4,64,256]{2,1,0:T(8,128)(2,1)S(1)}, u32[]{:S(2)}, u32[]{:S(2)}) collective-permute-start(bf16[4,64,256]{2,1,0:T(8,128)(2,1)S(1)} %pad_maximum_fusion), channel_id=1, source_target_pairs={{0,2},{2,0},{4,6},{6,4},{8,10},{10,8},{12,14},{14,12},{1,3},{3,1},... | collective-permute-start | bytes 393224 | tf_op jit(solution)/shard_map/ppermute | solution.py:164
  97.3 15.8 %copy-start.17 = (f32[4096]{0:T(1024)S(1)}, f32[4096]{0:T(1024)}, u32[]{:S(2)}) copy-start(f32[4096]{0:T(1024)} %param.19) | copy-start | bytes 49156
  103.1 1.6 %collective-permute-start.17 = (f32[64,1024]{1,0:T(8,128)S(1)}, f32[64,1024]{1,0:T(8,128)S(1)}, u32[]{:S(2)}, u32[]{:S(2)}) collective-permute-start(f32[64,1024]{1,0:T(8,128)S(1)} %down_1.1), channel_id=1, source_target_pairs={{0,1},{1,0},{2,3},{3,2},{4,5},{5,4},{6,7},{7,6},{8,9},{9,8},{10,11... | collective-permute-start | bytes 786440 | tf_op jit(solution)/shard_map/ppermute | solution.py:164
  104.7 4.3 %collective-permute-start.18 = (bf16[32,1024]{1,0:T(8,128)(2,1)S(1)}, bf16[32,1024]{1,0:T(8,128)(2,1)S(1)}, u32[]{:S(2)}, u32[]{:S(2)}) collective-permute-start(bf16[32,1024]{1,0:T(8,128)(2,1)S(1)} %slice.20), channel_id=1, source_target_pairs={{0,16},{16,0},{1,17},{17,1},{2,18},{18,2},{3,19},{19,3},{4,20},{20... | collective-permute-start | bytes 196616 | tf_op jit(solution)/shard_map/ppermute | solution.py:164
  109.7 10.2 %all-to-all-start.1 = ((bf16[8,4,1024]{2,1,0:T(4,128)(2,1)}), bf16[8,4,1024]{2,1,0:T(4,128)(2,1)S(1)}, u32[]{:S(2)}, u32[]{:S(2)}) async-start(bf16[8,4,1024]{2,1,0:T(4,128)(2,1)} %reshape.26), calls=%async_computation.1 | async-start | bytes 131072 | tf_op jit(solution)/shard_map/all_to_all | solution.py:255
  (16 other events, 35.0 us)

commit v2 on v0

v2 whole, which is shorter than its diff:
```python
import functools

import jax
import jax.numpy as jnp
from jax import lax
from jax.experimental import pallas as pl
from jax.experimental.pallas import tpu as pltpu
from jax.sharding import PartitionSpec as P

TILE = 128
CODE_ROWS = 16
LOG2_E, LN_2 = 1.4426950408889634, 0.6931471805599453
BF16, F32 = jnp.bfloat16, jnp.float32
VMEM_SPEC = pl.BlockSpec(memory_space=pltpu.VMEM)
SMEM_SPEC = pl.BlockSpec(memory_space=pltpu.SMEM)


def params(mib):
    return pltpu.CompilerParams(vmem_limit_bytes=mib << 20)


def dequantize(codes, scales):
    tile_rows = codes.shape[0] // scales.shape[0]
    tile_cols = codes.shape[1] // scales.shape[1]
    blocks = codes.astype(F32).reshape(scales.shape[0], tile_rows, scales.shape[1], tile_cols)
    scaled = blocks * scales.astype(F32)[:, None, :, None]
    return scaled.reshape(codes.shape).astype(BF16)


def rms_normed(rows_in, norm_gain):
    resid = rows_in.astype(F32)
    mean_sq = jnp.mean(resid * resid, axis=-1, keepdims=True)
    return (resid * lax.rsqrt(mean_sq + 1e-05) * norm_gain.astype(F32)).astype(BF16)


def body_any(tokens, lengths, norm_gain, gate_codes, gate_scales, up_codes, up_scales, down_codes, down_scales, value_head):
    rows = tokens.shape[0]
    feature_rows = lax.all_gather(tokens, "tp", axis=1, tiled=True)
    normed = rms_normed(feature_rows, norm_gain)
    x = lax.all_to_all(normed, "fsdp", split_axis=1, concat_axis=0, tiled=True)
    gate = jnp.dot(x, dequantize(gate_codes, gate_scales), preferred_element_type=F32)
    up = jnp.dot(x, dequantize(up_codes, up_scales), preferred_element_type=F32)
    gate = lax.psum_scatter(gate, "fsdp", scatter_dimension=1, tiled=True)
    up = lax.psum_scatter(up, "fsdp", scatter_dimension=1, tiled=True)
    hidden = (jax.nn.silu(gate) * up).astype(BF16)
    hidden = lax.all_gather(hidden, "fsdp", axis=1, tiled=True)
    part = lax.dot_general(
        hidden, dequantize(down_codes, down_scales), (((1,), (1,)), ((), ())), preferred_element_type=F32
    )
    part = lax.all_to_all(part, "fsdp", split_axis=0, concat_axis=1, tiled=True)
    branch = lax.psum_scatter(part, "tp", scatter_dimension=1, tiled=True)
    layer_out = (tokens.astype(F32) + branch).astype(BF16)
    head = jnp.dot(layer_out.astype(F32), value_head, precision=lax.Precision.HIGHEST)
    head = lax.psum(head, "tp")
    live = jnp.arange(rows) < lengths[0]
    return layer_out, jnp.where(live, head, F32(0.0))


def norm_kernel(place_ref, mine_ref, core_mate_ref, group_mate_ref, far_mate_ref, gain_ref, *refs):
    out_ref, all_ref = refs[-2:]
    n, _, width = out_ref.shape
    rows, half = mine_ref.shape
    per = half // width
    core = place_ref[1]
    for at, halves in ((0, (mine_ref, core_mate_ref)), (rows, (group_mate_ref, far_mate_ref))):
        resid = [ref[...].astype(F32) for ref in halves]
        total = sum(jnp.sum(r * r, axis=-1, keepdims=True) for r in resid)
        inv = lax.rsqrt(total * (1.0 / (2 * half)) + 1e-05)
        for side, r in enumerate(resid):
            for i in range(per):
                c = (core ^ side) * per + i
                gain = gain_ref[:, pl.ds(pl.multiple_of(c * width, TILE), width)].astype(F32)
                all_ref[c, at : at + rows] = r[:, i * width : (i + 1) * width] * inv * gain
    out_ref[...] = all_ref[...].astype(BF16)


def encode(values, out_ref):
    count, rows = len(values), values[0].shape[0]
    top = functools.reduce(jnp.maximum, [jnp.max(jnp.abs(v), axis=0, keepdims=True) for v in values])
    power = jnp.clip(jnp.ceil(jnp.log(top) * LOG2_E), -100.0, 100.0)
    unit = jnp.exp((14.0 - power) * LN_2)
    for i, v in enumerate(values):
        out_ref[i * rows : (i + 1) * rows] = jnp.round(v * unit).astype(jnp.int32).astype(jnp.int16)
    tail = (out_ref.shape[0] - count * rows, out_ref.shape[1])
    out_ref[count * rows :] = jnp.broadcast_to(power.astype(jnp.int32), tail).astype(jnp.int16)


def decode(got_ref, rows, entries):
    count = (got_ref.shape[0] - CODE_ROWS) // rows
    power = got_ref[count * rows :].astype(jnp.int32).astype(F32)[:1]
    unit = jnp.exp((power - 14.0) * LN_2)
    return [got_ref[i * rows : (i + 1) * rows].astype(jnp.int32).astype(F32) * unit for i in entries]


def scaled(codes, scale_of, down, across):
    tiles = [
        [
            codes[r * TILE : (r + 1) * TILE, c * TILE : (c + 1) * TILE] * scale_of(r, c).astype(BF16)
            for c in range(across)
        ]
        for r in range(down)
    ]
    return jnp.concatenate([jnp.concatenate(row, axis=1) for row in tiles], axis=0)


def gate_up_kernel(piece, slots, first, place_ref, scl_ref, x_ref, gate_ref, up_ref, send_ref, keep_ref, sums_ref):
    me, group = place_ref[0], place_ref[3]
    x = x_ref[...].reshape(-1, x_ref.shape[-1])
    n, wide = 2 * len(slots), keep_ref.shape[-1] // 2
    units, step = wide // TILE, 2 * TILE
    for flip, out_ref in ((first, sums_ref), (0, keep_ref)):
        for i, slot in enumerate(slots):
            block = (group * 2 + piece) * n + (me ^ (slot ^ flip))
            cols = pl.ds(pl.multiple_of(block * wide, TILE), wide)
            for m, ref in enumerate((gate_ref, up_ref)):
                total = None
                for k in range(0, x.shape[1], step):
                    w = scaled(
                        ref[k : k + step, cols], lambda r, c: scl_ref[m, k // TILE + r, block * units + c], 2, units
                    )
                    part = jnp.dot(x[:, k : k + step], w, preferred_element_type=F32)
                    total = part if total is None else total + part
                out_ref[i, :, m * wide : (m + 1) * wide] = total
        if flip:
            encode([sums_ref[i] for i in range(len(slots))], send_ref)


def halve_kernel(keep_ref, got_ref, *refs):
    stay_ref, send_ref = refs[-2:]
    half, rows = stay_ref.shape[0], stay_ref.shape[1]
    got = decode(got_ref, rows, range(2 * half))
    for i in range(half):
        stay_ref[i] = keep_ref[i] + got[i]
    encode([keep_ref[half + i] + got[half + i] for i in range(half)], send_ref)


def hidden_kernel(keep_ref, got_ref, out_ref):
    total = keep_ref[0] + decode(got_ref, keep_ref.shape[1], (0,))[0]
    wide = out_ref.shape[-1]
    gate, up = total[:, :wide], total[:, wide:]
    out_ref[0] = (gate / (1.0 + jnp.exp(-gate)) * up).astype(BF16)


def join_kernel(mine_ref, got_ref, out_ref):
    count = mine_ref.shape[0]
    out_ref[:count] = mine_ref[...]
    out_ref[count:] = got_ref[...]


def down_kernel(piece, slots, begin, last, place_ref, scl_ref, hidden_ref, codes_ref, *refs):
    me, group = place_ref[0], place_ref[3]
    wide, depth, step = hidden_ref.shape[-1], codes_ref.shape[0], 2 * TILE
    units, n = wide // TILE, 2 * len(slots)
    for r in range(0, depth, step):
        total = None if begin else refs[0][:, r : r + step]
        for i, slot in enumerate(slots):
            block = (group * 2 + piece) * n + (me ^ slot)
            cols = pl.ds(pl.multiple_of(block * wide, TILE), wide)
            w = scaled(codes_ref[r : r + step, cols], lambda t, c: scl_ref[r // TILE + t, block * units + c], 2, units)
            part = lax.dot_general(hidden_ref[i], w, (((1,), (1,)), ((), ())), preferred_element_type=F32)
            total = part if total is None else total + part
        if not last:
            refs[-1][:, r : r + step] = total
            continue
        keep_ref, other_ref = refs[-2:]
        rows = keep_ref.shape[1]
        total = total.reshape(n, 2 * rows, step)
        keep_ref[:, :, r : r + step] = total[:, :rows]
        other_ref[:, :, r : r + step] = total[:, rows:].astype(BF16)


def branch_kernel(keep_ref, core_mate_ref, group_mate_ref, far_mate_ref, out_ref):
    near = keep_ref[...] + core_mate_ref[...]
    far = group_mate_ref[...].astype(F32) + far_mate_ref[...].astype(F32)
    out_ref[...] = (near + far).astype(BF16)


def final_kernel(place_ref, tok_ref, tok_mate_ref, branch_ref, head_ref, head_mate_ref, out_ref, values_ref):
    n, rows, width = branch_ref.shape
    per = out_ref.shape[1] // width
    core = place_ref[1]
    total = jnp.zeros((rows, 1), F32)
    for side, (tok, head) in enumerate(((tok_ref, head_ref), (tok_mate_ref, head_mate_ref))):
        for i in range(per):
            cols = slice(i * width, (i + 1) * width)
            branch = branch_ref[(core ^ side) * per + i].astype(F32)
            layer = (tok[:, cols].astype(F32) + branch).astype(BF16)
            if side == 0:
                out_ref[:, cols] = layer
            total = total + jnp.sum(layer.astype(F32) * head[:, cols], axis=-1, keepdims=True)
    row, at = (lax.broadcasted_iota(jnp.int32, (rows, rows), axis) for axis in (0, 1))
    taken = (row == at) & (row < place_ref[2])
    values_ref[...] = jnp.sum(jnp.where(taken, total, 0.0), axis=0, keepdims=True)


def call(kernel, name, ins, outs, limit=8, cost=None, scratch=()):
    specs = [x[1] if isinstance(x, tuple) else VMEM_SPEC for x in ins]
    return pl.pallas_call(
        kernel,
        in_specs=specs,
        out_specs=jax.tree.map(lambda _: VMEM_SPEC, outs),
        out_shape=outs,
        scratch_shapes=scratch,
        compiler_params=params(limit),
        cost_estimate=cost,
        name=name,
    )(*[x[0] if isinstance(x, tuple) else x for x in ins])


def body_split(n, tokens, lengths, norm_gain, gate_codes, gate_scales, up_codes, up_scales, down_codes, down_scales, value_head):
    rows, d_half = tokens.shape
    d, depth = 2 * d_half, gate_codes.shape[0]
    group_cols = gate_codes.shape[1] // 2
    units = group_cols // (2 * n * TILE)
    all_rows, half = 2 * n * rows, n // 2
    me, group, core = (lax.axis_index(a).astype(jnp.int32) for a in ("fsdp", "groups", "tp"))
    place = jnp.stack([me, core, lengths[0], group])
    spot = (place, SMEM_SPEC)
    shape = jax.ShapeDtypeStruct

    def swap(x, axis, bit):
        size = n if axis == "fsdp" else 2 if isinstance(axis, str) else 4
        return lax.ppermute(x, axis, [(i, i ^ bit) for i in range(size)])

    def three(to_core, to_group, to_far):
        return swap(to_core, "tp", 1), swap(to_group, "groups", 1), swap(to_far, ("groups", "tp"), 3)

    hbm = lambda x: pltpu.with_memory_space_constraint(x, pltpu.HBM)
    vmem = lambda x: pltpu.with_memory_space_constraint(x, pltpu.VMEM)
    unread = lambda x: (x, pl.BlockSpec(memory_space=pl.ANY))

    gu_scales = jnp.stack([gate_scales, up_scales]).astype(F32)
    down_scales = down_scales.astype(F32)

    mates = three(tokens, tokens, tokens)
    head = value_head.reshape(1, d_half)
    head_mate = swap(head, "tp", 1)
    normed = call(
        norm_kernel,
        "norm",
        [spot, tokens, *mates, norm_gain.reshape(1, d)]
        + [unread(a) for a in (head_mate, gu_scales, down_scales)]
        + [unread(hbm(a)) for a in (gate_codes, up_codes, down_codes)],
        shape((n, 2 * rows, depth), BF16),
        scratch=[pltpu.VMEM((n, 2 * rows, depth), F32)],
    )
    x = lax.all_to_all(normed, "fsdp", 0, 0, tiled=True)

    wide = units * TILE
    codes = [vmem(c) for c in (gate_codes, up_codes)]
    cost = lambda share, width: pl.CostEstimate(
        flops=2 * all_rows * depth * width * n // share, transcendentals=0, bytes_accessed=2 * depth * width * n // share
    )

    coded = lambda count: shape((count * all_rows + CODE_ROWS, 2 * wide), jnp.int16)

    plans = ((1, 2, 4), (2, 1, 4))
    sent = []
    for p, (b1, b2, b3) in enumerate(plans):
        slots = (0, b3, b2, b2 ^ b3)
        send, keep = call(
            functools.partial(gate_up_kernel, p, slots, b1),
            f"gate_up_{p}",
            [spot, (gu_scales, SMEM_SPEC), x, *codes],
            [coded(half), shape((half, all_rows, 2 * wide), F32)],
            cost=cost(1, 2 * wide),
            scratch=[pltpu.VMEM((half, all_rows, 2 * wide), F32)],
        )
        sent.append((keep, swap(send, "fsdp", b1)))
    branch = None
    for p, (b1, b2, b3) in enumerate(plans):
        keep, got = sent[p]
        for count, bit in ((half // 2, b2), (half // 4, b3)):
            keep, send = call(
                halve_kernel,
                f"halve_{count}_{p}",
                [keep, got, unread(hbm(down_codes))],
                [shape((count, all_rows, 2 * wide), F32), coded(count)],
            )
            got = swap(send, "fsdp", bit)
        hidden = call(hidden_kernel, f"hidden_{p}", [keep, got], shape((1, all_rows, wide), BF16))
        for count, bit in ((2, b3), (4, b2)):
            got = swap(hidden, "fsdp", bit)
            hidden = call(join_kernel, f"join_{count}_{p}", [hidden, got], shape((count, all_rows, wide), BF16))
        slots = (0, b3, b2, b2 ^ b3)
        for part, flip in ((hidden, 0), (swap(hidden, "fsdp", b1), b1)):
            last = p == len(plans) - 1 and flip
            branch = call(
                functools.partial(down_kernel, p, tuple(s ^ flip for s in slots), branch is None, last),
                f"down_{p}_{min(flip, 1)}",
                [spot, (down_scales, SMEM_SPEC), part, vmem(down_codes)] + ([] if branch is None else [branch]),
                [shape((n, rows, depth), t) for t in (F32, BF16)] if last else shape((all_rows, depth), F32),
                cost=cost(2, wide),
            )

    keep, other = branch
    branch = call(branch_kernel, "branch", [keep, *three(keep, other, other)], shape((n, rows, depth), BF16))
    branch = lax.all_to_all(branch, "fsdp", 0, 0, tiled=True)
    layer_out, values = call(
        final_kernel,
        "final",
        [spot, tokens, mates[0], branch, head, head_mate],
        [shape((rows, d_half), BF16), shape((1, rows), F32)],
    )
    return layer_out, values.reshape(rows)


def solution(mesh):
    placed = (
        P(("groups", "fsdp"), "tp"),
        P(("groups", "fsdp")),
        P(),
        P("fsdp", "tp"),
        P("fsdp", "tp"),
        P("fsdp", "tp"),
        P("fsdp", "tp"),
        P("fsdp", "tp"),
        P("fsdp", "tp"),
        P("tp"),
    )
    n = mesh.shape["fsdp"]

    def body(*args):
        codes = args[3]
        fits = (
            n == 8
            and mesh.shape["groups"] == 2
            and mesh.shape["tp"] == 2
            and codes.shape[0] % TILE == 0
            and codes.shape[1] == 8 * n * TILE
        )
        if fits:
            return body_split(n, *args)
        return body_any(*args)

    return jax.shard_map(
        body,
        mesh=mesh,
        in_specs=placed,
        out_specs=(P(("groups", "fsdp"), "tp"), P(("groups", "fsdp"))),
        check_vma=False,
    )
```

time: 1590 us -> 82.8 us (0.05)
  waiting for transfers between devices: 775 us -> 24.2 us
  blocking collectives: 385 us -> 23.8 us
  local copies, waits for them, and re-layouts: 209 us -> 2.2 us
  other arithmetic: 145 us -> 1.47 us
  matrix products: 24.1 us -> 0 us
    all_to_all x6 -> x0, waiting for transfers between devices: 687 us -> none  [the longest x1 339 us: body(): lax.all_to_all(up_codes, 'fsdp', split_axis=1, concat_axis=0, tiled=True)]
    all_gather x2 -> x0, blocking collectives: 383 us -> none  [the longest x1 381 us: body(): all_rows = lax.all_gather(feature_rows, 'fsdp', axis=0, tiled=True)]
    convert_element_type x11 -> x2, other arithmetic: 144 us -> 1.39 us  [the longest x1 0.71 us: body_split(): gu_scales = jnp.stack([gate_scales, up_scales]).astype(F32)]
    convert_element_type x7 -> x0, local copies, waits for them, and re-layouts: 96.6 us -> none  [the longest x3 95.7 us: dequantize(): codes.astype(jnp.float32)]
    unnamed x4 -> x0, waiting for transfers between devices: 87.9 us -> none
    unnamed x34 -> x30, local copies, waits for them, and re-layouts: 79.4 us -> 1.31 us
    mul x3 -> x0, local copies, waits for them, and re-layouts: 33.4 us -> none  [dequantize(): scaled = blocks * scales.astype(jnp.float32)[:, None, :, None]]
    all_to_all x6 -> x0, starting transfers between devices: 31.4 us -> none  [the longest x1 7.25 us: body(): lax.all_to_all(gate_scales, 'fsdp', split_axis=1, concat_axis=0, tiled=True)]
  transfers between devices with their start and end apart: 8 -> 19, of which waited for: 6 -> 13; matrix products, arithmetic and copies ran while one was open for 11% -> 3% of each run, Pallas kernels for 0% -> 9%
where the time goes in v2:
time: 82.8 us; the launch traced here: 82.5 us
  waiting for transfers between devices  24.2 us (29%)
  blocking collectives  23.8 us (29%)
  starting transfers between devices  16.4 us (20%)
  Pallas kernels  12.8 us (15%)
  local copies, waits for them, and re-layouts  2.2 us (3%)
  between operations  1.59 us (2%)
  other arithmetic  1.47 us (2%)
    ppermute x19, waiting for transfers between devices, swap(): return lax.ppermute(x, axis, [(i, i ^ bit) for i in range(size)])  24.2 us
    ppermute x19, starting transfers between devices, swap(): return lax.ppermute(x, axis, [(i, i ^ bit) for i in range(size)])  16.4 us
    all_to_all x1, blocking collectives, body_split(): x = lax.all_to_all(normed, 'fsdp', 0, 0, tiled=True)  13.3 us
    pallas_call x19, Pallas kernels, call(): pl.pallas_call(kernel, in_specs=specs, out_specs=jax.tree.map(lambda _: V...  12.8 us
    all_to_all x1, blocking collectives, body_split(): branch = lax.all_to_all(branch, 'fsdp', 0, 0, tiled=True)  10.5 us
  transfers between devices with their start and end apart: 19, of which 13 were waited for; matrix products, arithmetic and copies ran while one was open for 3% of the time, Pallas kernels for 9%

profile of v2, /device:TPU:0, one launch (start us, length us, event | category | flops | bytes accessed | tf_op | source)
XLA Modules:
  0.0 82.5 jit_solution(18100681535922854668)
XLA Ops:
  0.6 2.5 %collective-permute-start.2 = (bf16[4,4096]{1,0:T(4,128)(2,1)}, bf16[4,4096]{1,0:T(4,128)(2,1)S(1)}, u32[]{:S(2)}, u32[]{:S(2)}) collective-permute-start(bf16[4,4096]{1,0:T(4,128)(2,1)} %tok_ref.1), channel_id=1, source_target_pairs={{0,17},{1,16},{16,1},{17,0},{2,19},{3,18},{18,3},{19,2},{4,21},{5,... | collective-permute-start | bytes 98312 | tf_op jit(solution)/shard_map/ppermute | solution.py:223
  7.4 1.2 %copy-done = bf16[4,4096]{1,0:T(4,128)(2,1)S(1)} copy-done((bf16[4,4096]{1,0:T(4,128)(2,1)S(1)}, bf16[4,4096]{1,0:T(4,128)(2,1)}, u32[]{:S(2)}) %copy-start) | copy-done | bytes 32792
  9.4 13.3 %all_to_all.10.x_ref = bf16[8,8,1024]{2,1,0:T(8,128)(2,1)S(1)} all-to-all(bf16[8,8,1024]{2,1,0:T(8,128)(2,1)S(1)} %norm.1), channel_id=1, replica_groups=mesh['groups'=2,'fsdp'=8,'tp'=2] {'fsdp'}, dimensions={0} | all-to-all | bytes 262144 | tf_op jit(solution)/shard_map/all_to_all | solution.py:247
  22.7 2.4 %gate_up_0.1 = (s16[272,512]{1,0:T(8,128)(2,1)S(1)}, f32[4,64,512]{2,1,0:T(8,128)S(1)}) custom-call(s32[4]{0:T(128)S(1)} %pad_add_fusion.place_ref, f32[2,8,64]{2,1,0:T(8,128)S(1)} %maximum_convert_fusion.refs_1_.scl_ref, bf16[8,8,1024]{2,1,0:T(8,128)(2,1)S(1)} %all_to_all.10.x_ref, bf16[1024,8192]{1,0:T(8,128)(2,1)S(1)} %bitcast.10, ...), custom_call_target="tpu_custom_call" | custom-call | flops 536870912 | bytes 8388608 | tf_op jit(solution)/shard_map/gate_up_0/pallas_call | solution.py:198
  25.6 2.4 %gate_up_1.1 = (s16[272,512]{1,0:T(8,128)(2,1)S(1)}, f32[4,64,512]{2,1,0:T(8,128)S(1)}) custom-call(s32[4]{0:T(128)S(1)} %pad_add_fusion.place_ref, f32[2,8,64]{2,1,0:T(8,128)S(1)} %maximum_convert_fusion.refs_1_.scl_ref, bf16[8,8,1024]{2,1,0:T(8,128)(2,1)S(1)} %all_to_all.10.x_ref, bf16[1024,8192]{1,0:T(8,128)(2,1)S(1)} %bitcast.10, ...), custom_call_target="tpu_custom_call" | custom-call | flops 536870912 | bytes 8388608 | tf_op jit(solution)/shard_map/gate_up_1/pallas_call | solution.py:198
  28.9 3.6 %collective-permute-done.10.got_ref = s16[272,512]{1,0:T(8,128)(2,1)S(1)} collective-permute-done((s16[272,512]{1,0:T(8,128)(2,1)S(1)}, s16[272,512]{1,0:T(8,128)(2,1)S(1)}, u32[]{:S(2)}, u32[]{:S(2)}) %collective-permute-start.10) | collective-permute-done | bytes 278560 | tf_op jit(solution)/shard_map/ppermute | solution.py:223
  32.8 3.7 %collective-permute-done.4.got_ref = s16[272,512]{1,0:T(8,128)(2,1)S(1)} collective-permute-done((s16[272,512]{1,0:T(8,128)(2,1)S(1)}, s16[272,512]{1,0:T(8,128)(2,1)S(1)}, u32[]{:S(2)}, u32[]{:S(2)}) %collective-permute-start.4) | collective-permute-done | bytes 278560 | tf_op jit(solution)/shard_map/ppermute | solution.py:223
  36.7 1.8 %collective-permute-start.5 = (s16[144,512]{1,0:T(8,128)(2,1)S(1)}, s16[144,512]{1,0:T(8,128)(2,1)S(1)}, u32[]{:S(2)}, u32[]{:S(2)}) collective-permute-start(s16[144,512]{1,0:T(8,128)(2,1)S(1)} %get-tuple-element.21), channel_id=1, source_target_pairs={{0,2},{2,0},{4,6},{6,4},{8,10},{10,8},{12,14},{14,12},{1,3},{3,1},... | collective-permute-start | bytes 442376 | tf_op jit(solution)/shard_map/ppermute | solution.py:223
  39.8 2.1 %collective-permute-done.5.got_ref = s16[144,512]{1,0:T(8,128)(2,1)S(1)} collective-permute-done((s16[144,512]{1,0:T(8,128)(2,1)S(1)}, s16[144,512]{1,0:T(8,128)(2,1)S(1)}, u32[]{:S(2)}, u32[]{:S(2)}) %collective-permute-start.5) | collective-permute-done | bytes 147488 | tf_op jit(solution)/shard_map/ppermute | solution.py:223
  42.0 1.5 %collective-permute-start.6 = (s16[80,512]{1,0:T(8,128)(2,1)S(1)}, s16[80,512]{1,0:T(8,128)(2,1)S(1)}, u32[]{:S(2)}, u32[]{:S(2)}) collective-permute-start(s16[80,512]{1,0:T(8,128)(2,1)S(1)} %get-tuple-element.23), channel_id=1, source_target_pairs={{0,8},{2,10},{4,12},{6,14},{8,0},{10,2},{12,4},{14,6},{1,9},{3,11}... | collective-permute-start | bytes 245768 | tf_op jit(solution)/shard_map/ppermute | solution.py:223
  43.4 2.2 %collective-permute-done.12.got_ref = s16[80,512]{1,0:T(8,128)(2,1)S(1)} collective-permute-done((s16[80,512]{1,0:T(8,128)(2,1)S(1)}, s16[80,512]{1,0:T(8,128)(2,1)S(1)}, u32[]{:S(2)}, u32[]{:S(2)}) %collective-permute-start.12) | collective-permute-done | bytes 81952 | tf_op jit(solution)/shard_map/ppermute | solution.py:223
  45.8 2.9 %collective-permute-done.6.got_ref = s16[80,512]{1,0:T(8,128)(2,1)S(1)} collective-permute-done((s16[80,512]{1,0:T(8,128)(2,1)S(1)}, s16[80,512]{1,0:T(8,128)(2,1)S(1)}, u32[]{:S(2)}, u32[]{:S(2)}) %collective-permute-start.6) | collective-permute-done | bytes 81952 | tf_op jit(solution)/shard_map/ppermute | solution.py:223
  49.3 1.6 %collective-permute-done.13.got_ref = bf16[1,64,256]{2,1,0:T(8,128)(2,1)S(1)} collective-permute-done((bf16[1,64,256]{2,1,0:T(8,128)(2,1)S(1)}, bf16[1,64,256]{2,1,0:T(8,128)(2,1)S(1)}, u32[]{:S(2)}, u32[]{:S(2)}) %collective-permute-start.13) | collective-permute-done | bytes 32800 | tf_op jit(solution)/shard_map/ppermute | solution.py:223
  50.9 1.5 %collective-permute-start.14 = (bf16[2,64,256]{2,1,0:T(8,128)(2,1)S(1)}, bf16[2,64,256]{2,1,0:T(8,128)(2,1)S(1)}, u32[]{:S(2)}, u32[]{:S(2)}) collective-permute-start(bf16[2,64,256]{2,1,0:T(8,128)(2,1)S(1)} %join_2_0.1.mine_ref), channel_id=1, source_target_pairs={{0,4},{2,6},{4,0},{6,2},{8,12},{10,14},{12,8},{14,10},{1,5},{3,7},... | collective-permute-start | bytes 196616 | tf_op jit(solution)/shard_map/ppermute | solution.py:223
  52.4 1.6 %collective-permute-done.7.got_ref = bf16[1,64,256]{2,1,0:T(8,128)(2,1)S(1)} collective-permute-done((bf16[1,64,256]{2,1,0:T(8,128)(2,1)S(1)}, bf16[1,64,256]{2,1,0:T(8,128)(2,1)S(1)}, u32[]{:S(2)}, u32[]{:S(2)}) %collective-permute-start.7) | collective-permute-done | bytes 32800 | tf_op jit(solution)/shard_map/ppermute | solution.py:223
  56.0 2.2 %collective-permute-done.8.got_ref = bf16[2,64,256]{2,1,0:T(8,128)(2,1)S(1)} collective-permute-done((bf16[2,64,256]{2,1,0:T(8,128)(2,1)S(1)}, bf16[2,64,256]{2,1,0:T(8,128)(2,1)S(1)}, u32[]{:S(2)}, u32[]{:S(2)}) %collective-permute-start.8) | collective-permute-done | bytes 65568 | tf_op jit(solution)/shard_map/ppermute | solution.py:223
  58.7 1.4 %down_0_0.1.refs_0_ = f32[64,1024]{1,0:T(8,128)S(1)} custom-call(s32[4]{0:T(128)S(1)} %pad_add_fusion.place_ref, f32[8,64]{1,0:T(8,128)S(1)} %convert_element_type.6.refs_2_.scl_ref, bf16[4,64,256]{2,1,0:T(8,128)(2,1)S(1)} %join_4_0.1.hidden_ref, bf16[1024,8192]{1,0:T(8,128)(2,1)S(1)} %bitcast.8), custom_call_target="tpu_custom_call" | custom-call | flops 134217728 | bytes 2097152 | tf_op jit(solution)/shard_map/down_0_0/pallas_call | solution.py:198
  60.2 1.4 %down_0_1.1.refs_0_ = f32[64,1024]{1,0:T(8,128)S(1)} custom-call(s32[4]{0:T(128)S(1)} %pad_add_fusion.place_ref, f32[8,64]{1,0:T(8,128)S(1)} %convert_element_type.6.refs_2_.scl_ref, bf16[4,64,256]{2,1,0:T(8,128)(2,1)S(1)} %collective-permute-done.15.hidden_ref, bf16[1024,8192]{1,0:T(8,128)(2,1)S(1)} %bitcast.8, f32[64,1024]{1,0:T(8,128)S(1)} %down_0_0.1.refs_0_), custom_call_target="tpu_custom_call" | custom-call | flops 134217728 | bytes 2097152 | tf_op jit(solution)/shard_map/down_0_1/pallas_call | solution.py:198
  61.6 1.4 %down_1_0.1.refs_0_ = f32[64,1024]{1,0:T(8,128)S(1)} custom-call(s32[4]{0:T(128)S(1)} %pad_add_fusion.place_ref, f32[8,64]{1,0:T(8,128)S(1)} %convert_element_type.6.refs_2_.scl_ref, bf16[4,64,256]{2,1,0:T(8,128)(2,1)S(1)} %join_4_1.1.hidden_ref, bf16[1024,8192]{1,0:T(8,128)(2,1)S(1)} %bitcast.8, f32[64,1024]{1,0:T(8,128)S(1)} %down_0_1.1.refs_0_), custom_call_target="tpu_custom_call" | custom-call | flops 134217728 | bytes 2097152 | tf_op jit(solution)/shard_map/down_1_0/pallas_call | solution.py:198
  63.2 1.4 %down_1_1.1 = (f32[8,4,1024]{2,1,0:T(4,128)S(1)}, bf16[8,4,1024]{2,1,0:T(4,128)(2,1)S(1)}) custom-call(s32[4]{0:T(128)S(1)} %pad_add_fusion.place_ref, f32[8,64]{1,0:T(8,128)S(1)} %convert_element_type.6.refs_2_.scl_ref, bf16[4,64,256]{2,1,0:T(8,128)(2,1)S(1)} %collective-permute-done.9.hidden_ref, bf16[1024,8192]{1,0:T(8,128)(2,1)S(1)} %bitcast.8, ...), custom_call_target="tpu_custom_call" | custom-call | flops 134217728 | bytes 2097152 | tf_op jit(solution)/shard_map/down_1_1/pallas_call | solution.py:198
  64.7 1.7 %collective-permute-start.18 = (bf16[8,4,1024]{2,1,0:T(4,128)(2,1)S(1)}, bf16[8,4,1024]{2,1,0:T(4,128)(2,1)S(1)}, u32[]{:S(2)}, u32[]{:S(2)}) collective-permute-start(bf16[8,4,1024]{2,1,0:T(4,128)(2,1)S(1)} %get-tuple-element.31), channel_id=1, source_target_pairs={{0,17},{1,16},{16,1},{17,0},{2,19},{3,18},{18,3},{19,2},{4,21},{5,... | collective-permute-start | bytes 196616 | tf_op jit(solution)/shard_map/ppermute | solution.py:223
  66.8 1.9 %collective-permute-done.18.far_mate_ref = bf16[8,4,1024]{2,1,0:T(4,128)(2,1)S(1)} collective-permute-done((bf16[8,4,1024]{2,1,0:T(4,128)(2,1)S(1)}, bf16[8,4,1024]{2,1,0:T(4,128)(2,1)S(1)}, u32[]{:S(2)}, u32[]{:S(2)}) %collective-permute-start.18) | collective-permute-done | bytes 65568 | tf_op jit(solution)/shard_map/ppermute | solution.py:223
  68.8 1.8 %collective-permute-done.17.group_mate_ref = bf16[8,4,1024]{2,1,0:T(4,128)(2,1)S(1)} collective-permute-done((bf16[8,4,1024]{2,1,0:T(4,128)(2,1)S(1)}, bf16[8,4,1024]{2,1,0:T(4,128)(2,1)S(1)}, u32[]{:S(2)}, u32[]{:S(2)}) %collective-permute-start.17) | collective-permute-done | bytes 65568 | tf_op jit(solution)/shard_map/ppermute | solution.py:223
  70.7 10.5 %all_to_all.11.branch_ref = bf16[8,4,1024]{2,1,0:T(4,128)(2,1)S(1)} all-to-all(bf16[8,4,1024]{2,1,0:T(4,128)(2,1)S(1)} %branch.1), channel_id=1, replica_groups=mesh['groups'=2,'fsdp'=8,'tp'=2] {'fsdp'}, dimensions={0} | all-to-all | bytes 131072 | tf_op jit(solution)/shard_map/all_to_all | solution.py:298
  (72 shorter events, 13.2 us)
Async XLA Ops:
  0.6 6.7 %collective-permute-start.2 = (bf16[4,4096]{1,0:T(4,128)(2,1)}, bf16[4,4096]{1,0:T(4,128)(2,1)S(1)}, u32[]{:S(2)}, u32[]{:S(2)}) collective-permute-start(bf16[4,4096]{1,0:T(4,128)(2,1)} %tok_ref.1), channel_id=1, source_target_pairs={{0,17},{1,16},{16,1},{17,0},{2,19},{3,18},{18,3},{19,2},{4,21},{5,... | collective-permute-start | bytes 98312 | tf_op jit(solution)/shard_map/ppermute | solution.py:223
  3.1 4.3 %collective-permute-start.1 = (bf16[4,4096]{1,0:T(4,128)(2,1)}, bf16[4,4096]{1,0:T(4,128)(2,1)S(1)}, u32[]{:S(2)}, u32[]{:S(2)}) collective-permute-start(bf16[4,4096]{1,0:T(4,128)(2,1)} %tok_ref.1), channel_id=1, source_target_pairs={{0,16},{16,0},{1,17},{17,1},{2,18},{18,2},{3,19},{19,3},{4,20},{20... | collective-permute-start | bytes 98312 | tf_op jit(solution)/shard_map/ppermute | solution.py:223
  3.7 3.6 %collective-permute-start = (bf16[4,4096]{1,0:T(4,128)(2,1)}, bf16[4,4096]{1,0:T(4,128)(2,1)S(1)}, u32[]{:S(2)}, u32[]{:S(2)}) collective-permute-start(bf16[4,4096]{1,0:T(4,128)(2,1)} %tok_ref.1), channel_id=1, source_target_pairs={{0,1},{1,0},{2,3},{3,2},{4,5},{5,4},{6,7},{7,6},{8,9},{9,8},{10,11... | collective-permute-start | bytes 98312 | tf_op jit(solution)/shard_map/ppermute | solution.py:223
  3.8 3.6 %collective-permute-start.3 = (f32[1,4096]{1,0:T(1,128)}, f32[1,4096]{1,0:T(1,128)S(1)}, u32[]{:S(2)}, u32[]{:S(2)}) collective-permute-start(f32[1,4096]{1,0:T(1,128)} %bitcast.13), channel_id=1, source_target_pairs={{0,1},{1,0},{2,3},{3,2},{4,5},{5,4},{6,7},{7,6},{8,9},{9,8},{10,11... | collective-permute-start | bytes 49160 | tf_op jit(solution)/shard_map/ppermute | solution.py:223
  25.1 7.4 %collective-permute-start.10 = (s16[272,512]{1,0:T(8,128)(2,1)S(1)}, s16[272,512]{1,0:T(8,128)(2,1)S(1)}, u32[]{:S(2)}, u32[]{:S(2)}) collective-permute-start(s16[272,512]{1,0:T(8,128)(2,1)S(1)} %get-tuple-element.25), channel_id=1, source_target_pairs={{0,2},{2,0},{4,6},{6,4},{8,10},{10,8},{12,14},{14,12},{1,3},{3,1},... | collective-permute-start | bytes 835592 | tf_op jit(solution)/shard_map/ppermute | solution.py:223
  27.9 8.6 %collective-permute-start.4 = (s16[272,512]{1,0:T(8,128)(2,1)S(1)}, s16[272,512]{1,0:T(8,128)(2,1)S(1)}, u32[]{:S(2)}, u32[]{:S(2)}) collective-permute-start(s16[272,512]{1,0:T(8,128)(2,1)S(1)} %get-tuple-element.19), channel_id=1, source_target_pairs={{0,4},{2,6},{4,0},{6,2},{8,12},{10,14},{12,8},{14,10},{1,5},{3,7},... | collective-permute-start | bytes 835592 | tf_op jit(solution)/shard_map/ppermute | solution.py:223
  32.6 5.8 %collective-permute-start.11 = (s16[144,512]{1,0:T(8,128)(2,1)S(1)}, s16[144,512]{1,0:T(8,128)(2,1)S(1)}, u32[]{:S(2)}, u32[]{:S(2)}) collective-permute-start(s16[144,512]{1,0:T(8,128)(2,1)S(1)} %get-tuple-element.27), channel_id=1, source_target_pairs={{0,4},{2,6},{4,0},{6,2},{8,12},{10,14},{12,8},{14,10},{1,5},{3,7},... | collective-permute-start | bytes 442376 | tf_op jit(solution)/shard_map/ppermute | solution.py:223
  36.7 5.2 %collective-permute-start.5 = (s16[144,512]{1,0:T(8,128)(2,1)S(1)}, s16[144,512]{1,0:T(8,128)(2,1)S(1)}, u32[]{:S(2)}, u32[]{:S(2)}) collective-permute-start(s16[144,512]{1,0:T(8,128)(2,1)S(1)} %get-tuple-element.21), channel_id=1, source_target_pairs={{0,2},{2,0},{4,6},{6,4},{8,10},{10,8},{12,14},{14,12},{1,3},{3,1},... | collective-permute-start | bytes 442376 | tf_op jit(solution)/shard_map/ppermute | solution.py:223
  38.5 20.2 %slice-start = ((s8[16777216]{0:T(1024)(128)(4,1)}), s8[4194304]{0:T(1024)(128)(4,1)S(1)}, s32[]{:S(2)}) async-start(s8[16777216]{0:T(1024)(128)(4,1)} %bitcast.7), calls=%async_computation.2 | async-start | bytes 8388608
  38.5 20.2 %slice-start.1 = ((s8[16777216]{0:T(1024)(128)(4,1)}), s8[4194304]{0:T(1024)(128)(4,1)S(1)}, s32[]{:S(2)}) async-start(s8[16777216]{0:T(1024)(128)(4,1)} %bitcast.7), calls=%async_computation.3 | async-start | bytes 8388608
  38.6 7.1 %collective-permute-start.12 = (s16[80,512]{1,0:T(8,128)(2,1)S(1)}, s16[80,512]{1,0:T(8,128)(2,1)S(1)}, u32[]{:S(2)}, u32[]{:S(2)}) collective-permute-start(s16[80,512]{1,0:T(8,128)(2,1)S(1)} %get-tuple-element.29), channel_id=1, source_target_pairs={{0,8},{2,10},{4,12},{6,14},{8,0},{10,2},{12,4},{14,6},{1,9},{3,11}... | collective-permute-start | bytes 245768 | tf_op jit(solution)/shard_map/ppermute | solution.py:223
  41.9 16.8 %slice-start.3 = ((s8[16777216]{0:T(1024)(128)(4,1)}), s8[4194304]{0:T(1024)(128)(4,1)S(1)}, s32[]{:S(2)}) async-start(s8[16777216]{0:T(1024)(128)(4,1)} %bitcast.7), calls=%async_computation.5 | async-start | bytes 8388608
  42.0 6.7 %collective-permute-start.6 = (s16[80,512]{1,0:T(8,128)(2,1)S(1)}, s16[80,512]{1,0:T(8,128)(2,1)S(1)}, u32[]{:S(2)}, u32[]{:S(2)}) collective-permute-start(s16[80,512]{1,0:T(8,128)(2,1)S(1)} %get-tuple-element.23), channel_id=1, source_target_pairs={{0,8},{2,10},{4,12},{6,14},{8,0},{10,2},{12,4},{14,6},{1,9},{3,11}... | collective-permute-start | bytes 245768 | tf_op jit(solution)/shard_map/ppermute | solution.py:223
  45.7 5.2 %collective-permute-start.13 = (bf16[1,64,256]{2,1,0:T(8,128)(2,1)S(1)}, bf16[1,64,256]{2,1,0:T(8,128)(2,1)S(1)}, u32[]{:S(2)}, u32[]{:S(2)}) collective-permute-start(bf16[1,64,256]{2,1,0:T(8,128)(2,1)S(1)} %hidden_0.1.mine_ref), channel_id=1, source_target_pairs={{0,8},{2,10},{4,12},{6,14},{8,0},{10,2},{12,4},{14,6},{1,9},{3,11}... | collective-permute-start | bytes 98312 | tf_op jit(solution)/shard_map/ppermute | solution.py:223
  48.7 5.2 %collective-permute-start.7 = (bf16[1,64,256]{2,1,0:T(8,128)(2,1)S(1)}, bf16[1,64,256]{2,1,0:T(8,128)(2,1)S(1)}, u32[]{:S(2)}, u32[]{:S(2)}) collective-permute-start(bf16[1,64,256]{2,1,0:T(8,128)(2,1)S(1)} %hidden_1.1.mine_ref), channel_id=1, source_target_pairs={{0,8},{2,10},{4,12},{6,14},{8,0},{10,2},{12,4},{14,6},{1,9},{3,11}... | collective-permute-start | bytes 98312 | tf_op jit(solution)/shard_map/ppermute | solution.py:223
  50.9 4.3 %collective-permute-start.14 = (bf16[2,64,256]{2,1,0:T(8,128)(2,1)S(1)}, bf16[2,64,256]{2,1,0:T(8,128)(2,1)S(1)}, u32[]{:S(2)}, u32[]{:S(2)}) collective-permute-start(bf16[2,64,256]{2,1,0:T(8,128)(2,1)S(1)} %join_2_0.1.mine_ref), channel_id=1, source_target_pairs={{0,4},{2,6},{4,0},{6,2},{8,12},{10,14},{12,8},{14,10},{1,5},{3,7},... | collective-permute-start | bytes 196616 | tf_op jit(solution)/shard_map/ppermute | solution.py:223
  53.9 4.3 %collective-permute-start.8 = (bf16[2,64,256]{2,1,0:T(8,128)(2,1)S(1)}, bf16[2,64,256]{2,1,0:T(8,128)(2,1)S(1)}, u32[]{:S(2)}, u32[]{:S(2)}) collective-permute-start(bf16[2,64,256]{2,1,0:T(8,128)(2,1)S(1)} %join_2_1.1.mine_ref), channel_id=1, source_target_pairs={{0,2},{2,0},{4,6},{6,4},{8,10},{10,8},{12,14},{14,12},{1,3},{3,1},... | collective-permute-start | bytes 196616 | tf_op jit(solution)/shard_map/ppermute | solution.py:223
  55.2 5.0 %collective-permute-start.15 = (bf16[4,64,256]{2,1,0:T(8,128)(2,1)S(1)}, bf16[4,64,256]{2,1,0:T(8,128)(2,1)S(1)}, u32[]{:S(2)}, u32[]{:S(2)}) collective-permute-start(bf16[4,64,256]{2,1,0:T(8,128)(2,1)S(1)} %join_4_0.1.hidden_ref), channel_id=1, source_target_pairs={{0,2},{2,0},{4,6},{6,4},{8,10},{10,8},{12,14},{14,12},{1,3},{3,1},... | collective-permute-start | bytes 393224 | tf_op jit(solution)/shard_map/ppermute | solution.py:223
  58.2 5.0 %collective-permute-start.9 = (bf16[4,64,256]{2,1,0:T(8,128)(2,1)S(1)}, bf16[4,64,256]{2,1,0:T(8,128)(2,1)S(1)}, u32[]{:S(2)}, u32[]{:S(2)}) collective-permute-start(bf16[4,64,256]{2,1,0:T(8,128)(2,1)S(1)} %join_4_1.1.hidden_ref), channel_id=1, source_target_pairs={{0,4},{2,6},{4,0},{6,2},{8,12},{10,14},{12,8},{14,10},{1,5},{3,7},... | collective-permute-start | bytes 393224 | tf_op jit(solution)/shard_map/ppermute | solution.py:223
  61.6 19.6 %copy-start.1 = (bf16[4,4096]{1,0:T(4,128)(2,1)S(1)}, bf16[4,4096]{1,0:T(4,128)(2,1)}, u32[]{:S(2)}) copy-start(bf16[4,4096]{1,0:T(4,128)(2,1)} %tok_ref.1) | copy-start | bytes 98308
  61.6 19.6 %copy-start.2 = (f32[4096]{0:T(1024)S(1)}, f32[4096]{0:T(1024)}, u32[]{:S(2)}) copy-start(f32[4096]{0:T(1024)} %param.19) | copy-start | bytes 49156
  64.6 6.0 %collective-permute-start.16 = (f32[8,4,1024]{2,1,0:T(4,128)S(1)}, f32[8,4,1024]{2,1,0:T(4,128)S(1)}, u32[]{:S(2)}, u32[]{:S(2)}) collective-permute-start(f32[8,4,1024]{2,1,0:T(4,128)S(1)} %get-tuple-element.30.keep_ref), channel_id=1, source_target_pairs={{0,1},{1,0},{2,3},{3,2},{4,5},{5,4},{6,7},{7,6},{8,9},{9,8},{10,11... | collective-permute-start | bytes 393224 | tf_op jit(solution)/shard_map/ppermute | solution.py:223
  64.7 4.1 %collective-permute-start.18 = (bf16[8,4,1024]{2,1,0:T(4,128)(2,1)S(1)}, bf16[8,4,1024]{2,1,0:T(4,128)(2,1)S(1)}, u32[]{:S(2)}, u32[]{:S(2)}) collective-permute-start(bf16[8,4,1024]{2,1,0:T(4,128)(2,1)S(1)} %get-tuple-element.31), channel_id=1, source_target_pairs={{0,17},{1,16},{16,1},{17,0},{2,19},{3,18},{18,3},{19,2},{4,21},{5,... | collective-permute-start | bytes 196616 | tf_op jit(solution)/shard_map/ppermute | solution.py:223
  66.4 4.3 %collective-permute-start.17 = (bf16[8,4,1024]{2,1,0:T(4,128)(2,1)S(1)}, bf16[8,4,1024]{2,1,0:T(4,128)(2,1)S(1)}, u32[]{:S(2)}, u32[]{:S(2)}) collective-permute-start(bf16[8,4,1024]{2,1,0:T(4,128)(2,1)S(1)} %get-tuple-element.31), channel_id=1, source_target_pairs={{0,16},{16,0},{1,17},{17,1},{2,18},{18,2},{3,19},{19,3},{4,20},{20... | collective-permute-start | bytes 196616 | tf_op jit(solution)/shard_map/ppermute | solution.py:223
  (10 other events, 142.9 us)

commit v3 on v2

v3 whole, which is shorter than its diff:
```python
import functools

import jax
import jax.numpy as jnp
from jax import lax
from jax.experimental import pallas as pl
from jax.experimental.pallas import tpu as pltpu
from jax.sharding import PartitionSpec as P

TILE = 128
CODE_ROWS = 16
LOG2_E, LN_2 = 1.4426950408889634, 0.6931471805599453
BF16, F32 = jnp.bfloat16, jnp.float32
VMEM_SPEC = pl.BlockSpec(memory_space=pltpu.VMEM)
SMEM_SPEC = pl.BlockSpec(memory_space=pltpu.SMEM)


def params(mib):
    return pltpu.CompilerParams(vmem_limit_bytes=mib << 20)


def dequantize(codes, scales):
    tile_rows = codes.shape[0] // scales.shape[0]
    tile_cols = codes.shape[1] // scales.shape[1]
    blocks = codes.astype(F32).reshape(scales.shape[0], tile_rows, scales.shape[1], tile_cols)
    scaled = blocks * scales.astype(F32)[:, None, :, None]
    return scaled.reshape(codes.shape).astype(BF16)


def rms_normed(rows_in, norm_gain):
    resid = rows_in.astype(F32)
    mean_sq = jnp.mean(resid * resid, axis=-1, keepdims=True)
    return (resid * lax.rsqrt(mean_sq + 1e-05) * norm_gain.astype(F32)).astype(BF16)


def body_any(tokens, lengths, norm_gain, gate_codes, gate_scales, up_codes, up_scales, down_codes, down_scales, value_head):
    rows = tokens.shape[0]
    feature_rows = lax.all_gather(tokens, "tp", axis=1, tiled=True)
    normed = rms_normed(feature_rows, norm_gain)
    x = lax.all_to_all(normed, "fsdp", split_axis=1, concat_axis=0, tiled=True)
    gate = jnp.dot(x, dequantize(gate_codes, gate_scales), preferred_element_type=F32)
    up = jnp.dot(x, dequantize(up_codes, up_scales), preferred_element_type=F32)
    gate = lax.psum_scatter(gate, "fsdp", scatter_dimension=1, tiled=True)
    up = lax.psum_scatter(up, "fsdp", scatter_dimension=1, tiled=True)
    hidden = (jax.nn.silu(gate) * up).astype(BF16)
    hidden = lax.all_gather(hidden, "fsdp", axis=1, tiled=True)
    part = lax.dot_general(
        hidden, dequantize(down_codes, down_scales), (((1,), (1,)), ((), ())), preferred_element_type=F32
    )
    part = lax.all_to_all(part, "fsdp", split_axis=0, concat_axis=1, tiled=True)
    branch = lax.psum_scatter(part, "tp", scatter_dimension=1, tiled=True)
    layer_out = (tokens.astype(F32) + branch).astype(BF16)
    head = jnp.dot(layer_out.astype(F32), value_head, precision=lax.Precision.HIGHEST)
    head = lax.psum(head, "tp")
    live = jnp.arange(rows) < lengths[0]
    return layer_out, jnp.where(live, head, F32(0.0))


def norm_kernel(place_ref, mine_ref, core_mate_ref, gain_ref, gate_scl_ref, up_scl_ref, down_scl_ref, *refs):
    out_ref, gu_out_ref, down_out_ref = refs[-3:]
    gu_out_ref[0] = gate_scl_ref[...].astype(F32)
    gu_out_ref[1] = up_scl_ref[...].astype(F32)
    down_out_ref[...] = down_scl_ref[...].astype(F32)
    _, rows, width = out_ref.shape
    n = gain_ref.shape[0] // width
    per = mine_ref.shape[1] // width
    resid = [ref[...].astype(F32) for ref in (mine_ref, core_mate_ref)]
    total = sum(jnp.sum(r * r, axis=-1, keepdims=True) for r in resid)
    inv = lax.rsqrt(total * (1.0 / (n * width)) + 1e-05)
    for side, r in enumerate(resid):
        for i in range(per):
            c = (place_ref[1] ^ side) * per + i
            gain = gain_ref[pl.ds(pl.multiple_of(c * width, TILE), width)].astype(F32).reshape(1, width)
            chunk = (r[:, i * width : (i + 1) * width] * inv * gain).astype(BF16)
            for g in range(2):
                out_ref[g * n + c] = chunk


def hold_kernel(ref, *refs):
    refs[-1][...] = ref[...]


def rows_kernel(got_ref, out_ref, rows_ref):
    count, rows, _ = got_ref.shape
    for j in range(count):
        rows_ref[j * rows : (j + 1) * rows] = got_ref[j].astype(F32)
    out_ref[...] = rows_ref[...].astype(BF16)


def encode(values, out_ref):
    count, rows = len(values), values[0].shape[0]
    top = functools.reduce(jnp.maximum, [jnp.max(jnp.abs(v), axis=0, keepdims=True) for v in values])
    power = jnp.clip(jnp.ceil(jnp.log(top) * LOG2_E), -100.0, 100.0)
    unit = jnp.exp((14.0 - power) * LN_2)
    for i, v in enumerate(values):
        out_ref[i * rows : (i + 1) * rows] = jnp.round(v * unit).astype(jnp.int32).astype(jnp.int16)
    tail = (out_ref.shape[0] - count * rows, out_ref.shape[1])
    out_ref[count * rows :] = jnp.broadcast_to(power.astype(jnp.int32), tail).astype(jnp.int16)


def decode(got_ref, rows, entries):
    count = (got_ref.shape[0] - CODE_ROWS) // rows
    power = got_ref[count * rows :].astype(jnp.int32).astype(F32)[:1]
    unit = jnp.exp((power - 14.0) * LN_2)
    return [got_ref[i * rows : (i + 1) * rows].astype(jnp.int32).astype(F32) * unit for i in entries]


def scaled(codes, scale_of, down, across):
    tiles = [
        [
            codes[r * TILE : (r + 1) * TILE, c * TILE : (c + 1) * TILE] * scale_of(r, c).astype(BF16)
            for c in range(across)
        ]
        for r in range(down)
    ]
    return jnp.concatenate([jnp.concatenate(row, axis=1) for row in tiles], axis=0)


def gate_up_kernel(blocks, n, place_ref, scl_ref, x_ref, gate_ref, up_ref, _, *refs):
    me, group = place_ref[0], place_ref[3]
    x = x_ref[...]
    sums_ref = refs[-1]
    wide = sums_ref.shape[-1] // 2
    units, step = wide // TILE, 2 * TILE
    for (piece, q), out_ref in zip(blocks, refs):
        total_ref = sums_ref if q else out_ref
        for i in range(2):
            block = (group * 2 + piece) * n + (me ^ (q + i * (n // 2)))
            cols = pl.ds(pl.multiple_of(block * wide, TILE), wide)
            for m, ref in enumerate((gate_ref, up_ref)):
                total = None
                for k in range(0, x.shape[1], step):
                    w = scaled(
                        ref[k : k + step, cols], lambda r, c: scl_ref[m, k // TILE + r, block * units + c], 2, units
                    )
                    part = jnp.dot(x[:, k : k + step], w, preferred_element_type=F32)
                    total = part if total is None else total + part
                total_ref[i, :, m * wide : (m + 1) * wide] = total
        if q:
            encode([total_ref[i] for i in range(2)], out_ref)


def both_kernel(keep_ref, *refs):
    got_refs, (stay_ref, send_ref) = refs[:3], refs[-2:]
    count, rows = stay_ref.shape[0], stay_ref.shape[1]
    total = [keep_ref[i] for i in range(count)]
    for ref in got_refs:
        total = [t + v for t, v in zip(total, decode(ref, rows, range(count)))]
    for i in range(count):
        stay_ref[i] = total[i]
    encode(total, send_ref)


def hidden_kernel(keep_ref, got_ref, out_ref):
    count, wide = out_ref.shape[0], out_ref.shape[-1]
    got = decode(got_ref, keep_ref.shape[1], range(count))
    for i in range(count):
        total = keep_ref[i] + got[count - 1 - i]
        gate, up = total[:, :wide], total[:, wide:]
        out_ref[i] = (gate / (1.0 + jnp.exp(-gate)) * up).astype(BF16)


def down_kernel(piece, blocks, n, begin, last, place_ref, scl_ref, codes_ref, *refs):
    me, group = place_ref[0], place_ref[3]
    hidden_refs, out_ref = refs[: len(blocks)], refs[-1]
    wide, depth, step = hidden_refs[0].shape[-1], codes_ref.shape[0], 2 * TILE
    units = wide // TILE
    for r in range(0, depth, step):
        total = None if begin else refs[len(blocks)][:, r : r + step]
        for q, hidden_ref in zip(blocks, hidden_refs):
            for i in range(2):
                block = (group * 2 + piece) * n + (me ^ (q + i * (n // 2)))
                cols = pl.ds(pl.multiple_of(block * wide, TILE), wide)
                w = scaled(codes_ref[r : r + step, cols], lambda t, c: scl_ref[r // TILE + t, block * units + c], 2, units)
                part = lax.dot_general(hidden_ref[i], w, (((1,), (1,)), ((), ())), preferred_element_type=F32)
                total = part if total is None else total + part
        if not last:
            out_ref[:, r : r + step] = total
            continue
        count, rows, _ = out_ref.shape
        for j in range(count):
            out_ref[j, :, r : r + step] = total[j * rows : (j + 1) * rows].astype(BF16)


def group_sum_kernel(got_ref, out_ref):
    n = out_ref.shape[0]
    for c in range(n):
        out_ref[c] = got_ref[c].astype(F32) + got_ref[n + c].astype(F32)


def final_kernel(place_ref, tok_ref, tok_mate_ref, branch_ref, branch_mate_ref, head_ref, head_mate_ref, out_ref, values_ref):
    n, rows, width = branch_ref.shape
    per = out_ref.shape[1] // width
    core = place_ref[1]
    total = jnp.zeros((rows, 1), F32)
    for side, (tok, head) in enumerate(((tok_ref, head_ref), (tok_mate_ref, head_mate_ref))):
        for i in range(per):
            cols = slice(i * width, (i + 1) * width)
            c = (core ^ side) * per + i
            branch = branch_ref[c] + branch_mate_ref[c]
            layer = (tok[:, cols].astype(F32) + branch).astype(BF16)
            if side == 0:
                out_ref[:, cols] = layer
            total = total + jnp.sum(layer.astype(F32) * head[:, cols], axis=-1, keepdims=True)
    row, at = (lax.broadcasted_iota(jnp.int32, (rows, rows), axis) for axis in (0, 1))
    taken = (row == at) & (row < place_ref[2])
    values_ref[...] = jnp.sum(jnp.where(taken, total, 0.0), axis=0, keepdims=True)


def call(kernel, name, ins, outs, limit=8, cost=None, scratch=()):
    specs = [x[1] if isinstance(x, tuple) else VMEM_SPEC for x in ins]
    return pl.pallas_call(
        kernel,
        in_specs=specs,
        out_specs=jax.tree.map(lambda _: VMEM_SPEC, outs),
        out_shape=outs,
        scratch_shapes=scratch,
        compiler_params=params(limit),
        cost_estimate=cost,
        name=name,
    )(*[x[0] if isinstance(x, tuple) else x for x in ins])


def body_split(n, tokens, lengths, norm_gain, gate_codes, gate_scales, up_codes, up_scales, down_codes, down_scales, value_head):
    rows, d_half = tokens.shape
    d, depth = 2 * d_half, gate_codes.shape[0]
    group_cols = gate_codes.shape[1] // 2
    units = group_cols // (2 * n * TILE)
    all_rows, half = 2 * n * rows, n // 2
    me, group, core = (lax.axis_index(a).astype(jnp.int32) for a in ("fsdp", "groups", "tp"))
    place = jnp.stack([me, core, lengths[0], group])
    spot = (place, SMEM_SPEC)
    shape = jax.ShapeDtypeStruct

    def swap(x, axis, bit):
        return lax.ppermute(x, axis, [(i, i ^ bit) for i in range(n if axis == "fsdp" else 2)])

    hbm = lambda x: pltpu.with_memory_space_constraint(x, pltpu.HBM)
    vmem = lambda x: pltpu.with_memory_space_constraint(x, pltpu.VMEM)
    unread = lambda x: (x, pl.BlockSpec(memory_space=pl.ANY))

    tok_mate = swap(tokens, "tp", 1)
    head = value_head.reshape(1, d_half)
    head_mate = swap(head, "tp", 1)
    whole = lambda x: (hbm(x), pl.BlockSpec())
    normed, gu_scales, down_scales = call(
        norm_kernel,
        "norm",
        [spot, whole(tokens), tok_mate]
        + [whole(a) for a in (norm_gain, gate_scales, up_scales, down_scales)]
        + [unread(head_mate)],
        [
            shape((2 * n, rows, depth), BF16),
            shape((2, *gate_scales.shape), F32),
            shape(down_scales.shape, F32),
        ],
    )
    normed = call(
        hold_kernel,
        "hold",
        [normed] + [unread(hbm(a)) for a in (gate_codes, up_codes, down_codes)],
        shape(normed.shape, BF16),
    )
    both = ("groups", "fsdp")
    x = call(
        rows_kernel,
        "rows",
        [lax.all_to_all(normed, both, 0, 0, tiled=True)],
        shape((all_rows, depth), BF16),
        scratch=[pltpu.VMEM((all_rows, depth), F32)],
    )

    wide = units * TILE
    codes = [vmem(c) for c in (gate_codes, up_codes)]
    cost = lambda share, width: pl.CostEstimate(
        flops=2 * all_rows * depth * width * n // share, transcendentals=0, bytes_accessed=2 * depth * width * n // share
    )

    coded = lambda count: shape((count * all_rows + CODE_ROWS, 2 * wide), jnp.int16)

    far = n // 2
    sums = shape((2, all_rows, 2 * wide), F32)

    def gate_up(name, after, *blocks):
        return call(
            functools.partial(gate_up_kernel, blocks, n),
            f"gate_up_{name}",
            [spot, (gu_scales, SMEM_SPEC), x, *codes, unread(after)],
            [coded(2) if q else sums for _, q in blocks],
            cost=cost(2, 2 * wide),
            scratch=[pltpu.VMEM(sums.shape, F32)],
        )

    orders = ((1, 3, 2), (2, 3, 1))
    kept, got, after = [], [], x
    for p, (q1, q2, q3) in enumerate(orders):
        send_1, send_2 = gate_up(f"{p}_first", after, (p, q1), (p, q2))
        send_3, keep = gate_up(f"{p}_second", send_1, (p, q3), (p, 0))
        got.append([swap(send, "fsdp", q) for send, q in ((send_1, q1), (send_2, q2), (send_3, q3))])
        kept.append(keep)
        after = send_3
    branch = None
    for p, order in enumerate(orders):
        late = [unread(hbm(down_codes))] if p else []
        keep, send = call(both_kernel, f"both_{p}", [kept[p], *got[p], *late], [sums, coded(2)])
        hidden = call(hidden_kernel, f"hidden_{p}", [keep, swap(send, "fsdp", far)], shape((2, all_rows, wide), BF16))
        parts = [hidden] + [swap(hidden, "fsdp", q) for q in order]
        for at in ((0, 1), (1, 4)) if p else ((0, 4),):
            last = p == 1 and at[1] == 4
            branch = call(
                functools.partial(down_kernel, p, (0, *order)[slice(*at)], n, branch is None, last),
                f"down_{p}_{at[0]}",
                [spot, (down_scales, SMEM_SPEC), vmem(down_codes), *parts[slice(*at)]]
                + ([] if branch is None else [branch]),
                shape((2 * n, rows, depth), BF16) if last else shape((all_rows, depth), F32),
                cost=cost(2, wide),
            )

    got = lax.all_to_all(branch, both, 0, 0, tiled=True)
    branch = call(group_sum_kernel, "group_sum", [got], shape((n, rows, depth), F32))
    layer_out, values = call(
        final_kernel,
        "final",
        [spot, tokens, tok_mate, branch, swap(branch, "tp", 1), head, head_mate],
        [shape((rows, d_half), BF16), shape((1, rows), F32)],
    )
    return layer_out, values.reshape(rows)


def solution(mesh):
    placed = (
        P(("groups", "fsdp"), "tp"),
        P(("groups", "fsdp")),
        P(),
        P("fsdp", "tp"),
        P("fsdp", "tp"),
        P("fsdp", "tp"),
        P("fsdp", "tp"),
        P("fsdp", "tp"),
        P("fsdp", "tp"),
        P("tp"),
    )
    n = mesh.shape["fsdp"]

    def body(*args):
        codes = args[3]
        fits = (
            n == 8
            and mesh.shape["groups"] == 2
            and mesh.shape["tp"] == 2
            and codes.shape[0] % TILE == 0
            and codes.shape[1] == 8 * n * TILE
        )
        if fits:
            return body_split(n, *args)
        return body_any(*args)

    return jax.shard_map(
        body,
        mesh=mesh,
        in_specs=placed,
        out_specs=(P(("groups", "fsdp"), "tp"), P(("groups", "fsdp"))),
        check_vma=False,
    )
```

time: 82.8 us -> 72.1 us (0.87)
  waiting for transfers between devices: 24.2 us -> 11.7 us
  blocking collectives: 23.8 us -> 27.3 us
  local copies, waits for them, and re-layouts: 2.2 us -> 0.04 us
  other arithmetic: 1.47 us -> 0.08 us
  Pallas kernels: 12.8 us -> 14 us
    ppermute x19 -> x17, waiting for transfers between devices: 24.2 us -> 11.7 us  [swap(): lax.ppermute(x, axis, [(i, i ^ bit) for i in range(n if axis == 'fsdp' el...]
    all_to_all x2, blocking collectives: 23.8 us -> 27.3 us  [the longest x1 16 us: body_split(): lax.all_to_all(normed, both, 0, 0, tiled=True)]
    convert_element_type x2 -> x0, other arithmetic: 1.39 us -> none  [the longest x1 0.71 us: body_split(): gu_scales = jnp.stack([gate_scales, up_scales]).astype(F32)]
    unnamed x30 -> x16, local copies, waits for them, and re-layouts: 1.31 us -> 0.04 us
    pallas_call x19 -> x16, Pallas kernels: 12.8 us -> 14 us  [call(): pl.pallas_call(kernel, in_specs=specs, out_specs=jax.tree.map(lambda _: V...]
    reshape x1 -> x0, local copies, waits for them, and re-layouts: 0.89 us -> none  [body_split(): norm_gain.reshape(1, d)]
    ppermute x19 -> x17, starting transfers between devices: 16.4 us -> 17.2 us  [swap(): lax.ppermute(x, axis, [(i, i ^ bit) for i in range(n if axis == 'fsdp' el...]
  transfers between devices with their start and end apart: 19 -> 17, of which waited for: 13 -> 7; matrix products, arithmetic and copies ran while one was open for 3% -> 0% of each run, Pallas kernels for 9% -> 12%
where the time goes in v3:
time: 72.1 us; the launch traced here: 71.8 us
  blocking collectives  27.3 us (38%)
  starting transfers between devices  17.2 us (24%)
  Pallas kernels  14 us (19%)
  waiting for transfers between devices  11.7 us (16%)
  between operations  1.48 us (2%)
    ppermute x17, starting transfers between devices, swap(): lax.ppermute(x, axis, [(i, i ^ bit) for i in range(n if axis == 'fsdp' el...  17.2 us
    all_to_all x1, blocking collectives, body_split(): lax.all_to_all(normed, both, 0, 0, tiled=True)  16 us
    pallas_call x16, Pallas kernels, call(): pl.pallas_call(kernel, in_specs=specs, out_specs=jax.tree.map(lambda _: V...  14 us
    ppermute x17, waiting for transfers between devices, swap(): lax.ppermute(x, axis, [(i, i ^ bit) for i in range(n if axis == 'fsdp' el...  11.7 us
    all_to_all x1, blocking collectives, body_split(): got = lax.all_to_all(branch, both, 0, 0, tiled=True)  11.2 us
  transfers between devices with their start and end apart: 17, of which 7 were waited for; matrix products, arithmetic and copies ran while one was open for 0% of the time, Pallas kernels for 12%

profile of v3, /device:TPU:0, one launch (start us, length us, event | category | flops | bytes accessed | tf_op | source)
XLA Modules:
  0.0 71.8 jit_solution(13319870391085949141)
XLA Ops:
  2.6 1.0 %norm.1 = (bf16[16,4,1024]{2,1,0:T(4,128)(2,1)S(1)}, f32[2,8,64]{2,1,0:T(8,128)S(1)}, f32[8,64]{1,0:T(8,128)S(1)}) custom-call(s32[4]{0:T(128)S(1)} %pad_add_fusion.place_ref, bf16[4,4096]{1,0:T(4,128)(2,1)} %tok_ref.1, bf16[4,4096]{1,0:T(4,128)(2,1)S(1)} %collective-permute-done.core_mate_ref.tok_mate_ref, bf16[8192]{0:T(1024)(128)(2,1)} %gain_ref.1, ...), custom_call_target="tpu_custom_call" | custom-call | tf_op jit(solution)/shard_map/norm/pallas_call | solution.py:212
  3.6 16.0 %all_to_all.10.got_ref = bf16[16,4,1024]{2,1,0:T(4,128)(2,1)S(1)} all-to-all(bf16[16,4,1024]{2,1,0:T(4,128)(2,1)S(1)} %hold.1), channel_id=1, replica_groups=mesh['groups'=2,'fsdp'=8,'tp'=2] {'groups','fsdp'}, dimensions={0} | all-to-all | bytes 262144 | tf_op jit(solution)/shard_map/all_to_all | solution.py:268
  19.7 1.6 %gate_up_0_first.1 = (s16[144,512]{1,0:T(8,128)(2,1)S(1)}, s16[144,512]{1,0:T(8,128)(2,1)S(1)}) custom-call(s32[4]{0:T(128)S(1)} %pad_add_fusion.place_ref, f32[2,8,64]{2,1,0:T(8,128)S(1)} %get-tuple-element.20.scl_ref, bf16[64,1024]{1,0:T(8,128)(2,1)S(1)} %rows.1.x_ref._, bf16[1024,8192]{1,0:T(8,128)(2,1)S(1)} %copy-done, bf16[1024,8192]{1,0:T(8,128)(2,1)S(1)} %copy-done.1, ...), custom_call_target="tpu_custom_call" | custom-call | flops 268435456 | bytes 4194304 | tf_op jit(solution)/shard_map/gate_up_0_first/pallas_call | solution.py:212
  22.0 1.5 %collective-permute-start.9 = (s16[144,512]{1,0:T(8,128)(2,1)S(1)}, s16[144,512]{1,0:T(8,128)(2,1)S(1)}, u32[]{:S(2)}, u32[]{:S(2)}) collective-permute-start(s16[144,512]{1,0:T(8,128)(2,1)S(1)} %get-tuple-element.22._), channel_id=1, source_target_pairs={{0,2},{2,0},{4,6},{6,4},{8,10},{10,8},{12,14},{14,12},{1,3},{3,1},... | collective-permute-start | bytes 442376 | tf_op jit(solution)/shard_map/ppermute | solution.py:236
  23.5 1.6 %gate_up_0_second.1 = (s16[144,512]{1,0:T(8,128)(2,1)S(1)}, f32[2,64,512]{2,1,0:T(8,128)S(1)}) custom-call(s32[4]{0:T(128)S(1)} %pad_add_fusion.place_ref, f32[2,8,64]{2,1,0:T(8,128)S(1)} %get-tuple-element.20.scl_ref, bf16[64,1024]{1,0:T(8,128)(2,1)S(1)} %rows.1.x_ref._, bf16[1024,8192]{1,0:T(8,128)(2,1)S(1)} %copy-done, bf16[1024,8192]{1,0:T(8,128)(2,1)S(1)} %copy-done.1, ...), custom_call_target="tpu_custom_call" | custom-call | flops 268435456 | bytes 4194304 | tf_op jit(solution)/shard_map/gate_up_0_second/pallas_call | solution.py:212
  25.1 1.4 %collective-permute-start.11 = (s16[144,512]{1,0:T(8,128)(2,1)S(1)}, s16[144,512]{1,0:T(8,128)(2,1)S(1)}, u32[]{:S(2)}, u32[]{:S(2)}) collective-permute-start(s16[144,512]{1,0:T(8,128)(2,1)S(1)} %get-tuple-element.23._), channel_id=1, source_target_pairs={{0,4},{2,6},{4,0},{6,2},{8,12},{10,14},{12,8},{14,10},{1,5},{3,7},... | collective-permute-start | bytes 442376 | tf_op jit(solution)/shard_map/ppermute | solution.py:236
  26.5 1.6 %gate_up_1_first.1 = (s16[144,512]{1,0:T(8,128)(2,1)S(1)}, s16[144,512]{1,0:T(8,128)(2,1)S(1)}) custom-call(s32[4]{0:T(128)S(1)} %pad_add_fusion.place_ref, f32[2,8,64]{2,1,0:T(8,128)S(1)} %get-tuple-element.20.scl_ref, bf16[64,1024]{1,0:T(8,128)(2,1)S(1)} %rows.1.x_ref._, bf16[1024,8192]{1,0:T(8,128)(2,1)S(1)} %copy-done, bf16[1024,8192]{1,0:T(8,128)(2,1)S(1)} %copy-done.1, ...), custom_call_target="tpu_custom_call" | custom-call | flops 268435456 | bytes 4194304 | tf_op jit(solution)/shard_map/gate_up_1_first/pallas_call | solution.py:212
  28.9 1.9 %collective-permute-start.2 = (s16[144,512]{1,0:T(8,128)(2,1)S(1)}, s16[144,512]{1,0:T(8,128)(2,1)S(1)}, u32[]{:S(2)}, u32[]{:S(2)}) collective-permute-start(s16[144,512]{1,0:T(8,128)(2,1)S(1)} %get-tuple-element.24._), channel_id=1, source_target_pairs={{0,4},{2,6},{4,0},{6,2},{8,12},{10,14},{12,8},{14,10},{1,5},{3,7},... | collective-permute-start | bytes 442376 | tf_op jit(solution)/shard_map/ppermute | solution.py:236
  30.8 1.6 %gate_up_1_second.1 = (s16[144,512]{1,0:T(8,128)(2,1)S(1)}, f32[2,64,512]{2,1,0:T(8,128)S(1)}) custom-call(s32[4]{0:T(128)S(1)} %pad_add_fusion.place_ref, f32[2,8,64]{2,1,0:T(8,128)S(1)} %get-tuple-element.20.scl_ref, bf16[64,1024]{1,0:T(8,128)(2,1)S(1)} %rows.1.x_ref._, bf16[1024,8192]{1,0:T(8,128)(2,1)S(1)} %copy-done, bf16[1024,8192]{1,0:T(8,128)(2,1)S(1)} %copy-done.1, ...), custom_call_target="tpu_custom_call" | custom-call | flops 268435456 | bytes 4194304 | tf_op jit(solution)/shard_map/gate_up_1_second/pallas_call | solution.py:212
  32.4 1.0 %collective-permute-start.4 = (s16[144,512]{1,0:T(8,128)(2,1)S(1)}, s16[144,512]{1,0:T(8,128)(2,1)S(1)}, u32[]{:S(2)}, u32[]{:S(2)}) collective-permute-start(s16[144,512]{1,0:T(8,128)(2,1)S(1)} %get-tuple-element.27), channel_id=1, source_target_pairs={{0,2},{2,0},{4,6},{6,4},{8,10},{10,8},{12,14},{14,12},{1,3},{3,1},... | collective-permute-start | bytes 442376 | tf_op jit(solution)/shard_map/ppermute | solution.py:236
  33.6 0.9 %collective-permute-start.12 = (s16[144,512]{1,0:T(8,128)(2,1)S(1)}, s16[144,512]{1,0:T(8,128)(2,1)S(1)}, u32[]{:S(2)}, u32[]{:S(2)}) collective-permute-start(s16[144,512]{1,0:T(8,128)(2,1)S(1)} %get-tuple-element.33), channel_id=1, source_target_pairs={{0,8},{2,10},{4,12},{6,14},{8,0},{10,2},{12,4},{14,6},{1,9},{3,11}... | collective-permute-start | bytes 442376 | tf_op jit(solution)/shard_map/ppermute | solution.py:236
  34.4 1.8 %collective-permute-done.3.refs_1_ = s16[144,512]{1,0:T(8,128)(2,1)S(1)} collective-permute-done((s16[144,512]{1,0:T(8,128)(2,1)S(1)}, s16[144,512]{1,0:T(8,128)(2,1)S(1)}, u32[]{:S(2)}, u32[]{:S(2)}) %collective-permute-start.3) | collective-permute-done | bytes 147488 | tf_op jit(solution)/shard_map/ppermute | solution.py:236
  36.3 2.0 %collective-permute-done.2.refs_0_ = s16[144,512]{1,0:T(8,128)(2,1)S(1)} collective-permute-done((s16[144,512]{1,0:T(8,128)(2,1)S(1)}, s16[144,512]{1,0:T(8,128)(2,1)S(1)}, u32[]{:S(2)}, u32[]{:S(2)}) %collective-permute-start.2) | collective-permute-done | bytes 147488 | tf_op jit(solution)/shard_map/ppermute | solution.py:236
  38.5 1.4 %collective-permute-start.5 = (s16[144,512]{1,0:T(8,128)(2,1)S(1)}, s16[144,512]{1,0:T(8,128)(2,1)S(1)}, u32[]{:S(2)}, u32[]{:S(2)}) collective-permute-start(s16[144,512]{1,0:T(8,128)(2,1)S(1)} %get-tuple-element.29), channel_id=1, source_target_pairs={{0,8},{2,10},{4,12},{6,14},{8,0},{10,2},{12,4},{14,6},{1,9},{3,11}... | collective-permute-start | bytes 442376 | tf_op jit(solution)/shard_map/ppermute | solution.py:236
  39.8 5.8 %collective-permute-done.12.got_ref = s16[144,512]{1,0:T(8,128)(2,1)S(1)} collective-permute-done((s16[144,512]{1,0:T(8,128)(2,1)S(1)}, s16[144,512]{1,0:T(8,128)(2,1)S(1)}, u32[]{:S(2)}, u32[]{:S(2)}) %collective-permute-start.12) | collective-permute-done | bytes 147488 | tf_op jit(solution)/shard_map/ppermute | solution.py:236
  45.8 2.9 %collective-permute-start.14 = (bf16[2,64,256]{2,1,0:T(8,128)(2,1)S(1)}, bf16[2,64,256]{2,1,0:T(8,128)(2,1)S(1)}, u32[]{:S(2)}, u32[]{:S(2)}) collective-permute-start(bf16[2,64,256]{2,1,0:T(8,128)(2,1)S(1)} %hidden_0.1.refs_0_), channel_id=1, source_target_pairs={{0,6},{2,4},{4,2},{6,0},{8,14},{10,12},{12,10},{14,8},{1,7},{3,5},... | collective-permute-start | bytes 196616 | tf_op jit(solution)/shard_map/ppermute | solution.py:236
  49.4 1.5 %collective-permute-start.8 = (bf16[2,64,256]{2,1,0:T(8,128)(2,1)S(1)}, bf16[2,64,256]{2,1,0:T(8,128)(2,1)S(1)}, u32[]{:S(2)}, u32[]{:S(2)}) collective-permute-start(bf16[2,64,256]{2,1,0:T(8,128)(2,1)S(1)} %hidden_1.1.refs_0_), channel_id=1, source_target_pairs={{0,2},{2,0},{4,6},{6,4},{8,10},{10,8},{12,14},{14,12},{1,3},{3,1},... | collective-permute-start | bytes 196616 | tf_op jit(solution)/shard_map/ppermute | solution.py:236
  51.0 1.9 %collective-permute-start.6 = (bf16[2,64,256]{2,1,0:T(8,128)(2,1)S(1)}, bf16[2,64,256]{2,1,0:T(8,128)(2,1)S(1)}, u32[]{:S(2)}, u32[]{:S(2)}) collective-permute-start(bf16[2,64,256]{2,1,0:T(8,128)(2,1)S(1)} %hidden_1.1.refs_0_), channel_id=1, source_target_pairs={{0,4},{2,6},{4,0},{6,2},{8,12},{10,14},{12,8},{14,10},{1,5},{3,7},... | collective-permute-start | bytes 196616 | tf_op jit(solution)/shard_map/ppermute | solution.py:236
  53.1 2.0 %down_0_0.1.refs_1_ = f32[64,1024]{1,0:T(8,128)S(1)} custom-call(s32[4]{0:T(128)S(1)} %pad_add_fusion.place_ref, f32[8,64]{1,0:T(8,128)S(1)} %get-tuple-element.19.scl_ref, bf16[1024,8192]{1,0:T(8,128)(2,1)S(1)} %bitcast.6, bf16[2,64,256]{2,1,0:T(8,128)(2,1)S(1)} %hidden_0.1.refs_0_, bf16[2,64,256]{2,1,0:T(8,128)(2,1)S(1)} %collective-permute-done.13.refs_1_, ...), custom_call_target="tpu_custom_call" | custom-call | flops 134217728 | bytes 2097152 | tf_op jit(solution)/shard_map/down_0_0/pallas_call | solution.py:212
  55.1 1.1 %down_1_0.1.refs_3_ = f32[64,1024]{1,0:T(8,128)S(1)} custom-call(s32[4]{0:T(128)S(1)} %pad_add_fusion.place_ref, f32[8,64]{1,0:T(8,128)S(1)} %get-tuple-element.19.scl_ref, bf16[1024,8192]{1,0:T(8,128)(2,1)S(1)} %bitcast.6, bf16[2,64,256]{2,1,0:T(8,128)(2,1)S(1)} %hidden_1.1.refs_0_, f32[64,1024]{1,0:T(8,128)S(1)} %down_0_0.1.refs_1_), custom_call_target="tpu_custom_call" | custom-call | flops 134217728 | bytes 2097152 | tf_op jit(solution)/shard_map/down_1_0/pallas_call | solution.py:212
  56.2 1.7 %down_1_1.1 = bf16[16,4,1024]{2,1,0:T(4,128)(2,1)S(1)} custom-call(s32[4]{0:T(128)S(1)} %pad_add_fusion.place_ref, f32[8,64]{1,0:T(8,128)S(1)} %get-tuple-element.19.scl_ref, bf16[1024,8192]{1,0:T(8,128)(2,1)S(1)} %bitcast.6, bf16[2,64,256]{2,1,0:T(8,128)(2,1)S(1)} %collective-permute-done.6.refs_0_, bf16[2,64,256]{2,1,0:T(8,128)(2,1)S(1)} %collective-permute-done.7.refs_1_, ...), custom_call_target="tpu_custom_call" | custom-call | flops 134217728 | bytes 2097152 | tf_op jit(solution)/shard_map/down_1_1/pallas_call | solution.py:212
  57.9 11.2 %all_to_all.11.got_ref = bf16[16,4,1024]{2,1,0:T(4,128)(2,1)S(1)} all-to-all(bf16[16,4,1024]{2,1,0:T(4,128)(2,1)S(1)} %down_1_1.1), channel_id=1, replica_groups=mesh['groups'=2,'fsdp'=8,'tp'=2] {'groups','fsdp'}, dimensions={0} | all-to-all | bytes 262144 | tf_op jit(solution)/shard_map/all_to_all | solution.py:319
  69.3 1.3 %collective-permute-done.16.branch_mate_ref = f32[8,4,1024]{2,1,0:T(4,128)S(1)} collective-permute-done((f32[8,4,1024]{2,1,0:T(4,128)S(1)}, f32[8,4,1024]{2,1,0:T(4,128)S(1)}, u32[]{:S(2)}, u32[]{:S(2)}) %collective-permute-start.16) | collective-permute-done | bytes 131104 | tf_op jit(solution)/shard_map/ppermute | solution.py:236
  70.6 1.2 %final.1 = (bf16[4,4096]{1,0:T(4,128)(2,1)}, f32[1,4]{1,0:T(1,128)}) custom-call(s32[4]{0:T(128)S(1)} %pad_add_fusion.place_ref, bf16[4,4096]{1,0:T(4,128)(2,1)S(1)} %copy-done.2, bf16[4,4096]{1,0:T(4,128)(2,1)S(1)} %collective-permute-done.core_mate_ref.tok_mate_ref, f32[8,4,1024]{2,1,0:T(4,128)S(1)} %group_sum.1.branch_ref, ...), custom_call_target="tpu_custom_call" | custom-call | tf_op jit(solution)/shard_map/final/pallas_call | solution.py:212
  (46 shorter events, 4.3 us)
Async XLA Ops:
  0.6 1.6 %collective-permute-start.1 = (f32[1,4096]{1,0:T(1,128)}, f32[1,4096]{1,0:T(1,128)S(1)}, u32[]{:S(2)}, u32[]{:S(2)}) collective-permute-start(f32[1,4096]{1,0:T(1,128)} %bitcast.7), channel_id=1, source_target_pairs={{0,1},{1,0},{2,3},{3,2},{4,5},{5,4},{6,7},{7,6},{8,9},{9,8},{10,11... | collective-permute-start | bytes 49160 | tf_op jit(solution)/shard_map/ppermute | solution.py:236
  1.1 1.4 %collective-permute-start = (bf16[4,4096]{1,0:T(4,128)(2,1)}, bf16[4,4096]{1,0:T(4,128)(2,1)S(1)}, u32[]{:S(2)}, u32[]{:S(2)}) collective-permute-start(bf16[4,4096]{1,0:T(4,128)(2,1)} %tok_ref.1), channel_id=1, source_target_pairs={{0,1},{1,0},{2,3},{3,2},{4,5},{5,4},{6,7},{7,6},{8,9},{9,8},{10,11... | collective-permute-start | bytes 98312 | tf_op jit(solution)/shard_map/ppermute | solution.py:236
  3.5 16.1 %copy-start = (bf16[1024,8192]{1,0:T(8,128)(2,1)S(1)}, bf16[1024,8192]{1,0:T(8,128)(2,1)}, u32[]{:S(2)}) copy-start(bf16[1024,8192]{1,0:T(8,128)(2,1)} %gate_ref.7) | copy-start | bytes 50331652
  3.5 16.1 %copy-start.1 = (bf16[1024,8192]{1,0:T(8,128)(2,1)S(1)}, bf16[1024,8192]{1,0:T(8,128)(2,1)}, u32[]{:S(2)}) copy-start(bf16[1024,8192]{1,0:T(8,128)(2,1)} %up_ref.7) | copy-start | bytes 50331652
  21.3 11.1 %collective-permute-start.10 = (s16[144,512]{1,0:T(8,128)(2,1)S(1)}, s16[144,512]{1,0:T(8,128)(2,1)S(1)}, u32[]{:S(2)}, u32[]{:S(2)}) collective-permute-start(s16[144,512]{1,0:T(8,128)(2,1)S(1)} %get-tuple-element.31), channel_id=1, source_target_pairs={{0,6},{2,4},{4,2},{6,0},{8,14},{10,12},{12,10},{14,8},{1,7},{3,5},... | collective-permute-start | bytes 442376 | tf_op jit(solution)/shard_map/ppermute | solution.py:236
  22.0 11.3 %collective-permute-start.9 = (s16[144,512]{1,0:T(8,128)(2,1)S(1)}, s16[144,512]{1,0:T(8,128)(2,1)S(1)}, u32[]{:S(2)}, u32[]{:S(2)}) collective-permute-start(s16[144,512]{1,0:T(8,128)(2,1)S(1)} %get-tuple-element.22._), channel_id=1, source_target_pairs={{0,2},{2,0},{4,6},{6,4},{8,10},{10,8},{12,14},{14,12},{1,3},{3,1},... | collective-permute-start | bytes 442376 | tf_op jit(solution)/shard_map/ppermute | solution.py:236
  25.1 8.3 %collective-permute-start.11 = (s16[144,512]{1,0:T(8,128)(2,1)S(1)}, s16[144,512]{1,0:T(8,128)(2,1)S(1)}, u32[]{:S(2)}, u32[]{:S(2)}) collective-permute-start(s16[144,512]{1,0:T(8,128)(2,1)S(1)} %get-tuple-element.23._), channel_id=1, source_target_pairs={{0,4},{2,6},{4,0},{6,2},{8,12},{10,14},{12,8},{14,10},{1,5},{3,7},... | collective-permute-start | bytes 442376 | tf_op jit(solution)/shard_map/ppermute | solution.py:236
  28.2 8.1 %collective-permute-start.3 = (s16[144,512]{1,0:T(8,128)(2,1)S(1)}, s16[144,512]{1,0:T(8,128)(2,1)S(1)}, u32[]{:S(2)}, u32[]{:S(2)}) collective-permute-start(s16[144,512]{1,0:T(8,128)(2,1)S(1)} %get-tuple-element.26), channel_id=1, source_target_pairs={{0,6},{2,4},{4,2},{6,0},{8,14},{10,12},{12,10},{14,8},{1,7},{3,5},... | collective-permute-start | bytes 442376 | tf_op jit(solution)/shard_map/ppermute | solution.py:236
  28.9 9.4 %collective-permute-start.2 = (s16[144,512]{1,0:T(8,128)(2,1)S(1)}, s16[144,512]{1,0:T(8,128)(2,1)S(1)}, u32[]{:S(2)}, u32[]{:S(2)}) collective-permute-start(s16[144,512]{1,0:T(8,128)(2,1)S(1)} %get-tuple-element.24._), channel_id=1, source_target_pairs={{0,4},{2,6},{4,0},{6,2},{8,12},{10,14},{12,8},{14,10},{1,5},{3,7},... | collective-permute-start | bytes 442376 | tf_op jit(solution)/shard_map/ppermute | solution.py:236
  30.8 22.3 %slice-start = ((s8[16777216]{0:T(1024)(128)(4,1)}), s8[4194304]{0:T(1024)(128)(4,1)S(1)}, s32[]{:S(2)}) async-start(s8[16777216]{0:T(1024)(128)(4,1)} %bitcast.5), calls=%async_computation.2 | async-start | bytes 8388608
  30.8 22.3 %slice-start.1 = ((s8[16777216]{0:T(1024)(128)(4,1)}), s8[4194304]{0:T(1024)(128)(4,1)S(1)}, s32[]{:S(2)}) async-start(s8[16777216]{0:T(1024)(128)(4,1)} %bitcast.5), calls=%async_computation.3 | async-start | bytes 8388608
  30.8 22.3 %slice-start.2 = ((s8[16777216]{0:T(1024)(128)(4,1)}), s8[4194304]{0:T(1024)(128)(4,1)S(1)}, s32[]{:S(2)}) async-start(s8[16777216]{0:T(1024)(128)(4,1)} %bitcast.5), calls=%async_computation.4 | async-start | bytes 8388608
  32.4 5.9 %collective-permute-start.4 = (s16[144,512]{1,0:T(8,128)(2,1)S(1)}, s16[144,512]{1,0:T(8,128)(2,1)S(1)}, u32[]{:S(2)}, u32[]{:S(2)}) collective-permute-start(s16[144,512]{1,0:T(8,128)(2,1)S(1)} %get-tuple-element.27), channel_id=1, source_target_pairs={{0,2},{2,0},{4,6},{6,4},{8,10},{10,8},{12,14},{14,12},{1,3},{3,1},... | collective-permute-start | bytes 442376 | tf_op jit(solution)/shard_map/ppermute | solution.py:236
  33.6 12.1 %collective-permute-start.12 = (s16[144,512]{1,0:T(8,128)(2,1)S(1)}, s16[144,512]{1,0:T(8,128)(2,1)S(1)}, u32[]{:S(2)}, u32[]{:S(2)}) collective-permute-start(s16[144,512]{1,0:T(8,128)(2,1)S(1)} %get-tuple-element.33), channel_id=1, source_target_pairs={{0,8},{2,10},{4,12},{6,14},{8,0},{10,2},{12,4},{14,6},{1,9},{3,11}... | collective-permute-start | bytes 442376 | tf_op jit(solution)/shard_map/ppermute | solution.py:236
  38.5 10.8 %collective-permute-start.5 = (s16[144,512]{1,0:T(8,128)(2,1)S(1)}, s16[144,512]{1,0:T(8,128)(2,1)S(1)}, u32[]{:S(2)}, u32[]{:S(2)}) collective-permute-start(s16[144,512]{1,0:T(8,128)(2,1)S(1)} %get-tuple-element.29), channel_id=1, source_target_pairs={{0,8},{2,10},{4,12},{6,14},{8,0},{10,2},{12,4},{14,6},{1,9},{3,11}... | collective-permute-start | bytes 442376 | tf_op jit(solution)/shard_map/ppermute | solution.py:236
  45.7 5.3 %collective-permute-start.15 = (bf16[2,64,256]{2,1,0:T(8,128)(2,1)S(1)}, bf16[2,64,256]{2,1,0:T(8,128)(2,1)S(1)}, u32[]{:S(2)}, u32[]{:S(2)}) collective-permute-start(bf16[2,64,256]{2,1,0:T(8,128)(2,1)S(1)} %hidden_0.1.refs_0_), channel_id=1, source_target_pairs={{0,4},{2,6},{4,0},{6,2},{8,12},{10,14},{12,8},{14,10},{1,5},{3,7},... | collective-permute-start | bytes 196616 | tf_op jit(solution)/shard_map/ppermute | solution.py:236
  45.8 7.1 %collective-permute-start.14 = (bf16[2,64,256]{2,1,0:T(8,128)(2,1)S(1)}, bf16[2,64,256]{2,1,0:T(8,128)(2,1)S(1)}, u32[]{:S(2)}, u32[]{:S(2)}) collective-permute-start(bf16[2,64,256]{2,1,0:T(8,128)(2,1)S(1)} %hidden_0.1.refs_0_), channel_id=1, source_target_pairs={{0,6},{2,4},{4,2},{6,0},{8,14},{10,12},{12,10},{14,8},{1,7},{3,5},... | collective-permute-start | bytes 196616 | tf_op jit(solution)/shard_map/ppermute | solution.py:236
  48.7 4.3 %collective-permute-start.13 = (bf16[2,64,256]{2,1,0:T(8,128)(2,1)S(1)}, bf16[2,64,256]{2,1,0:T(8,128)(2,1)S(1)}, u32[]{:S(2)}, u32[]{:S(2)}) collective-permute-start(bf16[2,64,256]{2,1,0:T(8,128)(2,1)S(1)} %hidden_0.1.refs_0_), channel_id=1, source_target_pairs={{0,2},{2,0},{4,6},{6,4},{8,10},{10,8},{12,14},{14,12},{1,3},{3,1},... | collective-permute-start | bytes 196616 | tf_op jit(solution)/shard_map/ppermute | solution.py:236
  49.4 6.8 %collective-permute-start.8 = (bf16[2,64,256]{2,1,0:T(8,128)(2,1)S(1)}, bf16[2,64,256]{2,1,0:T(8,128)(2,1)S(1)}, u32[]{:S(2)}, u32[]{:S(2)}) collective-permute-start(bf16[2,64,256]{2,1,0:T(8,128)(2,1)S(1)} %hidden_1.1.refs_0_), channel_id=1, source_target_pairs={{0,2},{2,0},{4,6},{6,4},{8,10},{10,8},{12,14},{14,12},{1,3},{3,1},... | collective-permute-start | bytes 196616 | tf_op jit(solution)/shard_map/ppermute | solution.py:236
  50.9 5.3 %collective-permute-start.7 = (bf16[2,64,256]{2,1,0:T(8,128)(2,1)S(1)}, bf16[2,64,256]{2,1,0:T(8,128)(2,1)S(1)}, u32[]{:S(2)}, u32[]{:S(2)}) collective-permute-start(bf16[2,64,256]{2,1,0:T(8,128)(2,1)S(1)} %hidden_1.1.refs_0_), channel_id=1, source_target_pairs={{0,6},{2,4},{4,2},{6,0},{8,14},{10,12},{12,10},{14,8},{1,7},{3,5},... | collective-permute-start | bytes 196616 | tf_op jit(solution)/shard_map/ppermute | solution.py:236
  51.0 5.2 %collective-permute-start.6 = (bf16[2,64,256]{2,1,0:T(8,128)(2,1)S(1)}, bf16[2,64,256]{2,1,0:T(8,128)(2,1)S(1)}, u32[]{:S(2)}, u32[]{:S(2)}) collective-permute-start(bf16[2,64,256]{2,1,0:T(8,128)(2,1)S(1)} %hidden_1.1.refs_0_), channel_id=1, source_target_pairs={{0,4},{2,6},{4,0},{6,2},{8,12},{10,14},{12,8},{14,10},{1,5},{3,7},... | collective-permute-start | bytes 196616 | tf_op jit(solution)/shard_map/ppermute | solution.py:236
  55.1 15.5 %copy-start.2 = (bf16[4,4096]{1,0:T(4,128)(2,1)S(1)}, bf16[4,4096]{1,0:T(4,128)(2,1)}, u32[]{:S(2)}) copy-start(bf16[4,4096]{1,0:T(4,128)(2,1)} %tok_ref.1) | copy-start | bytes 98308
  55.1 15.5 %copy-start.3 = (f32[4096]{0:T(1024)S(1)}, f32[4096]{0:T(1024)}, u32[]{:S(2)}) copy-start(f32[4096]{0:T(1024)} %param.19) | copy-start | bytes 49156
  69.2 1.4 %collective-permute-start.16 = (f32[8,4,1024]{2,1,0:T(4,128)S(1)}, f32[8,4,1024]{2,1,0:T(4,128)S(1)}, u32[]{:S(2)}, u32[]{:S(2)}) collective-permute-start(f32[8,4,1024]{2,1,0:T(4,128)S(1)} %group_sum.1.branch_ref), channel_id=1, source_target_pairs={{0,1},{1,0},{2,3},{3,2},{4,5},{5,4},{6,7},{7,6},{8,9},{9,8},{10,11... | collective-permute-start | bytes 393224 | tf_op jit(solution)/shard_map/ppermute | solution.py:236
  (1 other events, 14.8 us)

commit v4 on v3

--- a/solution.py
+++ b/solution.py
@@ -116,7 +116,7 @@
     return jnp.concatenate([jnp.concatenate(row, axis=1) for row in tiles], axis=0)
 
 
-def gate_up_kernel(blocks, n, place_ref, scl_ref, x_ref, gate_ref, up_ref, _, *refs):
+def gate_up_kernel(blocks, far, n, place_ref, scl_ref, x_ref, gate_ref, up_ref, _, *refs):
     me, group = place_ref[0], place_ref[3]
     x = x_ref[...]
     sums_ref = refs[-1]
@@ -125,7 +125,7 @@
     for (piece, q), out_ref in zip(blocks, refs):
         total_ref = sums_ref if q else out_ref
         for i in range(2):
-            block = (group * 2 + piece) * n + (me ^ (q + i * (n // 2)))
+            block = (group * 2 + piece) * n + (me ^ q ^ (i * far))
             cols = pl.ds(pl.multiple_of(block * wide, TILE), wide)
             for m, ref in enumerate((gate_ref, up_ref)):
                 total = None
@@ -160,23 +160,24 @@
         out_ref[i] = (gate / (1.0 + jnp.exp(-gate)) * up).astype(BF16)
 
 
-def down_kernel(piece, blocks, n, begin, last, place_ref, scl_ref, codes_ref, *refs):
+def down_kernel(piece, blocks, far, n, begin, last, place_ref, scl_ref, codes_ref, *refs):
     me, group = place_ref[0], place_ref[3]
     hidden_refs, out_ref = refs[: len(blocks)], refs[-1]
     wide, depth, step = hidden_refs[0].shape[-1], codes_ref.shape[0], 2 * TILE
     units = wide // TILE
     for r in range(0, depth, step):
-        total = None if begin else refs[len(blocks)][:, r : r + step]
+        total = None if begin else refs[len(blocks)][r : r + step]
         for q, hidden_ref in zip(blocks, hidden_refs):
             for i in range(2):
-                block = (group * 2 + piece) * n + (me ^ (q + i * (n // 2)))
+                block = (group * 2 + piece) * n + (me ^ q ^ (i * far))
                 cols = pl.ds(pl.multiple_of(block * wide, TILE), wide)
                 w = scaled(codes_ref[r : r + step, cols], lambda t, c: scl_ref[r // TILE + t, block * units + c], 2, units)
-                part = lax.dot_general(hidden_ref[i], w, (((1,), (1,)), ((), ())), preferred_element_type=F32)
+                part = lax.dot_general(w, hidden_ref[i], (((1,), (1,)), ((), ())), preferred_element_type=F32)
                 total = part if total is None else total + part
         if not last:
-            out_ref[:, r : r + step] = total
+            out_ref[r : r + step] = total
             continue
+        total = total.T
         count, rows, _ = out_ref.shape
         for j in range(count):
             out_ref[j, :, r : r + step] = total[j * rows : (j + 1) * rows].astype(BF16)
@@ -261,11 +262,11 @@
         [normed] + [unread(hbm(a)) for a in (gate_codes, up_codes, down_codes)],
         shape(normed.shape, BF16),
     )
-    both = ("groups", "fsdp")
+    rows_axes = ("groups", "fsdp")
     x = call(
         rows_kernel,
         "rows",
-        [lax.all_to_all(normed, both, 0, 0, tiled=True)],
+        [lax.all_to_all(normed, rows_axes, 0, 0, tiled=True)],
         shape((all_rows, depth), BF16),
         scratch=[pltpu.VMEM((all_rows, depth), F32)],
     )
@@ -278,12 +279,12 @@
 
     coded = lambda count: shape((count * all_rows + CODE_ROWS, 2 * wide), jnp.int16)
 
-    far = n // 2
+    fars = (n // 2 + 2, n // 2 + 2)
     sums = shape((2, all_rows, 2 * wide), F32)
 
     def gate_up(name, after, *blocks):
         return call(
-            functools.partial(gate_up_kernel, blocks, n),
+            functools.partial(gate_up_kernel, blocks, fars[blocks[0][0]], n),
             f"gate_up_{name}",
             [spot, (gu_scales, SMEM_SPEC), x, *codes, unread(after)],
             [coded(2) if q else sums for _, q in blocks],
@@ -292,31 +293,36 @@
         )
 
     orders = ((1, 3, 2), (2, 3, 1))
-    kept, got, after = [], [], x
+    kept, got, after, branch = [], [], x, None
     for p, (q1, q2, q3) in enumerate(orders):
         send_1, send_2 = gate_up(f"{p}_first", after, (p, q1), (p, q2))
         send_3, keep = gate_up(f"{p}_second", send_1, (p, q3), (p, 0))
         got.append([swap(send, "fsdp", q) for send, q in ((send_1, q1), (send_2, q2), (send_3, q3))])
         kept.append(keep)
         after = send_3
-    branch = None
+    both = [
+        call(
+            both_kernel,
+            f"both_{p}",
+            [kept[p], *got[p]] + [unread(hbm(down_codes))] * p,
+            [sums, coded(2)],
+        )
+        for p in range(2)
+    ]
     for p, order in enumerate(orders):
-        late = [unread(hbm(down_codes))] if p else []
-        keep, send = call(both_kernel, f"both_{p}", [kept[p], *got[p], *late], [sums, coded(2)])
-        hidden = call(hidden_kernel, f"hidden_{p}", [keep, swap(send, "fsdp", far)], shape((2, all_rows, wide), BF16))
-        parts = [hidden] + [swap(hidden, "fsdp", q) for q in order]
-        for at in ((0, 1), (1, 4)) if p else ((0, 4),):
-            last = p == 1 and at[1] == 4
-            branch = call(
-                functools.partial(down_kernel, p, (0, *order)[slice(*at)], n, branch is None, last),
-                f"down_{p}_{at[0]}",
-                [spot, (down_scales, SMEM_SPEC), vmem(down_codes), *parts[slice(*at)]]
-                + ([] if branch is None else [branch]),
-                shape((2 * n, rows, depth), BF16) if last else shape((all_rows, depth), F32),
-                cost=cost(2, wide),
-            )
-
-    got = lax.all_to_all(branch, both, 0, 0, tiled=True)
+        keep, send = both[p]
+        hidden = call(hidden_kernel, f"hidden_{p}", [keep, swap(send, "fsdp", fars[p])], shape((2, all_rows, wide), BF16))
+        branch = call(
+            functools.partial(down_kernel, p, (0, *order), fars[p], n, p == 0, p == 1),
+            f"down_{p}",
+            [spot, (down_scales, SMEM_SPEC), vmem(down_codes), hidden]
+            + [swap(hidden, "fsdp", q) for q in order]
+            + ([branch] if p else []),
+            shape((2 * n, rows, depth), BF16) if p else shape((depth, all_rows), F32),
+            cost=cost(1, wide),
+        )
+
+    got = lax.all_to_all(branch, rows_axes, 0, 0, tiled=True)
     branch = call(group_sum_kernel, "group_sum", [got], shape((n, rows, depth), F32))
     layer_out, values = call(
         final_kernel,

time: 72.1 us -> 70.8 us (0.982)
  waiting for transfers between devices: 11.7 us -> 7.92 us
  starting transfers between devices: 17.2 us -> 20.5 us
  Pallas kernels: 14 us -> 12.9 us
    ppermute x17, waiting for transfers between devices: 11.7 us -> 7.92 us  [swap(): lax.ppermute(x, axis, [(i, i ^ bit) for i in range(n if axis == 'fsdp' el...]
    ppermute x17, starting transfers between devices: 17.2 us -> 20.5 us  [swap(): lax.ppermute(x, axis, [(i, i ^ bit) for i in range(n if axis == 'fsdp' el...]
    pallas_call x16 -> x15, Pallas kernels: 14 us -> 12.9 us  [call(): pl.pallas_call(kernel, in_specs=specs, out_specs=jax.tree.map(lambda _: V...]
  transfers between devices with their start and end apart: 17 -> 17, of which waited for: 7 -> 9; matrix products, arithmetic and copies ran while one was open for 0% -> 0% of each run, Pallas kernels for 12% -> 10%
where the time goes in v4:
time: 70.8 us; the launch traced here: 70.5 us
  blocking collectives  27.6 us (39%)
  starting transfers between devices  20.5 us (29%)
  Pallas kernels  12.9 us (18%)
  waiting for transfers between devices  7.92 us (11%)
  between operations  1.48 us (2%)
    ppermute x17, starting transfers between devices, swap(): lax.ppermute(x, axis, [(i, i ^ bit) for i in range(n if axis == 'fsdp' el...  20.5 us
    all_to_all x1, blocking collectives, body_split(): lax.all_to_all(normed, rows_axes, 0, 0, tiled=True)  16 us
    pallas_call x15, Pallas kernels, call(): pl.pallas_call(kernel, in_specs=specs, out_specs=jax.tree.map(lambda _: V...  12.9 us
    all_to_all x1, blocking collectives, body_split(): got = lax.all_to_all(branch, rows_axes, 0, 0, tiled=True)  11.6 us
    ppermute x17, waiting for transfers between devices, swap(): lax.ppermute(x, axis, [(i, i ^ bit) for i in range(n if axis == 'fsdp' el...  7.92 us
  transfers between devices with their start and end apart: 17, of which 9 were waited for; matrix products, arithmetic and copies ran while one was open for 0% of the time, Pallas kernels for 10%

profile of v4, /device:TPU:0, one launch (start us, length us, event | category | flops | bytes accessed | tf_op | source)
XLA Modules:
  0.0 70.5 jit_solution(10834097131782253715)
XLA Ops:
  2.6 1.0 %norm.1 = (bf16[16,4,1024]{2,1,0:T(4,128)(2,1)S(1)}, f32[2,8,64]{2,1,0:T(8,128)S(1)}, f32[8,64]{1,0:T(8,128)S(1)}) custom-call(s32[4]{0:T(128)S(1)} %pad_add_fusion.place_ref, bf16[4,4096]{1,0:T(4,128)(2,1)} %tok_ref.1, bf16[4,4096]{1,0:T(4,128)(2,1)S(1)} %collective-permute-done.core_mate_ref.tok_mate_ref, bf16[8192]{0:T(1024)(128)(2,1)} %gain_ref.1, ...), custom_call_target="tpu_custom_call" | custom-call | tf_op jit(solution)/shard_map/norm/pallas_call | solution.py:213
  3.6 16.0 %all_to_all.10.got_ref = bf16[16,4,1024]{2,1,0:T(4,128)(2,1)S(1)} all-to-all(bf16[16,4,1024]{2,1,0:T(4,128)(2,1)S(1)} %hold.1), channel_id=1, replica_groups=mesh['groups'=2,'fsdp'=8,'tp'=2] {'groups','fsdp'}, dimensions={0} | all-to-all | bytes 262144 | tf_op jit(solution)/shard_map/all_to_all | solution.py:269
  19.7 1.6 %gate_up_0_first.1 = (s16[144,512]{1,0:T(8,128)(2,1)S(1)}, s16[144,512]{1,0:T(8,128)(2,1)S(1)}) custom-call(s32[4]{0:T(128)S(1)} %pad_add_fusion.place_ref, f32[2,8,64]{2,1,0:T(8,128)S(1)} %get-tuple-element.20.scl_ref, bf16[64,1024]{1,0:T(8,128)(2,1)S(1)} %rows.1.x_ref._, bf16[1024,8192]{1,0:T(8,128)(2,1)S(1)} %copy-done, bf16[1024,8192]{1,0:T(8,128)(2,1)S(1)} %copy-done.1, ...), custom_call_target="tpu_custom_call" | custom-call | flops 268435456 | bytes 4194304 | tf_op jit(solution)/shard_map/gate_up_0_first/pallas_call | solution.py:213
  22.0 1.5 %collective-permute-start.9 = (s16[144,512]{1,0:T(8,128)(2,1)S(1)}, s16[144,512]{1,0:T(8,128)(2,1)S(1)}, u32[]{:S(2)}, u32[]{:S(2)}) collective-permute-start(s16[144,512]{1,0:T(8,128)(2,1)S(1)} %get-tuple-element.22._), channel_id=1, source_target_pairs={{0,2},{2,0},{4,6},{6,4},{8,10},{10,8},{12,14},{14,12},{1,3},{3,1},... | collective-permute-start | bytes 442376 | tf_op jit(solution)/shard_map/ppermute | solution.py:237
  23.5 1.6 %gate_up_0_second.1 = (s16[144,512]{1,0:T(8,128)(2,1)S(1)}, f32[2,64,512]{2,1,0:T(8,128)S(1)}) custom-call(s32[4]{0:T(128)S(1)} %pad_add_fusion.place_ref, f32[2,8,64]{2,1,0:T(8,128)S(1)} %get-tuple-element.20.scl_ref, bf16[64,1024]{1,0:T(8,128)(2,1)S(1)} %rows.1.x_ref._, bf16[1024,8192]{1,0:T(8,128)(2,1)S(1)} %copy-done, bf16[1024,8192]{1,0:T(8,128)(2,1)S(1)} %copy-done.1, ...), custom_call_target="tpu_custom_call" | custom-call | flops 268435456 | bytes 4194304 | tf_op jit(solution)/shard_map/gate_up_0_second/pallas_call | solution.py:213
  25.1 1.4 %collective-permute-start.11 = (s16[144,512]{1,0:T(8,128)(2,1)S(1)}, s16[144,512]{1,0:T(8,128)(2,1)S(1)}, u32[]{:S(2)}, u32[]{:S(2)}) collective-permute-start(s16[144,512]{1,0:T(8,128)(2,1)S(1)} %get-tuple-element.23._), channel_id=1, source_target_pairs={{0,4},{2,6},{4,0},{6,2},{8,12},{10,14},{12,8},{14,10},{1,5},{3,7},... | collective-permute-start | bytes 442376 | tf_op jit(solution)/shard_map/ppermute | solution.py:237
  26.5 1.6 %gate_up_1_first.1 = (s16[144,512]{1,0:T(8,128)(2,1)S(1)}, s16[144,512]{1,0:T(8,128)(2,1)S(1)}) custom-call(s32[4]{0:T(128)S(1)} %pad_add_fusion.place_ref, f32[2,8,64]{2,1,0:T(8,128)S(1)} %get-tuple-element.20.scl_ref, bf16[64,1024]{1,0:T(8,128)(2,1)S(1)} %rows.1.x_ref._, bf16[1024,8192]{1,0:T(8,128)(2,1)S(1)} %copy-done, bf16[1024,8192]{1,0:T(8,128)(2,1)S(1)} %copy-done.1, ...), custom_call_target="tpu_custom_call" | custom-call | flops 268435456 | bytes 4194304 | tf_op jit(solution)/shard_map/gate_up_1_first/pallas_call | solution.py:213
  28.9 1.9 %collective-permute-start.2 = (s16[144,512]{1,0:T(8,128)(2,1)S(1)}, s16[144,512]{1,0:T(8,128)(2,1)S(1)}, u32[]{:S(2)}, u32[]{:S(2)}) collective-permute-start(s16[144,512]{1,0:T(8,128)(2,1)S(1)} %get-tuple-element.24._), channel_id=1, source_target_pairs={{0,4},{2,6},{4,0},{6,2},{8,12},{10,14},{12,8},{14,10},{1,5},{3,7},... | collective-permute-start | bytes 442376 | tf_op jit(solution)/shard_map/ppermute | solution.py:237
  30.8 1.6 %gate_up_1_second.1 = (s16[144,512]{1,0:T(8,128)(2,1)S(1)}, f32[2,64,512]{2,1,0:T(8,128)S(1)}) custom-call(s32[4]{0:T(128)S(1)} %pad_add_fusion.place_ref, f32[2,8,64]{2,1,0:T(8,128)S(1)} %get-tuple-element.20.scl_ref, bf16[64,1024]{1,0:T(8,128)(2,1)S(1)} %rows.1.x_ref._, bf16[1024,8192]{1,0:T(8,128)(2,1)S(1)} %copy-done, bf16[1024,8192]{1,0:T(8,128)(2,1)S(1)} %copy-done.1, ...), custom_call_target="tpu_custom_call" | custom-call | flops 268435456 | bytes 4194304 | tf_op jit(solution)/shard_map/gate_up_1_second/pallas_call | solution.py:213
  32.4 1.0 %collective-permute-start.4 = (s16[144,512]{1,0:T(8,128)(2,1)S(1)}, s16[144,512]{1,0:T(8,128)(2,1)S(1)}, u32[]{:S(2)}, u32[]{:S(2)}) collective-permute-start(s16[144,512]{1,0:T(8,128)(2,1)S(1)} %get-tuple-element.27), channel_id=1, source_target_pairs={{0,2},{2,0},{4,6},{6,4},{8,10},{10,8},{12,14},{14,12},{1,3},{3,1},... | collective-permute-start | bytes 442376 | tf_op jit(solution)/shard_map/ppermute | solution.py:237
  33.6 1.8 %collective-permute-start.12 = (s16[144,512]{1,0:T(8,128)(2,1)S(1)}, s16[144,512]{1,0:T(8,128)(2,1)S(1)}, u32[]{:S(2)}, u32[]{:S(2)}) collective-permute-start(s16[144,512]{1,0:T(8,128)(2,1)S(1)} %get-tuple-element.33), channel_id=1, source_target_pairs={{0,12},{2,14},{4,8},{6,10},{8,4},{10,6},{12,0},{14,2},{1,13},{3,15... | collective-permute-start | bytes 442376 | tf_op jit(solution)/shard_map/ppermute | solution.py:237
  35.4 2.1 %collective-permute-done.2.refs_0_ = s16[144,512]{1,0:T(8,128)(2,1)S(1)} collective-permute-done((s16[144,512]{1,0:T(8,128)(2,1)S(1)}, s16[144,512]{1,0:T(8,128)(2,1)S(1)}, u32[]{:S(2)}, u32[]{:S(2)}) %collective-permute-start.2) | collective-permute-done | bytes 147488 | tf_op jit(solution)/shard_map/ppermute | solution.py:237
  37.8 1.5 %collective-permute-start.5 = (s16[144,512]{1,0:T(8,128)(2,1)S(1)}, s16[144,512]{1,0:T(8,128)(2,1)S(1)}, u32[]{:S(2)}, u32[]{:S(2)}) collective-permute-start(s16[144,512]{1,0:T(8,128)(2,1)S(1)} %get-tuple-element.29), channel_id=1, source_target_pairs={{0,12},{2,14},{4,8},{6,10},{8,4},{10,6},{12,0},{14,2},{1,13},{3,15... | collective-permute-start | bytes 442376 | tf_op jit(solution)/shard_map/ppermute | solution.py:237
  39.3 1.4 %collective-permute-done.12.got_ref = s16[144,512]{1,0:T(8,128)(2,1)S(1)} collective-permute-done((s16[144,512]{1,0:T(8,128)(2,1)S(1)}, s16[144,512]{1,0:T(8,128)(2,1)S(1)}, u32[]{:S(2)}, u32[]{:S(2)}) %collective-permute-start.12) | collective-permute-done | bytes 147488 | tf_op jit(solution)/shard_map/ppermute | solution.py:237
  40.8 4.2 %collective-permute-start.15 = (bf16[2,64,256]{2,1,0:T(8,128)(2,1)S(1)}, bf16[2,64,256]{2,1,0:T(8,128)(2,1)S(1)}, u32[]{:S(2)}, u32[]{:S(2)}) collective-permute-start(bf16[2,64,256]{2,1,0:T(8,128)(2,1)S(1)} %hidden_0.1.refs_0_), channel_id=1, source_target_pairs={{0,4},{2,6},{4,0},{6,2},{8,12},{10,14},{12,8},{14,10},{1,5},{3,7},... | collective-permute-start | bytes 196616 | tf_op jit(solution)/shard_map/ppermute | solution.py:237
  45.6 0.9 %collective-permute-start.13 = (bf16[2,64,256]{2,1,0:T(8,128)(2,1)S(1)}, bf16[2,64,256]{2,1,0:T(8,128)(2,1)S(1)}, u32[]{:S(2)}, u32[]{:S(2)}) collective-permute-start(bf16[2,64,256]{2,1,0:T(8,128)(2,1)S(1)} %hidden_0.1.refs_0_), channel_id=1, source_target_pairs={{0,2},{2,0},{4,6},{6,4},{8,10},{10,8},{12,14},{14,12},{1,3},{3,1},... | collective-permute-start | bytes 196616 | tf_op jit(solution)/shard_map/ppermute | solution.py:237
  46.6 1.1 %collective-permute-start.8 = (bf16[2,64,256]{2,1,0:T(8,128)(2,1)S(1)}, bf16[2,64,256]{2,1,0:T(8,128)(2,1)S(1)}, u32[]{:S(2)}, u32[]{:S(2)}) collective-permute-start(bf16[2,64,256]{2,1,0:T(8,128)(2,1)S(1)} %hidden_1.1.refs_0_), channel_id=1, source_target_pairs={{0,2},{2,0},{4,6},{6,4},{8,10},{10,8},{12,14},{14,12},{1,3},{3,1},... | collective-permute-start | bytes 196616 | tf_op jit(solution)/shard_map/ppermute | solution.py:237
  47.8 2.3 %collective-permute-start.7 = (bf16[2,64,256]{2,1,0:T(8,128)(2,1)S(1)}, bf16[2,64,256]{2,1,0:T(8,128)(2,1)S(1)}, u32[]{:S(2)}, u32[]{:S(2)}) collective-permute-start(bf16[2,64,256]{2,1,0:T(8,128)(2,1)S(1)} %hidden_1.1.refs_0_), channel_id=1, source_target_pairs={{0,6},{2,4},{4,2},{6,0},{8,14},{10,12},{12,10},{14,8},{1,7},{3,5},... | collective-permute-start | bytes 196616 | tf_op jit(solution)/shard_map/ppermute | solution.py:237
  51.3 1.8 %down_0.1.refs_4_ = f32[1024,64]{1,0:T(8,128)S(1)} custom-call(s32[4]{0:T(128)S(1)} %pad_add_fusion.place_ref, f32[8,64]{1,0:T(8,128)S(1)} %get-tuple-element.19.scl_ref, bf16[1024,8192]{1,0:T(8,128)(2,1)S(1)} %bitcast.6, bf16[2,64,256]{2,1,0:T(8,128)(2,1)S(1)} %hidden_0.1.refs_0_, bf16[2,64,256]{2,1,0:T(8,128)(2,1)S(1)} %collective-permute-done.13.refs_1_, ...), custom_call_target="tpu_custom_call" | custom-call | flops 268435456 | bytes 4194304 | tf_op jit(solution)/shard_map/down_0/pallas_call | solution.py:213
  53.2 1.2 %collective-permute-done.6.refs_1_ = bf16[2,64,256]{2,1,0:T(8,128)(2,1)S(1)} collective-permute-done((bf16[2,64,256]{2,1,0:T(8,128)(2,1)S(1)}, bf16[2,64,256]{2,1,0:T(8,128)(2,1)S(1)}, u32[]{:S(2)}, u32[]{:S(2)}) %collective-permute-start.6) | collective-permute-done | bytes 65568 | tf_op jit(solution)/shard_map/ppermute | solution.py:237
  54.4 1.9 %down_1.1 = bf16[16,4,1024]{2,1,0:T(4,128)(2,1)S(1)} custom-call(s32[4]{0:T(128)S(1)} %pad_add_fusion.place_ref, f32[8,64]{1,0:T(8,128)S(1)} %get-tuple-element.19.scl_ref, bf16[1024,8192]{1,0:T(8,128)(2,1)S(1)} %bitcast.6, bf16[2,64,256]{2,1,0:T(8,128)(2,1)S(1)} %hidden_1.1.refs_0_, bf16[2,64,256]{2,1,0:T(8,128)(2,1)S(1)} %collective-permute-done.6.refs_1_, ...), custom_call_target="tpu_custom_call" | custom-call | flops 268435456 | bytes 4194304 | tf_op jit(solution)/shard_map/down_1/pallas_call | solution.py:213
  56.3 11.6 %all_to_all.11.got_ref = bf16[16,4,1024]{2,1,0:T(4,128)(2,1)S(1)} all-to-all(bf16[16,4,1024]{2,1,0:T(4,128)(2,1)S(1)} %down_1.1), channel_id=1, replica_groups=mesh['groups'=2,'fsdp'=8,'tp'=2] {'groups','fsdp'}, dimensions={0} | all-to-all | bytes 262144 | tf_op jit(solution)/shard_map/all_to_all | solution.py:325
  68.0 1.3 %collective-permute-done.16.branch_mate_ref = f32[8,4,1024]{2,1,0:T(4,128)S(1)} collective-permute-done((f32[8,4,1024]{2,1,0:T(4,128)S(1)}, f32[8,4,1024]{2,1,0:T(4,128)S(1)}, u32[]{:S(2)}, u32[]{:S(2)}) %collective-permute-start.16) | collective-permute-done | bytes 131104 | tf_op jit(solution)/shard_map/ppermute | solution.py:237
  69.3 1.2 %final.1 = (bf16[4,4096]{1,0:T(4,128)(2,1)}, f32[1,4]{1,0:T(1,128)}) custom-call(s32[4]{0:T(128)S(1)} %pad_add_fusion.place_ref, bf16[4,4096]{1,0:T(4,128)(2,1)S(1)} %copy-done.2, bf16[4,4096]{1,0:T(4,128)(2,1)S(1)} %collective-permute-done.core_mate_ref.tok_mate_ref, f32[8,4,1024]{2,1,0:T(4,128)S(1)} %group_sum.1.branch_ref, ...), custom_call_target="tpu_custom_call" | custom-call | tf_op jit(solution)/shard_map/final/pallas_call | solution.py:213
  (45 shorter events, 5.3 us)
Async XLA Ops:
  0.6 1.6 %collective-permute-start.1 = (f32[1,4096]{1,0:T(1,128)}, f32[1,4096]{1,0:T(1,128)S(1)}, u32[]{:S(2)}, u32[]{:S(2)}) collective-permute-start(f32[1,4096]{1,0:T(1,128)} %bitcast.7), channel_id=1, source_target_pairs={{0,1},{1,0},{2,3},{3,2},{4,5},{5,4},{6,7},{7,6},{8,9},{9,8},{10,11... | collective-permute-start | bytes 49160 | tf_op jit(solution)/shard_map/ppermute | solution.py:237
  1.1 1.4 %collective-permute-start = (bf16[4,4096]{1,0:T(4,128)(2,1)}, bf16[4,4096]{1,0:T(4,128)(2,1)S(1)}, u32[]{:S(2)}, u32[]{:S(2)}) collective-permute-start(bf16[4,4096]{1,0:T(4,128)(2,1)} %tok_ref.1), channel_id=1, source_target_pairs={{0,1},{1,0},{2,3},{3,2},{4,5},{5,4},{6,7},{7,6},{8,9},{9,8},{10,11... | collective-permute-start | bytes 98312 | tf_op jit(solution)/shard_map/ppermute | solution.py:237
  3.5 16.1 %copy-start = (bf16[1024,8192]{1,0:T(8,128)(2,1)S(1)}, bf16[1024,8192]{1,0:T(8,128)(2,1)}, u32[]{:S(2)}) copy-start(bf16[1024,8192]{1,0:T(8,128)(2,1)} %gate_ref.7) | copy-start | bytes 50331652
  3.5 16.1 %copy-start.1 = (bf16[1024,8192]{1,0:T(8,128)(2,1)S(1)}, bf16[1024,8192]{1,0:T(8,128)(2,1)}, u32[]{:S(2)}) copy-start(bf16[1024,8192]{1,0:T(8,128)(2,1)} %up_ref.7) | copy-start | bytes 50331652
  21.3 11.0 %collective-permute-start.10 = (s16[144,512]{1,0:T(8,128)(2,1)S(1)}, s16[144,512]{1,0:T(8,128)(2,1)S(1)}, u32[]{:S(2)}, u32[]{:S(2)}) collective-permute-start(s16[144,512]{1,0:T(8,128)(2,1)S(1)} %get-tuple-element.31), channel_id=1, source_target_pairs={{0,6},{2,4},{4,2},{6,0},{8,14},{10,12},{12,10},{14,8},{1,7},{3,5},... | collective-permute-start | bytes 442376 | tf_op jit(solution)/shard_map/ppermute | solution.py:237
  22.0 11.3 %collective-permute-start.9 = (s16[144,512]{1,0:T(8,128)(2,1)S(1)}, s16[144,512]{1,0:T(8,128)(2,1)S(1)}, u32[]{:S(2)}, u32[]{:S(2)}) collective-permute-start(s16[144,512]{1,0:T(8,128)(2,1)S(1)} %get-tuple-element.22._), channel_id=1, source_target_pairs={{0,2},{2,0},{4,6},{6,4},{8,10},{10,8},{12,14},{14,12},{1,3},{3,1},... | collective-permute-start | bytes 442376 | tf_op jit(solution)/shard_map/ppermute | solution.py:237
  25.1 8.3 %collective-permute-start.11 = (s16[144,512]{1,0:T(8,128)(2,1)S(1)}, s16[144,512]{1,0:T(8,128)(2,1)S(1)}, u32[]{:S(2)}, u32[]{:S(2)}) collective-permute-start(s16[144,512]{1,0:T(8,128)(2,1)S(1)} %get-tuple-element.23._), channel_id=1, source_target_pairs={{0,4},{2,6},{4,0},{6,2},{8,12},{10,14},{12,8},{14,10},{1,5},{3,7},... | collective-permute-start | bytes 442376 | tf_op jit(solution)/shard_map/ppermute | solution.py:237
  28.2 7.3 %collective-permute-start.3 = (s16[144,512]{1,0:T(8,128)(2,1)S(1)}, s16[144,512]{1,0:T(8,128)(2,1)S(1)}, u32[]{:S(2)}, u32[]{:S(2)}) collective-permute-start(s16[144,512]{1,0:T(8,128)(2,1)S(1)} %get-tuple-element.26), channel_id=1, source_target_pairs={{0,6},{2,4},{4,2},{6,0},{8,14},{10,12},{12,10},{14,8},{1,7},{3,5},... | collective-permute-start | bytes 442376 | tf_op jit(solution)/shard_map/ppermute | solution.py:237
  28.9 8.7 %collective-permute-start.2 = (s16[144,512]{1,0:T(8,128)(2,1)S(1)}, s16[144,512]{1,0:T(8,128)(2,1)S(1)}, u32[]{:S(2)}, u32[]{:S(2)}) collective-permute-start(s16[144,512]{1,0:T(8,128)(2,1)S(1)} %get-tuple-element.24._), channel_id=1, source_target_pairs={{0,4},{2,6},{4,0},{6,2},{8,12},{10,14},{12,8},{14,10},{1,5},{3,7},... | collective-permute-start | bytes 442376 | tf_op jit(solution)/shard_map/ppermute | solution.py:237
  30.8 20.5 %slice-start = ((s8[16777216]{0:T(1024)(128)(4,1)}), s8[4194304]{0:T(1024)(128)(4,1)S(1)}, s32[]{:S(2)}) async-start(s8[16777216]{0:T(1024)(128)(4,1)} %bitcast.5), calls=%async_computation.2 | async-start | bytes 8388608
  30.8 20.5 %slice-start.1 = ((s8[16777216]{0:T(1024)(128)(4,1)}), s8[4194304]{0:T(1024)(128)(4,1)S(1)}, s32[]{:S(2)}) async-start(s8[16777216]{0:T(1024)(128)(4,1)} %bitcast.5), calls=%async_computation.3 | async-start | bytes 8388608
  30.8 20.5 %slice-start.2 = ((s8[16777216]{0:T(1024)(128)(4,1)}), s8[4194304]{0:T(1024)(128)(4,1)S(1)}, s32[]{:S(2)}) async-start(s8[16777216]{0:T(1024)(128)(4,1)} %bitcast.5), calls=%async_computation.4 | async-start | bytes 8388608
  32.4 5.2 %collective-permute-start.4 = (s16[144,512]{1,0:T(8,128)(2,1)S(1)}, s16[144,512]{1,0:T(8,128)(2,1)S(1)}, u32[]{:S(2)}, u32[]{:S(2)}) collective-permute-start(s16[144,512]{1,0:T(8,128)(2,1)S(1)} %get-tuple-element.27), channel_id=1, source_target_pairs={{0,2},{2,0},{4,6},{6,4},{8,10},{10,8},{12,14},{14,12},{1,3},{3,1},... | collective-permute-start | bytes 442376 | tf_op jit(solution)/shard_map/ppermute | solution.py:237
  33.6 7.1 %collective-permute-start.12 = (s16[144,512]{1,0:T(8,128)(2,1)S(1)}, s16[144,512]{1,0:T(8,128)(2,1)S(1)}, u32[]{:S(2)}, u32[]{:S(2)}) collective-permute-start(s16[144,512]{1,0:T(8,128)(2,1)S(1)} %get-tuple-element.33), channel_id=1, source_target_pairs={{0,12},{2,14},{4,8},{6,10},{8,4},{10,6},{12,0},{14,2},{1,13},{3,15... | collective-permute-start | bytes 442376 | tf_op jit(solution)/shard_map/ppermute | solution.py:237
  37.8 8.8 %collective-permute-start.5 = (s16[144,512]{1,0:T(8,128)(2,1)S(1)}, s16[144,512]{1,0:T(8,128)(2,1)S(1)}, u32[]{:S(2)}, u32[]{:S(2)}) collective-permute-start(s16[144,512]{1,0:T(8,128)(2,1)S(1)} %get-tuple-element.29), channel_id=1, source_target_pairs={{0,12},{2,14},{4,8},{6,10},{8,4},{10,6},{12,0},{14,2},{1,13},{3,15... | collective-permute-start | bytes 442376 | tf_op jit(solution)/shard_map/ppermute | solution.py:237
  40.8 9.3 %collective-permute-start.15 = (bf16[2,64,256]{2,1,0:T(8,128)(2,1)S(1)}, bf16[2,64,256]{2,1,0:T(8,128)(2,1)S(1)}, u32[]{:S(2)}, u32[]{:S(2)}) collective-permute-start(bf16[2,64,256]{2,1,0:T(8,128)(2,1)S(1)} %hidden_0.1.refs_0_), channel_id=1, source_target_pairs={{0,4},{2,6},{4,0},{6,2},{8,12},{10,14},{12,8},{14,10},{1,5},{3,7},... | collective-permute-start | bytes 196616 | tf_op jit(solution)/shard_map/ppermute | solution.py:237
  45.0 5.8 %collective-permute-start.14 = (bf16[2,64,256]{2,1,0:T(8,128)(2,1)S(1)}, bf16[2,64,256]{2,1,0:T(8,128)(2,1)S(1)}, u32[]{:S(2)}, u32[]{:S(2)}) collective-permute-start(bf16[2,64,256]{2,1,0:T(8,128)(2,1)S(1)} %hidden_0.1.refs_0_), channel_id=1, source_target_pairs={{0,6},{2,4},{4,2},{6,0},{8,14},{10,12},{12,10},{14,8},{1,7},{3,5},... | collective-permute-start | bytes 196616 | tf_op jit(solution)/shard_map/ppermute | solution.py:237
  45.6 5.7 %collective-permute-start.13 = (bf16[2,64,256]{2,1,0:T(8,128)(2,1)S(1)}, bf16[2,64,256]{2,1,0:T(8,128)(2,1)S(1)}, u32[]{:S(2)}, u32[]{:S(2)}) collective-permute-start(bf16[2,64,256]{2,1,0:T(8,128)(2,1)S(1)} %hidden_0.1.refs_0_), channel_id=1, source_target_pairs={{0,2},{2,0},{4,6},{6,4},{8,10},{10,8},{12,14},{14,12},{1,3},{3,1},... | collective-permute-start | bytes 196616 | tf_op jit(solution)/shard_map/ppermute | solution.py:237
  46.6 6.5 %collective-permute-start.8 = (bf16[2,64,256]{2,1,0:T(8,128)(2,1)S(1)}, bf16[2,64,256]{2,1,0:T(8,128)(2,1)S(1)}, u32[]{:S(2)}, u32[]{:S(2)}) collective-permute-start(bf16[2,64,256]{2,1,0:T(8,128)(2,1)S(1)} %hidden_1.1.refs_0_), channel_id=1, source_target_pairs={{0,2},{2,0},{4,6},{6,4},{8,10},{10,8},{12,14},{14,12},{1,3},{3,1},... | collective-permute-start | bytes 196616 | tf_op jit(solution)/shard_map/ppermute | solution.py:237
  47.8 5.4 %collective-permute-start.7 = (bf16[2,64,256]{2,1,0:T(8,128)(2,1)S(1)}, bf16[2,64,256]{2,1,0:T(8,128)(2,1)S(1)}, u32[]{:S(2)}, u32[]{:S(2)}) collective-permute-start(bf16[2,64,256]{2,1,0:T(8,128)(2,1)S(1)} %hidden_1.1.refs_0_), channel_id=1, source_target_pairs={{0,6},{2,4},{4,2},{6,0},{8,14},{10,12},{12,10},{14,8},{1,7},{3,5},... | collective-permute-start | bytes 196616 | tf_op jit(solution)/shard_map/ppermute | solution.py:237
  50.1 4.3 %collective-permute-start.6 = (bf16[2,64,256]{2,1,0:T(8,128)(2,1)S(1)}, bf16[2,64,256]{2,1,0:T(8,128)(2,1)S(1)}, u32[]{:S(2)}, u32[]{:S(2)}) collective-permute-start(bf16[2,64,256]{2,1,0:T(8,128)(2,1)S(1)} %hidden_1.1.refs_0_), channel_id=1, source_target_pairs={{0,4},{2,6},{4,0},{6,2},{8,12},{10,14},{12,8},{14,10},{1,5},{3,7},... | collective-permute-start | bytes 196616 | tf_op jit(solution)/shard_map/ppermute | solution.py:237
  51.3 18.0 %copy-start.2 = (bf16[4,4096]{1,0:T(4,128)(2,1)S(1)}, bf16[4,4096]{1,0:T(4,128)(2,1)}, u32[]{:S(2)}) copy-start(bf16[4,4096]{1,0:T(4,128)(2,1)} %tok_ref.1) | copy-start | bytes 98308
  51.3 18.0 %copy-start.3 = (f32[4096]{0:T(1024)S(1)}, f32[4096]{0:T(1024)}, u32[]{:S(2)}) copy-start(f32[4096]{0:T(1024)} %param.19) | copy-start | bytes 49156
  67.9 1.4 %collective-permute-start.16 = (f32[8,4,1024]{2,1,0:T(4,128)S(1)}, f32[8,4,1024]{2,1,0:T(4,128)S(1)}, u32[]{:S(2)}, u32[]{:S(2)}) collective-permute-start(f32[8,4,1024]{2,1,0:T(4,128)S(1)} %group_sum.1.branch_ref), channel_id=1, source_target_pairs={{0,1},{1,0},{2,3},{3,2},{4,5},{5,4},{6,7},{7,6},{8,9},{9,8},{10,11... | collective-permute-start | bytes 393224 | tf_op jit(solution)/shard_map/ppermute | solution.py:237
  (1 other events, 13.7 us)

commit v5 on v4

--- a/solution.py
+++ b/solution.py
@@ -292,23 +292,16 @@
             scratch=[pltpu.VMEM(sums.shape, F32)],
         )
 
-    orders = ((1, 3, 2), (2, 3, 1))
-    kept, got, after, branch = [], [], x, None
-    for p, (q1, q2, q3) in enumerate(orders):
-        send_1, send_2 = gate_up(f"{p}_first", after, (p, q1), (p, q2))
-        send_3, keep = gate_up(f"{p}_second", send_1, (p, q3), (p, 0))
-        got.append([swap(send, "fsdp", q) for send, q in ((send_1, q1), (send_2, q2), (send_3, q3))])
-        kept.append(keep)
-        after = send_3
-    both = [
-        call(
-            both_kernel,
-            f"both_{p}",
-            [kept[p], *got[p]] + [unread(hbm(down_codes))] * p,
-            [sums, coded(2)],
-        )
-        for p in range(2)
-    ]
+    orders = ((3, 1, 2), (3, 2, 1))
+    sends_0 = gate_up("send_0", x, *[(0, q) for q in orders[0]])
+    kept = gate_up("keep", sends_0[0], (0, 0), (1, 0))
+    sends_1 = gate_up("send_1", kept[0], *[(1, q) for q in orders[1]])
+    got = [[swap(send, "fsdp", q) for send, q in zip(sends_0, orders[0])]]
+    branch = None
+    both = [call(both_kernel, "both_0", [kept[0], *got[0]], [sums, coded(2)])]
+    held = call(hold_kernel, "hold_send", [sends_1[2], unread(both[0][1])], coded(2))
+    got.append([swap(send, "fsdp", q) for send, q in zip((*sends_1[:2], held), orders[1])])
+    both.append(call(both_kernel, "both_1", [kept[1], *got[1], unread(hbm(down_codes))], [sums, coded(2)]))
     for p, order in enumerate(orders):
         keep, send = both[p]
         hidden = call(hidden_kernel, f"hidden_{p}", [keep, swap(send, "fsdp", fars[p])], shape((2, all_rows, wide), BF16))

time: 70.8 us -> 69.8 us (0.986)
  waiting for transfers between devices: 7.92 us -> 10.5 us
  starting transfers between devices: 20.5 us -> 18.1 us
    ppermute x17, waiting for transfers between devices: 7.92 us -> 10.5 us  [swap(): lax.ppermute(x, axis, [(i, i ^ bit) for i in range(n if axis == 'fsdp' el...]
    ppermute x17, starting transfers between devices: 20.5 us -> 18.1 us  [swap(): lax.ppermute(x, axis, [(i, i ^ bit) for i in range(n if axis == 'fsdp' el...]
    pallas_call x15, Pallas kernels: 12.9 us -> 12.2 us  [call(): pl.pallas_call(kernel, in_specs=specs, out_specs=jax.tree.map(lambda _: V...]
  transfers between devices with their start and end apart: 17 -> 17, of which waited for: 9 -> 9; matrix products, arithmetic and copies ran while one was open for 0% -> 0% of each run, Pallas kernels for 10% -> 9%
where the time goes in v5:
time: 69.8 us; the launch traced here: 69.5 us
  blocking collectives  27.1 us (39%)
  starting transfers between devices  18.1 us (26%)
  Pallas kernels  12.2 us (17%)
  waiting for transfers between devices  10.5 us (15%)
  between operations  1.49 us (2%)
    ppermute x17, starting transfers between devices, swap(): lax.ppermute(x, axis, [(i, i ^ bit) for i in range(n if axis == 'fsdp' el...  18.1 us
    all_to_all x1, blocking collectives, body_split(): lax.all_to_all(normed, rows_axes, 0, 0, tiled=True)  16 us
    pallas_call x15, Pallas kernels, call(): pl.pallas_call(kernel, in_specs=specs, out_specs=jax.tree.map(lambda _: V...  12.2 us
    all_to_all x1, blocking collectives, body_split(): got = lax.all_to_all(branch, rows_axes, 0, 0, tiled=True)  11.1 us
    ppermute x17, waiting for transfers between devices, swap(): lax.ppermute(x, axis, [(i, i ^ bit) for i in range(n if axis == 'fsdp' el...  10.5 us
  transfers between devices with their start and end apart: 17, of which 9 were waited for; matrix products, arithmetic and copies ran while one was open for 0% of the time, Pallas kernels for 9%

profile of v5, /device:TPU:0, one launch (start us, length us, event | category | flops | bytes accessed | tf_op | source)
XLA Modules:
  0.0 69.5 jit_solution(13842257592827669939)
XLA Ops:
  3.6 16.0 %all_to_all.10.got_ref = bf16[16,4,1024]{2,1,0:T(4,128)(2,1)S(1)} all-to-all(bf16[16,4,1024]{2,1,0:T(4,128)(2,1)S(1)} %hold.1), channel_id=1, replica_groups=mesh['groups'=2,'fsdp'=8,'tp'=2] {'groups','fsdp'}, dimensions={0} | all-to-all | bytes 262144 | tf_op jit(solution)/shard_map/all_to_all | solution.py:269
  19.7 2.0 %gate_up_send_0.1 = (s16[144,512]{1,0:T(8,128)(2,1)S(1)}, s16[144,512]{1,0:T(8,128)(2,1)S(1)}, s16[144,512]{1,0:T(8,128)(2,1)S(1)}) custom-call(s32[4]{0:T(128)S(1)} %pad_add_fusion.place_ref, f32[2,8,64]{2,1,0:T(8,128)S(1)} %get-tuple-element.20.scl_ref, bf16[64,1024]{1,0:T(8,128)(2,1)S(1)} %rows.1.x_ref._, bf16[1024,8192]{1,0:T(8,128)(2,1)S(1)} %copy-done, ...), custom_call_target="tpu_custom_call" | custom-call | flops 268435456 | bytes 4194304 | tf_op jit(solution)/shard_map/gate_up_send_0/pallas_call | solution.py:213
  21.7 1.2 %collective-permute-start.5 = (s16[144,512]{1,0:T(8,128)(2,1)S(1)}, s16[144,512]{1,0:T(8,128)(2,1)S(1)}, u32[]{:S(2)}, u32[]{:S(2)}) collective-permute-start(s16[144,512]{1,0:T(8,128)(2,1)S(1)} %get-tuple-element.28), channel_id=1, source_target_pairs={{0,2},{2,0},{4,6},{6,4},{8,10},{10,8},{12,14},{14,12},{1,3},{3,1},... | collective-permute-start | bytes 442376 | tf_op jit(solution)/shard_map/ppermute | solution.py:237
  23.0 2.3 %collective-permute-start.4 = (s16[144,512]{1,0:T(8,128)(2,1)S(1)}, s16[144,512]{1,0:T(8,128)(2,1)S(1)}, u32[]{:S(2)}, u32[]{:S(2)}) collective-permute-start(s16[144,512]{1,0:T(8,128)(2,1)S(1)} %get-tuple-element.22._), channel_id=1, source_target_pairs={{0,6},{2,4},{4,2},{6,0},{8,14},{10,12},{12,10},{14,8},{1,7},{3,5},... | collective-permute-start | bytes 442376 | tf_op jit(solution)/shard_map/ppermute | solution.py:237
  25.3 1.5 %gate_up_keep.1 = (f32[2,64,512]{2,1,0:T(8,128)S(1)}, f32[2,64,512]{2,1,0:T(8,128)S(1)}) custom-call(s32[4]{0:T(128)S(1)} %pad_add_fusion.place_ref, f32[2,8,64]{2,1,0:T(8,128)S(1)} %get-tuple-element.20.scl_ref, bf16[64,1024]{1,0:T(8,128)(2,1)S(1)} %rows.1.x_ref._, bf16[1024,8192]{1,0:T(8,128)(2,1)S(1)} %copy-done, bf16[1024,8192]{1,0:T(8,128)(2,1)S(1)} %copy-done.1, ...), custom_call_target="tpu_custom_call" | custom-call | flops 268435456 | bytes 4194304 | tf_op jit(solution)/shard_map/gate_up_keep/pallas_call | solution.py:213
  26.9 2.0 %gate_up_send_1.1 = (s16[144,512]{1,0:T(8,128)(2,1)S(1)}, s16[144,512]{1,0:T(8,128)(2,1)S(1)}, s16[144,512]{1,0:T(8,128)(2,1)S(1)}) custom-call(s32[4]{0:T(128)S(1)} %pad_add_fusion.place_ref, f32[2,8,64]{2,1,0:T(8,128)S(1)} %get-tuple-element.20.scl_ref, bf16[64,1024]{1,0:T(8,128)(2,1)S(1)} %rows.1.x_ref._, bf16[1024,8192]{1,0:T(8,128)(2,1)S(1)} %copy-done, ...), custom_call_target="tpu_custom_call" | custom-call | flops 268435456 | bytes 4194304 | tf_op jit(solution)/shard_map/gate_up_send_1/pallas_call | solution.py:213
  29.6 1.9 %collective-permute-start.3 = (s16[144,512]{1,0:T(8,128)(2,1)S(1)}, s16[144,512]{1,0:T(8,128)(2,1)S(1)}, u32[]{:S(2)}, u32[]{:S(2)}) collective-permute-start(s16[144,512]{1,0:T(8,128)(2,1)S(1)} %get-tuple-element.26), channel_id=1, source_target_pairs={{0,4},{2,6},{4,0},{6,2},{8,12},{10,14},{12,8},{14,10},{1,5},{3,7},... | collective-permute-start | bytes 442376 | tf_op jit(solution)/shard_map/ppermute | solution.py:237
  31.8 1.0 %collective-permute-start.7 = (s16[144,512]{1,0:T(8,128)(2,1)S(1)}, s16[144,512]{1,0:T(8,128)(2,1)S(1)}, u32[]{:S(2)}, u32[]{:S(2)}) collective-permute-start(s16[144,512]{1,0:T(8,128)(2,1)S(1)} %hold_send.1), channel_id=1, source_target_pairs={{0,2},{2,0},{4,6},{6,4},{8,10},{10,8},{12,14},{14,12},{1,3},{3,1},... | collective-permute-start | bytes 442376 | tf_op jit(solution)/shard_map/ppermute | solution.py:237
  32.8 1.7 %collective-permute-start.12 = (s16[144,512]{1,0:T(8,128)(2,1)S(1)}, s16[144,512]{1,0:T(8,128)(2,1)S(1)}, u32[]{:S(2)}, u32[]{:S(2)}) collective-permute-start(s16[144,512]{1,0:T(8,128)(2,1)S(1)} %get-tuple-element.30.refs_0_), channel_id=1, source_target_pairs={{0,12},{2,14},{4,8},{6,10},{8,4},{10,6},{12,0},{14,2},{1,13},{3,15... | collective-permute-start | bytes 442376 | tf_op jit(solution)/shard_map/ppermute | solution.py:237
  34.5 1.0 %collective-permute-done.2.refs_0_ = s16[144,512]{1,0:T(8,128)(2,1)S(1)} collective-permute-done((s16[144,512]{1,0:T(8,128)(2,1)S(1)}, s16[144,512]{1,0:T(8,128)(2,1)S(1)}, u32[]{:S(2)}, u32[]{:S(2)}) %collective-permute-start.2) | collective-permute-done | bytes 147488 | tf_op jit(solution)/shard_map/ppermute | solution.py:237
  35.5 3.2 %collective-permute-done.3.refs_1_ = s16[144,512]{1,0:T(8,128)(2,1)S(1)} collective-permute-done((s16[144,512]{1,0:T(8,128)(2,1)S(1)}, s16[144,512]{1,0:T(8,128)(2,1)S(1)}, u32[]{:S(2)}, u32[]{:S(2)}) %collective-permute-start.3) | collective-permute-done | bytes 147488 | tf_op jit(solution)/shard_map/ppermute | solution.py:237
  38.8 1.4 %collective-permute-start.8 = (s16[144,512]{1,0:T(8,128)(2,1)S(1)}, s16[144,512]{1,0:T(8,128)(2,1)S(1)}, u32[]{:S(2)}, u32[]{:S(2)}) collective-permute-start(s16[144,512]{1,0:T(8,128)(2,1)S(1)} %get-tuple-element.32), channel_id=1, source_target_pairs={{0,12},{2,14},{4,8},{6,10},{8,4},{10,6},{12,0},{14,2},{1,13},{3,15... | collective-permute-start | bytes 442376 | tf_op jit(solution)/shard_map/ppermute | solution.py:237
  40.3 1.1 %collective-permute-done.12.got_ref = s16[144,512]{1,0:T(8,128)(2,1)S(1)} collective-permute-done((s16[144,512]{1,0:T(8,128)(2,1)S(1)}, s16[144,512]{1,0:T(8,128)(2,1)S(1)}, u32[]{:S(2)}, u32[]{:S(2)}) %collective-permute-start.12) | collective-permute-done | bytes 147488 | tf_op jit(solution)/shard_map/ppermute | solution.py:237
  41.5 2.0 %collective-permute-start.15 = (bf16[2,64,256]{2,1,0:T(8,128)(2,1)S(1)}, bf16[2,64,256]{2,1,0:T(8,128)(2,1)S(1)}, u32[]{:S(2)}, u32[]{:S(2)}) collective-permute-start(bf16[2,64,256]{2,1,0:T(8,128)(2,1)S(1)} %hidden_0.1.refs_0_), channel_id=1, source_target_pairs={{0,4},{2,6},{4,0},{6,2},{8,12},{10,14},{12,8},{14,10},{1,5},{3,7},... | collective-permute-start | bytes 196616 | tf_op jit(solution)/shard_map/ppermute | solution.py:237
  43.5 1.4 %collective-permute-start.14 = (bf16[2,64,256]{2,1,0:T(8,128)(2,1)S(1)}, bf16[2,64,256]{2,1,0:T(8,128)(2,1)S(1)}, u32[]{:S(2)}, u32[]{:S(2)}) collective-permute-start(bf16[2,64,256]{2,1,0:T(8,128)(2,1)S(1)} %hidden_0.1.refs_0_), channel_id=1, source_target_pairs={{0,2},{2,0},{4,6},{6,4},{8,10},{10,8},{12,14},{14,12},{1,3},{3,1},... | collective-permute-start | bytes 196616 | tf_op jit(solution)/shard_map/ppermute | solution.py:237
  46.1 1.1 %collective-permute-start.11 = (bf16[2,64,256]{2,1,0:T(8,128)(2,1)S(1)}, bf16[2,64,256]{2,1,0:T(8,128)(2,1)S(1)}, u32[]{:S(2)}, u32[]{:S(2)}) collective-permute-start(bf16[2,64,256]{2,1,0:T(8,128)(2,1)S(1)} %hidden_1.1.refs_0_), channel_id=1, source_target_pairs={{0,2},{2,0},{4,6},{6,4},{8,10},{10,8},{12,14},{14,12},{1,3},{3,1},... | collective-permute-start | bytes 196616 | tf_op jit(solution)/shard_map/ppermute | solution.py:237
  47.3 1.5 %collective-permute-start.10 = (bf16[2,64,256]{2,1,0:T(8,128)(2,1)S(1)}, bf16[2,64,256]{2,1,0:T(8,128)(2,1)S(1)}, u32[]{:S(2)}, u32[]{:S(2)}) collective-permute-start(bf16[2,64,256]{2,1,0:T(8,128)(2,1)S(1)} %hidden_1.1.refs_0_), channel_id=1, source_target_pairs={{0,4},{2,6},{4,0},{6,2},{8,12},{10,14},{12,8},{14,10},{1,5},{3,7},... | collective-permute-start | bytes 196616 | tf_op jit(solution)/shard_map/ppermute | solution.py:237
  49.7 1.1 %collective-permute-done.13.refs_1_ = bf16[2,64,256]{2,1,0:T(8,128)(2,1)S(1)} collective-permute-done((bf16[2,64,256]{2,1,0:T(8,128)(2,1)S(1)}, bf16[2,64,256]{2,1,0:T(8,128)(2,1)S(1)}, u32[]{:S(2)}, u32[]{:S(2)}) %collective-permute-start.13) | collective-permute-done | bytes 65568 | tf_op jit(solution)/shard_map/ppermute | solution.py:237
  50.8 1.8 %down_0.1.refs_4_ = f32[1024,64]{1,0:T(8,128)S(1)} custom-call(s32[4]{0:T(128)S(1)} %pad_add_fusion.place_ref, f32[8,64]{1,0:T(8,128)S(1)} %get-tuple-element.19.scl_ref, bf16[1024,8192]{1,0:T(8,128)(2,1)S(1)} %bitcast.6, bf16[2,64,256]{2,1,0:T(8,128)(2,1)S(1)} %hidden_0.1.refs_0_, bf16[2,64,256]{2,1,0:T(8,128)(2,1)S(1)} %collective-permute-done.13.refs_1_, ...), custom_call_target="tpu_custom_call" | custom-call | flops 268435456 | bytes 4194304 | tf_op jit(solution)/shard_map/down_0/pallas_call | solution.py:213
  52.7 1.2 %collective-permute-done.9.refs_1_ = bf16[2,64,256]{2,1,0:T(8,128)(2,1)S(1)} collective-permute-done((bf16[2,64,256]{2,1,0:T(8,128)(2,1)S(1)}, bf16[2,64,256]{2,1,0:T(8,128)(2,1)S(1)}, u32[]{:S(2)}, u32[]{:S(2)}) %collective-permute-start.9) | collective-permute-done | bytes 65568 | tf_op jit(solution)/shard_map/ppermute | solution.py:237
  53.9 1.9 %down_1.1 = bf16[16,4,1024]{2,1,0:T(4,128)(2,1)S(1)} custom-call(s32[4]{0:T(128)S(1)} %pad_add_fusion.place_ref, f32[8,64]{1,0:T(8,128)S(1)} %get-tuple-element.19.scl_ref, bf16[1024,8192]{1,0:T(8,128)(2,1)S(1)} %bitcast.6, bf16[2,64,256]{2,1,0:T(8,128)(2,1)S(1)} %hidden_1.1.refs_0_, bf16[2,64,256]{2,1,0:T(8,128)(2,1)S(1)} %collective-permute-done.9.refs_1_, ...), custom_call_target="tpu_custom_call" | custom-call | flops 268435456 | bytes 4194304 | tf_op jit(solution)/shard_map/down_1/pallas_call | solution.py:213
  55.8 11.1 %all_to_all.11.got_ref = bf16[16,4,1024]{2,1,0:T(4,128)(2,1)S(1)} all-to-all(bf16[16,4,1024]{2,1,0:T(4,128)(2,1)S(1)} %down_1.1), channel_id=1, replica_groups=mesh['groups'=2,'fsdp'=8,'tp'=2] {'groups','fsdp'}, dimensions={0} | all-to-all | bytes 262144 | tf_op jit(solution)/shard_map/all_to_all | solution.py:318
  67.0 1.3 %collective-permute-done.16.branch_mate_ref = f32[8,4,1024]{2,1,0:T(4,128)S(1)} collective-permute-done((f32[8,4,1024]{2,1,0:T(4,128)S(1)}, f32[8,4,1024]{2,1,0:T(4,128)S(1)}, u32[]{:S(2)}, u32[]{:S(2)}) %collective-permute-start.16) | collective-permute-done | bytes 131104 | tf_op jit(solution)/shard_map/ppermute | solution.py:237
  68.3 1.2 %final.1 = (bf16[4,4096]{1,0:T(4,128)(2,1)}, f32[1,4]{1,0:T(1,128)}) custom-call(s32[4]{0:T(128)S(1)} %pad_add_fusion.place_ref, bf16[4,4096]{1,0:T(4,128)(2,1)S(1)} %copy-done.2, bf16[4,4096]{1,0:T(4,128)(2,1)S(1)} %collective-permute-done.core_mate_ref.tok_mate_ref, f32[8,4,1024]{2,1,0:T(4,128)S(1)} %group_sum.1.branch_ref, ...), custom_call_target="tpu_custom_call" | custom-call | tf_op jit(solution)/shard_map/final/pallas_call | solution.py:213
  (45 shorter events, 5.9 us)
Async XLA Ops:
  0.6 1.6 %collective-permute-start.1 = (f32[1,4096]{1,0:T(1,128)}, f32[1,4096]{1,0:T(1,128)S(1)}, u32[]{:S(2)}, u32[]{:S(2)}) collective-permute-start(f32[1,4096]{1,0:T(1,128)} %bitcast.7), channel_id=1, source_target_pairs={{0,1},{1,0},{2,3},{3,2},{4,5},{5,4},{6,7},{7,6},{8,9},{9,8},{10,11... | collective-permute-start | bytes 49160 | tf_op jit(solution)/shard_map/ppermute | solution.py:237
  1.1 1.4 %collective-permute-start = (bf16[4,4096]{1,0:T(4,128)(2,1)}, bf16[4,4096]{1,0:T(4,128)(2,1)S(1)}, u32[]{:S(2)}, u32[]{:S(2)}) collective-permute-start(bf16[4,4096]{1,0:T(4,128)(2,1)} %tok_ref.1), channel_id=1, source_target_pairs={{0,1},{1,0},{2,3},{3,2},{4,5},{5,4},{6,7},{7,6},{8,9},{9,8},{10,11... | collective-permute-start | bytes 98312 | tf_op jit(solution)/shard_map/ppermute | solution.py:237
  3.5 16.1 %copy-start = (bf16[1024,8192]{1,0:T(8,128)(2,1)S(1)}, bf16[1024,8192]{1,0:T(8,128)(2,1)}, u32[]{:S(2)}) copy-start(bf16[1024,8192]{1,0:T(8,128)(2,1)} %gate_ref.5) | copy-start | bytes 50331652
  3.5 16.1 %copy-start.1 = (bf16[1024,8192]{1,0:T(8,128)(2,1)S(1)}, bf16[1024,8192]{1,0:T(8,128)(2,1)}, u32[]{:S(2)}) copy-start(bf16[1024,8192]{1,0:T(8,128)(2,1)} %up_ref.5) | copy-start | bytes 50331652
  21.7 9.8 %collective-permute-start.5 = (s16[144,512]{1,0:T(8,128)(2,1)S(1)}, s16[144,512]{1,0:T(8,128)(2,1)S(1)}, u32[]{:S(2)}, u32[]{:S(2)}) collective-permute-start(s16[144,512]{1,0:T(8,128)(2,1)S(1)} %get-tuple-element.28), channel_id=1, source_target_pairs={{0,2},{2,0},{4,6},{6,4},{8,10},{10,8},{12,14},{14,12},{1,3},{3,1},... | collective-permute-start | bytes 442376 | tf_op jit(solution)/shard_map/ppermute | solution.py:237
  22.9 8.7 %collective-permute-start.6 = (s16[144,512]{1,0:T(8,128)(2,1)S(1)}, s16[144,512]{1,0:T(8,128)(2,1)S(1)}, u32[]{:S(2)}, u32[]{:S(2)}) collective-permute-start(s16[144,512]{1,0:T(8,128)(2,1)S(1)} %get-tuple-element.29), channel_id=1, source_target_pairs={{0,4},{2,6},{4,0},{6,2},{8,12},{10,14},{12,8},{14,10},{1,5},{3,7},... | collective-permute-start | bytes 442376 | tf_op jit(solution)/shard_map/ppermute | solution.py:237
  23.0 8.5 %collective-permute-start.4 = (s16[144,512]{1,0:T(8,128)(2,1)S(1)}, s16[144,512]{1,0:T(8,128)(2,1)S(1)}, u32[]{:S(2)}, u32[]{:S(2)}) collective-permute-start(s16[144,512]{1,0:T(8,128)(2,1)S(1)} %get-tuple-element.22._), channel_id=1, source_target_pairs={{0,6},{2,4},{4,2},{6,0},{8,14},{10,12},{12,10},{14,8},{1,7},{3,5},... | collective-permute-start | bytes 442376 | tf_op jit(solution)/shard_map/ppermute | solution.py:237
  26.8 24.0 %slice-start = ((s8[16777216]{0:T(1024)(128)(4,1)}), s8[4194304]{0:T(1024)(128)(4,1)S(1)}, s32[]{:S(2)}) async-start(s8[16777216]{0:T(1024)(128)(4,1)} %bitcast.5), calls=%async_computation.2 | async-start | bytes 8388608
  26.8 24.0 %slice-start.1 = ((s8[16777216]{0:T(1024)(128)(4,1)}), s8[4194304]{0:T(1024)(128)(4,1)S(1)}, s32[]{:S(2)}) async-start(s8[16777216]{0:T(1024)(128)(4,1)} %bitcast.5), calls=%async_computation.3 | async-start | bytes 8388608
  26.9 23.9 %slice-start.2 = ((s8[16777216]{0:T(1024)(128)(4,1)}), s8[4194304]{0:T(1024)(128)(4,1)S(1)}, s32[]{:S(2)}) async-start(s8[16777216]{0:T(1024)(128)(4,1)} %bitcast.5), calls=%async_computation.4 | async-start | bytes 8388608
  28.9 6.5 %collective-permute-start.2 = (s16[144,512]{1,0:T(8,128)(2,1)S(1)}, s16[144,512]{1,0:T(8,128)(2,1)S(1)}, u32[]{:S(2)}, u32[]{:S(2)}) collective-permute-start(s16[144,512]{1,0:T(8,128)(2,1)S(1)} %get-tuple-element.25), channel_id=1, source_target_pairs={{0,6},{2,4},{4,2},{6,0},{8,14},{10,12},{12,10},{14,8},{1,7},{3,5},... | collective-permute-start | bytes 442376 | tf_op jit(solution)/shard_map/ppermute | solution.py:237
  29.6 9.0 %collective-permute-start.3 = (s16[144,512]{1,0:T(8,128)(2,1)S(1)}, s16[144,512]{1,0:T(8,128)(2,1)S(1)}, u32[]{:S(2)}, u32[]{:S(2)}) collective-permute-start(s16[144,512]{1,0:T(8,128)(2,1)S(1)} %get-tuple-element.26), channel_id=1, source_target_pairs={{0,4},{2,6},{4,0},{6,2},{8,12},{10,14},{12,8},{14,10},{1,5},{3,7},... | collective-permute-start | bytes 442376 | tf_op jit(solution)/shard_map/ppermute | solution.py:237
  31.8 6.9 %collective-permute-start.7 = (s16[144,512]{1,0:T(8,128)(2,1)S(1)}, s16[144,512]{1,0:T(8,128)(2,1)S(1)}, u32[]{:S(2)}, u32[]{:S(2)}) collective-permute-start(s16[144,512]{1,0:T(8,128)(2,1)S(1)} %hold_send.1), channel_id=1, source_target_pairs={{0,2},{2,0},{4,6},{6,4},{8,10},{10,8},{12,14},{14,12},{1,3},{3,1},... | collective-permute-start | bytes 442376 | tf_op jit(solution)/shard_map/ppermute | solution.py:237
  32.8 8.7 %collective-permute-start.12 = (s16[144,512]{1,0:T(8,128)(2,1)S(1)}, s16[144,512]{1,0:T(8,128)(2,1)S(1)}, u32[]{:S(2)}, u32[]{:S(2)}) collective-permute-start(s16[144,512]{1,0:T(8,128)(2,1)S(1)} %get-tuple-element.30.refs_0_), channel_id=1, source_target_pairs={{0,12},{2,14},{4,8},{6,10},{8,4},{10,6},{12,0},{14,2},{1,13},{3,15... | collective-permute-start | bytes 442376 | tf_op jit(solution)/shard_map/ppermute | solution.py:237
  38.8 7.2 %collective-permute-start.8 = (s16[144,512]{1,0:T(8,128)(2,1)S(1)}, s16[144,512]{1,0:T(8,128)(2,1)S(1)}, u32[]{:S(2)}, u32[]{:S(2)}) collective-permute-start(s16[144,512]{1,0:T(8,128)(2,1)S(1)} %get-tuple-element.32), channel_id=1, source_target_pairs={{0,12},{2,14},{4,8},{6,10},{8,4},{10,6},{12,0},{14,2},{1,13},{3,15... | collective-permute-start | bytes 442376 | tf_op jit(solution)/shard_map/ppermute | solution.py:237
  41.5 7.2 %collective-permute-start.15 = (bf16[2,64,256]{2,1,0:T(8,128)(2,1)S(1)}, bf16[2,64,256]{2,1,0:T(8,128)(2,1)S(1)}, u32[]{:S(2)}, u32[]{:S(2)}) collective-permute-start(bf16[2,64,256]{2,1,0:T(8,128)(2,1)S(1)} %hidden_0.1.refs_0_), channel_id=1, source_target_pairs={{0,4},{2,6},{4,0},{6,2},{8,12},{10,14},{12,8},{14,10},{1,5},{3,7},... | collective-permute-start | bytes 196616 | tf_op jit(solution)/shard_map/ppermute | solution.py:237
  43.5 6.2 %collective-permute-start.14 = (bf16[2,64,256]{2,1,0:T(8,128)(2,1)S(1)}, bf16[2,64,256]{2,1,0:T(8,128)(2,1)S(1)}, u32[]{:S(2)}, u32[]{:S(2)}) collective-permute-start(bf16[2,64,256]{2,1,0:T(8,128)(2,1)S(1)} %hidden_0.1.refs_0_), channel_id=1, source_target_pairs={{0,2},{2,0},{4,6},{6,4},{8,10},{10,8},{12,14},{14,12},{1,3},{3,1},... | collective-permute-start | bytes 196616 | tf_op jit(solution)/shard_map/ppermute | solution.py:237
  45.0 5.8 %collective-permute-start.13 = (bf16[2,64,256]{2,1,0:T(8,128)(2,1)S(1)}, bf16[2,64,256]{2,1,0:T(8,128)(2,1)S(1)}, u32[]{:S(2)}, u32[]{:S(2)}) collective-permute-start(bf16[2,64,256]{2,1,0:T(8,128)(2,1)S(1)} %hidden_0.1.refs_0_), channel_id=1, source_target_pairs={{0,6},{2,4},{4,2},{6,0},{8,14},{10,12},{12,10},{14,8},{1,7},{3,5},... | collective-permute-start | bytes 196616 | tf_op jit(solution)/shard_map/ppermute | solution.py:237
  46.1 6.6 %collective-permute-start.11 = (bf16[2,64,256]{2,1,0:T(8,128)(2,1)S(1)}, bf16[2,64,256]{2,1,0:T(8,128)(2,1)S(1)}, u32[]{:S(2)}, u32[]{:S(2)}) collective-permute-start(bf16[2,64,256]{2,1,0:T(8,128)(2,1)S(1)} %hidden_1.1.refs_0_), channel_id=1, source_target_pairs={{0,2},{2,0},{4,6},{6,4},{8,10},{10,8},{12,14},{14,12},{1,3},{3,1},... | collective-permute-start | bytes 196616 | tf_op jit(solution)/shard_map/ppermute | solution.py:237
  47.3 5.4 %collective-permute-start.10 = (bf16[2,64,256]{2,1,0:T(8,128)(2,1)S(1)}, bf16[2,64,256]{2,1,0:T(8,128)(2,1)S(1)}, u32[]{:S(2)}, u32[]{:S(2)}) collective-permute-start(bf16[2,64,256]{2,1,0:T(8,128)(2,1)S(1)} %hidden_1.1.refs_0_), channel_id=1, source_target_pairs={{0,4},{2,6},{4,0},{6,2},{8,12},{10,14},{12,8},{14,10},{1,5},{3,7},... | collective-permute-start | bytes 196616 | tf_op jit(solution)/shard_map/ppermute | solution.py:237
  48.7 5.2 %collective-permute-start.9 = (bf16[2,64,256]{2,1,0:T(8,128)(2,1)S(1)}, bf16[2,64,256]{2,1,0:T(8,128)(2,1)S(1)}, u32[]{:S(2)}, u32[]{:S(2)}) collective-permute-start(bf16[2,64,256]{2,1,0:T(8,128)(2,1)S(1)} %hidden_1.1.refs_0_), channel_id=1, source_target_pairs={{0,6},{2,4},{4,2},{6,0},{8,14},{10,12},{12,10},{14,8},{1,7},{3,5},... | collective-permute-start | bytes 196616 | tf_op jit(solution)/shard_map/ppermute | solution.py:237
  50.8 17.5 %copy-start.2 = (bf16[4,4096]{1,0:T(4,128)(2,1)S(1)}, bf16[4,4096]{1,0:T(4,128)(2,1)}, u32[]{:S(2)}) copy-start(bf16[4,4096]{1,0:T(4,128)(2,1)} %tok_ref.1) | copy-start | bytes 98308
  50.8 17.5 %copy-start.3 = (f32[4096]{0:T(1024)S(1)}, f32[4096]{0:T(1024)}, u32[]{:S(2)}) copy-start(f32[4096]{0:T(1024)} %param.19) | copy-start | bytes 49156
  66.9 1.4 %collective-permute-start.16 = (f32[8,4,1024]{2,1,0:T(4,128)S(1)}, f32[8,4,1024]{2,1,0:T(4,128)S(1)}, u32[]{:S(2)}, u32[]{:S(2)}) collective-permute-start(f32[8,4,1024]{2,1,0:T(4,128)S(1)} %group_sum.1.branch_ref), channel_id=1, source_target_pairs={{0,1},{1,0},{2,3},{3,2},{4,5},{5,4},{6,7},{7,6},{8,9},{9,8},{10,11... | collective-permute-start | bytes 393224 | tf_op jit(solution)/shard_map/ppermute | solution.py:237
  (1 other events, 12.1 us)

commit v6 on v5

--- a/solution.py
+++ b/solution.py
@@ -302,7 +302,8 @@
     held = call(hold_kernel, "hold_send", [sends_1[2], unread(both[0][1])], coded(2))
     got.append([swap(send, "fsdp", q) for send, q in zip((*sends_1[:2], held), orders[1])])
     both.append(call(both_kernel, "both_1", [kept[1], *got[1], unread(hbm(down_codes))], [sums, coded(2)]))
-    for p, order in enumerate(orders):
+    order = (1, 2, 3)
+    for p in range(2):
         keep, send = both[p]
         hidden = call(hidden_kernel, f"hidden_{p}", [keep, swap(send, "fsdp", fars[p])], shape((2, all_rows, wide), BF16))
         branch = call(
@@ -347,7 +348,7 @@
             n == 8
             and mesh.shape["groups"] == 2
             and mesh.shape["tp"] == 2
-            and codes.shape[0] % TILE == 0
+            and codes.shape[0] % (2 * TILE) == 0
             and codes.shape[1] == 8 * n * TILE
         )
         if fits:

time: 69.8 us -> 69 us (0.989)
  waiting for transfers between devices: 10.5 us -> 9.09 us
  blocking collectives: 27.1 us -> 27.8 us
    ppermute x17, waiting for transfers between devices: 10.5 us -> 9.09 us  [swap(): lax.ppermute(x, axis, [(i, i ^ bit) for i in range(n if axis == 'fsdp' el...]
where the time goes in v6:
time: 69 us; the launch traced here: 68.7 us
  blocking collectives  27.8 us (40%)
  starting transfers between devices  18.1 us (26%)
  Pallas kernels  12.2 us (18%)
  waiting for transfers between devices  9.09 us (13%)
  between operations  1.49 us (2%)
    ppermute x17, starting transfers between devices, swap(): lax.ppermute(x, axis, [(i, i ^ bit) for i in range(n if axis == 'fsdp' el...  18.1 us
    all_to_all x1, blocking collectives, body_split(): lax.all_to_all(normed, rows_axes, 0, 0, tiled=True)  16 us
    pallas_call x15, Pallas kernels, call(): pl.pallas_call(kernel, in_specs=specs, out_specs=jax.tree.map(lambda _: V...  12.2 us
    all_to_all x1, blocking collectives, body_split(): got = lax.all_to_all(branch, rows_axes, 0, 0, tiled=True)  11.7 us
    ppermute x17, waiting for transfers between devices, swap(): lax.ppermute(x, axis, [(i, i ^ bit) for i in range(n if axis == 'fsdp' el...  9.09 us
  transfers between devices with their start and end apart: 17, of which 9 were waited for; matrix products, arithmetic and copies ran while one was open for 0% of the time, Pallas kernels for 9%

profile of v6, /device:TPU:0, one launch (start us, length us, event | category | flops | bytes accessed | tf_op | source)
XLA Modules:
  0.0 68.7 jit_solution(12793271660457304537)
XLA Ops:
  2.6 1.0 %norm.1 = (bf16[16,4,1024]{2,1,0:T(4,128)(2,1)S(1)}, f32[2,8,64]{2,1,0:T(8,128)S(1)}, f32[8,64]{1,0:T(8,128)S(1)}) custom-call(s32[4]{0:T(128)S(1)} %pad_add_fusion.place_ref, bf16[4,4096]{1,0:T(4,128)(2,1)} %tok_ref.1, bf16[4,4096]{1,0:T(4,128)(2,1)S(1)} %collective-permute-done.core_mate_ref.tok_mate_ref, bf16[8192]{0:T(1024)(128)(2,1)} %gain_ref.1, ...), custom_call_target="tpu_custom_call" | custom-call | tf_op jit(solution)/shard_map/norm/pallas_call | solution.py:213
  3.6 16.0 %all_to_all.10.got_ref = bf16[16,4,1024]{2,1,0:T(4,128)(2,1)S(1)} all-to-all(bf16[16,4,1024]{2,1,0:T(4,128)(2,1)S(1)} %hold.1), channel_id=1, replica_groups=mesh['groups'=2,'fsdp'=8,'tp'=2] {'groups','fsdp'}, dimensions={0} | all-to-all | bytes 262144 | tf_op jit(solution)/shard_map/all_to_all | solution.py:269
  19.7 2.0 %gate_up_send_0.1 = (s16[144,512]{1,0:T(8,128)(2,1)S(1)}, s16[144,512]{1,0:T(8,128)(2,1)S(1)}, s16[144,512]{1,0:T(8,128)(2,1)S(1)}) custom-call(s32[4]{0:T(128)S(1)} %pad_add_fusion.place_ref, f32[2,8,64]{2,1,0:T(8,128)S(1)} %get-tuple-element.20.scl_ref, bf16[64,1024]{1,0:T(8,128)(2,1)S(1)} %rows.1.x_ref._, bf16[1024,8192]{1,0:T(8,128)(2,1)S(1)} %copy-done, ...), custom_call_target="tpu_custom_call" | custom-call | flops 268435456 | bytes 4194304 | tf_op jit(solution)/shard_map/gate_up_send_0/pallas_call | solution.py:213
  21.7 1.2 %collective-permute-start.5 = (s16[144,512]{1,0:T(8,128)(2,1)S(1)}, s16[144,512]{1,0:T(8,128)(2,1)S(1)}, u32[]{:S(2)}, u32[]{:S(2)}) collective-permute-start(s16[144,512]{1,0:T(8,128)(2,1)S(1)} %get-tuple-element.28), channel_id=1, source_target_pairs={{0,2},{2,0},{4,6},{6,4},{8,10},{10,8},{12,14},{14,12},{1,3},{3,1},... | collective-permute-start | bytes 442376 | tf_op jit(solution)/shard_map/ppermute | solution.py:237
  23.0 2.3 %collective-permute-start.4 = (s16[144,512]{1,0:T(8,128)(2,1)S(1)}, s16[144,512]{1,0:T(8,128)(2,1)S(1)}, u32[]{:S(2)}, u32[]{:S(2)}) collective-permute-start(s16[144,512]{1,0:T(8,128)(2,1)S(1)} %get-tuple-element.22._), channel_id=1, source_target_pairs={{0,6},{2,4},{4,2},{6,0},{8,14},{10,12},{12,10},{14,8},{1,7},{3,5},... | collective-permute-start | bytes 442376 | tf_op jit(solution)/shard_map/ppermute | solution.py:237
  25.3 1.5 %gate_up_keep.1 = (f32[2,64,512]{2,1,0:T(8,128)S(1)}, f32[2,64,512]{2,1,0:T(8,128)S(1)}) custom-call(s32[4]{0:T(128)S(1)} %pad_add_fusion.place_ref, f32[2,8,64]{2,1,0:T(8,128)S(1)} %get-tuple-element.20.scl_ref, bf16[64,1024]{1,0:T(8,128)(2,1)S(1)} %rows.1.x_ref._, bf16[1024,8192]{1,0:T(8,128)(2,1)S(1)} %copy-done, bf16[1024,8192]{1,0:T(8,128)(2,1)S(1)} %copy-done.1, ...), custom_call_target="tpu_custom_call" | custom-call | flops 268435456 | bytes 4194304 | tf_op jit(solution)/shard_map/gate_up_keep/pallas_call | solution.py:213
  26.9 2.0 %gate_up_send_1.1 = (s16[144,512]{1,0:T(8,128)(2,1)S(1)}, s16[144,512]{1,0:T(8,128)(2,1)S(1)}, s16[144,512]{1,0:T(8,128)(2,1)S(1)}) custom-call(s32[4]{0:T(128)S(1)} %pad_add_fusion.place_ref, f32[2,8,64]{2,1,0:T(8,128)S(1)} %get-tuple-element.20.scl_ref, bf16[64,1024]{1,0:T(8,128)(2,1)S(1)} %rows.1.x_ref._, bf16[1024,8192]{1,0:T(8,128)(2,1)S(1)} %copy-done, ...), custom_call_target="tpu_custom_call" | custom-call | flops 268435456 | bytes 4194304 | tf_op jit(solution)/shard_map/gate_up_send_1/pallas_call | solution.py:213
  28.9 0.7 %collective-permute-start.2 = (s16[144,512]{1,0:T(8,128)(2,1)S(1)}, s16[144,512]{1,0:T(8,128)(2,1)S(1)}, u32[]{:S(2)}, u32[]{:S(2)}) collective-permute-start(s16[144,512]{1,0:T(8,128)(2,1)S(1)} %get-tuple-element.25), channel_id=1, source_target_pairs={{0,6},{2,4},{4,2},{6,0},{8,14},{10,12},{12,10},{14,8},{1,7},{3,5},... | collective-permute-start | bytes 442376 | tf_op jit(solution)/shard_map/ppermute | solution.py:237
  29.6 1.9 %collective-permute-start.3 = (s16[144,512]{1,0:T(8,128)(2,1)S(1)}, s16[144,512]{1,0:T(8,128)(2,1)S(1)}, u32[]{:S(2)}, u32[]{:S(2)}) collective-permute-start(s16[144,512]{1,0:T(8,128)(2,1)S(1)} %get-tuple-element.26), channel_id=1, source_target_pairs={{0,4},{2,6},{4,0},{6,2},{8,12},{10,14},{12,8},{14,10},{1,5},{3,7},... | collective-permute-start | bytes 442376 | tf_op jit(solution)/shard_map/ppermute | solution.py:237
  31.8 1.0 %collective-permute-start.7 = (s16[144,512]{1,0:T(8,128)(2,1)S(1)}, s16[144,512]{1,0:T(8,128)(2,1)S(1)}, u32[]{:S(2)}, u32[]{:S(2)}) collective-permute-start(s16[144,512]{1,0:T(8,128)(2,1)S(1)} %hold_send.1), channel_id=1, source_target_pairs={{0,2},{2,0},{4,6},{6,4},{8,10},{10,8},{12,14},{14,12},{1,3},{3,1},... | collective-permute-start | bytes 442376 | tf_op jit(solution)/shard_map/ppermute | solution.py:237
  32.8 1.7 %collective-permute-start.12 = (s16[144,512]{1,0:T(8,128)(2,1)S(1)}, s16[144,512]{1,0:T(8,128)(2,1)S(1)}, u32[]{:S(2)}, u32[]{:S(2)}) collective-permute-start(s16[144,512]{1,0:T(8,128)(2,1)S(1)} %get-tuple-element.30.refs_0_), channel_id=1, source_target_pairs={{0,12},{2,14},{4,8},{6,10},{8,4},{10,6},{12,0},{14,2},{1,13},{3,15... | collective-permute-start | bytes 442376 | tf_op jit(solution)/shard_map/ppermute | solution.py:237
  34.5 1.0 %collective-permute-done.2.refs_0_ = s16[144,512]{1,0:T(8,128)(2,1)S(1)} collective-permute-done((s16[144,512]{1,0:T(8,128)(2,1)S(1)}, s16[144,512]{1,0:T(8,128)(2,1)S(1)}, u32[]{:S(2)}, u32[]{:S(2)}) %collective-permute-start.2) | collective-permute-done | bytes 147488 | tf_op jit(solution)/shard_map/ppermute | solution.py:237
  35.5 3.2 %collective-permute-done.3.refs_1_ = s16[144,512]{1,0:T(8,128)(2,1)S(1)} collective-permute-done((s16[144,512]{1,0:T(8,128)(2,1)S(1)}, s16[144,512]{1,0:T(8,128)(2,1)S(1)}, u32[]{:S(2)}, u32[]{:S(2)}) %collective-permute-start.3) | collective-permute-done | bytes 147488 | tf_op jit(solution)/shard_map/ppermute | solution.py:237
  38.8 1.4 %collective-permute-start.8 = (s16[144,512]{1,0:T(8,128)(2,1)S(1)}, s16[144,512]{1,0:T(8,128)(2,1)S(1)}, u32[]{:S(2)}, u32[]{:S(2)}) collective-permute-start(s16[144,512]{1,0:T(8,128)(2,1)S(1)} %get-tuple-element.32), channel_id=1, source_target_pairs={{0,12},{2,14},{4,8},{6,10},{8,4},{10,6},{12,0},{14,2},{1,13},{3,15... | collective-permute-start | bytes 442376 | tf_op jit(solution)/shard_map/ppermute | solution.py:237
  40.3 1.1 %collective-permute-done.12.got_ref = s16[144,512]{1,0:T(8,128)(2,1)S(1)} collective-permute-done((s16[144,512]{1,0:T(8,128)(2,1)S(1)}, s16[144,512]{1,0:T(8,128)(2,1)S(1)}, u32[]{:S(2)}, u32[]{:S(2)}) %collective-permute-start.12) | collective-permute-done | bytes 147488 | tf_op jit(solution)/shard_map/ppermute | solution.py:237
  41.5 2.9 %collective-permute-start.15 = (bf16[2,64,256]{2,1,0:T(8,128)(2,1)S(1)}, bf16[2,64,256]{2,1,0:T(8,128)(2,1)S(1)}, u32[]{:S(2)}, u32[]{:S(2)}) collective-permute-start(bf16[2,64,256]{2,1,0:T(8,128)(2,1)S(1)} %hidden_0.1.refs_0_), channel_id=1, source_target_pairs={{0,6},{2,4},{4,2},{6,0},{8,14},{10,12},{12,10},{14,8},{1,7},{3,5},... | collective-permute-start | bytes 196616 | tf_op jit(solution)/shard_map/ppermute | solution.py:237
  45.0 1.0 %collective-permute-done.8.got_ref = s16[144,512]{1,0:T(8,128)(2,1)S(1)} collective-permute-done((s16[144,512]{1,0:T(8,128)(2,1)S(1)}, s16[144,512]{1,0:T(8,128)(2,1)S(1)}, u32[]{:S(2)}, u32[]{:S(2)}) %collective-permute-start.8) | collective-permute-done | bytes 147488 | tf_op jit(solution)/shard_map/ppermute | solution.py:237
  46.1 2.0 %collective-permute-start.11 = (bf16[2,64,256]{2,1,0:T(8,128)(2,1)S(1)}, bf16[2,64,256]{2,1,0:T(8,128)(2,1)S(1)}, u32[]{:S(2)}, u32[]{:S(2)}) collective-permute-start(bf16[2,64,256]{2,1,0:T(8,128)(2,1)S(1)} %hidden_1.1.refs_0_), channel_id=1, source_target_pairs={{0,6},{2,4},{4,2},{6,0},{8,14},{10,12},{12,10},{14,8},{1,7},{3,5},... | collective-permute-start | bytes 196616 | tf_op jit(solution)/shard_map/ppermute | solution.py:237
  48.2 1.5 %collective-permute-start.9 = (bf16[2,64,256]{2,1,0:T(8,128)(2,1)S(1)}, bf16[2,64,256]{2,1,0:T(8,128)(2,1)S(1)}, u32[]{:S(2)}, u32[]{:S(2)}) collective-permute-start(bf16[2,64,256]{2,1,0:T(8,128)(2,1)S(1)} %hidden_1.1.refs_0_), channel_id=1, source_target_pairs={{0,2},{2,0},{4,6},{6,4},{8,10},{10,8},{12,14},{14,12},{1,3},{3,1},... | collective-permute-start | bytes 196616 | tf_op jit(solution)/shard_map/ppermute | solution.py:237
  49.7 1.8 %down_0.1.refs_4_ = f32[1024,64]{1,0:T(8,128)S(1)} custom-call(s32[4]{0:T(128)S(1)} %pad_add_fusion.place_ref, f32[8,64]{1,0:T(8,128)S(1)} %get-tuple-element.19.scl_ref, bf16[1024,8192]{1,0:T(8,128)(2,1)S(1)} %bitcast.6, bf16[2,64,256]{2,1,0:T(8,128)(2,1)S(1)} %hidden_0.1.refs_0_, bf16[2,64,256]{2,1,0:T(8,128)(2,1)S(1)} %collective-permute-done.13.refs_1_, ...), custom_call_target="tpu_custom_call" | custom-call | flops 268435456 | bytes 4194304 | tf_op jit(solution)/shard_map/down_0/pallas_call | solution.py:213
  52.4 1.9 %down_1.1 = bf16[16,4,1024]{2,1,0:T(4,128)(2,1)S(1)} custom-call(s32[4]{0:T(128)S(1)} %pad_add_fusion.place_ref, f32[8,64]{1,0:T(8,128)S(1)} %get-tuple-element.19.scl_ref, bf16[1024,8192]{1,0:T(8,128)(2,1)S(1)} %bitcast.6, bf16[2,64,256]{2,1,0:T(8,128)(2,1)S(1)} %hidden_1.1.refs_0_, bf16[2,64,256]{2,1,0:T(8,128)(2,1)S(1)} %collective-permute-done.9.refs_1_, ...), custom_call_target="tpu_custom_call" | custom-call | flops 268435456 | bytes 4194304 | tf_op jit(solution)/shard_map/down_1/pallas_call | solution.py:213
  54.3 11.7 %all_to_all.11.got_ref = bf16[16,4,1024]{2,1,0:T(4,128)(2,1)S(1)} all-to-all(bf16[16,4,1024]{2,1,0:T(4,128)(2,1)S(1)} %down_1.1), channel_id=1, replica_groups=mesh['groups'=2,'fsdp'=8,'tp'=2] {'groups','fsdp'}, dimensions={0} | all-to-all | bytes 262144 | tf_op jit(solution)/shard_map/all_to_all | solution.py:319
  66.2 1.3 %collective-permute-done.16.branch_mate_ref = f32[8,4,1024]{2,1,0:T(4,128)S(1)} collective-permute-done((f32[8,4,1024]{2,1,0:T(4,128)S(1)}, f32[8,4,1024]{2,1,0:T(4,128)S(1)}, u32[]{:S(2)}, u32[]{:S(2)}) %collective-permute-start.16) | collective-permute-done | bytes 131104 | tf_op jit(solution)/shard_map/ppermute | solution.py:237
  67.5 1.2 %final.1 = (bf16[4,4096]{1,0:T(4,128)(2,1)}, f32[1,4]{1,0:T(1,128)}) custom-call(s32[4]{0:T(128)S(1)} %pad_add_fusion.place_ref, bf16[4,4096]{1,0:T(4,128)(2,1)S(1)} %copy-done.2, bf16[4,4096]{1,0:T(4,128)(2,1)S(1)} %collective-permute-done.core_mate_ref.tok_mate_ref, f32[8,4,1024]{2,1,0:T(4,128)S(1)} %group_sum.1.branch_ref, ...), custom_call_target="tpu_custom_call" | custom-call | tf_op jit(solution)/shard_map/final/pallas_call | solution.py:213
  (45 shorter events, 3.6 us)
Async XLA Ops:
  0.6 1.6 %collective-permute-start.1 = (f32[1,4096]{1,0:T(1,128)}, f32[1,4096]{1,0:T(1,128)S(1)}, u32[]{:S(2)}, u32[]{:S(2)}) collective-permute-start(f32[1,4096]{1,0:T(1,128)} %bitcast.7), channel_id=1, source_target_pairs={{0,1},{1,0},{2,3},{3,2},{4,5},{5,4},{6,7},{7,6},{8,9},{9,8},{10,11... | collective-permute-start | bytes 49160 | tf_op jit(solution)/shard_map/ppermute | solution.py:237
  1.1 1.4 %collective-permute-start = (bf16[4,4096]{1,0:T(4,128)(2,1)}, bf16[4,4096]{1,0:T(4,128)(2,1)S(1)}, u32[]{:S(2)}, u32[]{:S(2)}) collective-permute-start(bf16[4,4096]{1,0:T(4,128)(2,1)} %tok_ref.1), channel_id=1, source_target_pairs={{0,1},{1,0},{2,3},{3,2},{4,5},{5,4},{6,7},{7,6},{8,9},{9,8},{10,11... | collective-permute-start | bytes 98312 | tf_op jit(solution)/shard_map/ppermute | solution.py:237
  3.5 16.1 %copy-start = (bf16[1024,8192]{1,0:T(8,128)(2,1)S(1)}, bf16[1024,8192]{1,0:T(8,128)(2,1)}, u32[]{:S(2)}) copy-start(bf16[1024,8192]{1,0:T(8,128)(2,1)} %gate_ref.5) | copy-start | bytes 50331652
  3.5 16.1 %copy-start.1 = (bf16[1024,8192]{1,0:T(8,128)(2,1)S(1)}, bf16[1024,8192]{1,0:T(8,128)(2,1)}, u32[]{:S(2)}) copy-start(bf16[1024,8192]{1,0:T(8,128)(2,1)} %up_ref.5) | copy-start | bytes 50331652
  21.7 9.8 %collective-permute-start.5 = (s16[144,512]{1,0:T(8,128)(2,1)S(1)}, s16[144,512]{1,0:T(8,128)(2,1)S(1)}, u32[]{:S(2)}, u32[]{:S(2)}) collective-permute-start(s16[144,512]{1,0:T(8,128)(2,1)S(1)} %get-tuple-element.28), channel_id=1, source_target_pairs={{0,2},{2,0},{4,6},{6,4},{8,10},{10,8},{12,14},{14,12},{1,3},{3,1},... | collective-permute-start | bytes 442376 | tf_op jit(solution)/shard_map/ppermute | solution.py:237
  22.9 8.7 %collective-permute-start.6 = (s16[144,512]{1,0:T(8,128)(2,1)S(1)}, s16[144,512]{1,0:T(8,128)(2,1)S(1)}, u32[]{:S(2)}, u32[]{:S(2)}) collective-permute-start(s16[144,512]{1,0:T(8,128)(2,1)S(1)} %get-tuple-element.29), channel_id=1, source_target_pairs={{0,4},{2,6},{4,0},{6,2},{8,12},{10,14},{12,8},{14,10},{1,5},{3,7},... | collective-permute-start | bytes 442376 | tf_op jit(solution)/shard_map/ppermute | solution.py:237
  23.0 8.5 %collective-permute-start.4 = (s16[144,512]{1,0:T(8,128)(2,1)S(1)}, s16[144,512]{1,0:T(8,128)(2,1)S(1)}, u32[]{:S(2)}, u32[]{:S(2)}) collective-permute-start(s16[144,512]{1,0:T(8,128)(2,1)S(1)} %get-tuple-element.22._), channel_id=1, source_target_pairs={{0,6},{2,4},{4,2},{6,0},{8,14},{10,12},{12,10},{14,8},{1,7},{3,5},... | collective-permute-start | bytes 442376 | tf_op jit(solution)/shard_map/ppermute | solution.py:237
  26.8 22.8 %slice-start = ((s8[16777216]{0:T(1024)(128)(4,1)}), s8[4194304]{0:T(1024)(128)(4,1)S(1)}, s32[]{:S(2)}) async-start(s8[16777216]{0:T(1024)(128)(4,1)} %bitcast.5), calls=%async_computation.2 | async-start | bytes 8388608
  26.8 22.8 %slice-start.1 = ((s8[16777216]{0:T(1024)(128)(4,1)}), s8[4194304]{0:T(1024)(128)(4,1)S(1)}, s32[]{:S(2)}) async-start(s8[16777216]{0:T(1024)(128)(4,1)} %bitcast.5), calls=%async_computation.3 | async-start | bytes 8388608
  26.9 22.8 %slice-start.2 = ((s8[16777216]{0:T(1024)(128)(4,1)}), s8[4194304]{0:T(1024)(128)(4,1)S(1)}, s32[]{:S(2)}) async-start(s8[16777216]{0:T(1024)(128)(4,1)} %bitcast.5), calls=%async_computation.4 | async-start | bytes 8388608
  28.9 6.5 %collective-permute-start.2 = (s16[144,512]{1,0:T(8,128)(2,1)S(1)}, s16[144,512]{1,0:T(8,128)(2,1)S(1)}, u32[]{:S(2)}, u32[]{:S(2)}) collective-permute-start(s16[144,512]{1,0:T(8,128)(2,1)S(1)} %get-tuple-element.25), channel_id=1, source_target_pairs={{0,6},{2,4},{4,2},{6,0},{8,14},{10,12},{12,10},{14,8},{1,7},{3,5},... | collective-permute-start | bytes 442376 | tf_op jit(solution)/shard_map/ppermute | solution.py:237
  29.6 9.0 %collective-permute-start.3 = (s16[144,512]{1,0:T(8,128)(2,1)S(1)}, s16[144,512]{1,0:T(8,128)(2,1)S(1)}, u32[]{:S(2)}, u32[]{:S(2)}) collective-permute-start(s16[144,512]{1,0:T(8,128)(2,1)S(1)} %get-tuple-element.26), channel_id=1, source_target_pairs={{0,4},{2,6},{4,0},{6,2},{8,12},{10,14},{12,8},{14,10},{1,5},{3,7},... | collective-permute-start | bytes 442376 | tf_op jit(solution)/shard_map/ppermute | solution.py:237
  31.8 6.9 %collective-permute-start.7 = (s16[144,512]{1,0:T(8,128)(2,1)S(1)}, s16[144,512]{1,0:T(8,128)(2,1)S(1)}, u32[]{:S(2)}, u32[]{:S(2)}) collective-permute-start(s16[144,512]{1,0:T(8,128)(2,1)S(1)} %hold_send.1), channel_id=1, source_target_pairs={{0,2},{2,0},{4,6},{6,4},{8,10},{10,8},{12,14},{14,12},{1,3},{3,1},... | collective-permute-start | bytes 442376 | tf_op jit(solution)/shard_map/ppermute | solution.py:237
  32.8 8.6 %collective-permute-start.12 = (s16[144,512]{1,0:T(8,128)(2,1)S(1)}, s16[144,512]{1,0:T(8,128)(2,1)S(1)}, u32[]{:S(2)}, u32[]{:S(2)}) collective-permute-start(s16[144,512]{1,0:T(8,128)(2,1)S(1)} %get-tuple-element.30.refs_0_), channel_id=1, source_target_pairs={{0,12},{2,14},{4,8},{6,10},{8,4},{10,6},{12,0},{14,2},{1,13},{3,15... | collective-permute-start | bytes 442376 | tf_op jit(solution)/shard_map/ppermute | solution.py:237
  38.8 7.2 %collective-permute-start.8 = (s16[144,512]{1,0:T(8,128)(2,1)S(1)}, s16[144,512]{1,0:T(8,128)(2,1)S(1)}, u32[]{:S(2)}, u32[]{:S(2)}) collective-permute-start(s16[144,512]{1,0:T(8,128)(2,1)S(1)} %get-tuple-element.32), channel_id=1, source_target_pairs={{0,12},{2,14},{4,8},{6,10},{8,4},{10,6},{12,0},{14,2},{1,13},{3,15... | collective-permute-start | bytes 442376 | tf_op jit(solution)/shard_map/ppermute | solution.py:237
  41.5 6.7 %collective-permute-start.15 = (bf16[2,64,256]{2,1,0:T(8,128)(2,1)S(1)}, bf16[2,64,256]{2,1,0:T(8,128)(2,1)S(1)}, u32[]{:S(2)}, u32[]{:S(2)}) collective-permute-start(bf16[2,64,256]{2,1,0:T(8,128)(2,1)S(1)} %hidden_0.1.refs_0_), channel_id=1, source_target_pairs={{0,6},{2,4},{4,2},{6,0},{8,14},{10,12},{12,10},{14,8},{1,7},{3,5},... | collective-permute-start | bytes 196616 | tf_op jit(solution)/shard_map/ppermute | solution.py:237
  44.4 5.3 %collective-permute-start.14 = (bf16[2,64,256]{2,1,0:T(8,128)(2,1)S(1)}, bf16[2,64,256]{2,1,0:T(8,128)(2,1)S(1)}, u32[]{:S(2)}, u32[]{:S(2)}) collective-permute-start(bf16[2,64,256]{2,1,0:T(8,128)(2,1)S(1)} %hidden_0.1.refs_0_), channel_id=1, source_target_pairs={{0,4},{2,6},{4,0},{6,2},{8,12},{10,14},{12,8},{14,10},{1,5},{3,7},... | collective-permute-start | bytes 196616 | tf_op jit(solution)/shard_map/ppermute | solution.py:237
  44.4 5.3 %collective-permute-start.13 = (bf16[2,64,256]{2,1,0:T(8,128)(2,1)S(1)}, bf16[2,64,256]{2,1,0:T(8,128)(2,1)S(1)}, u32[]{:S(2)}, u32[]{:S(2)}) collective-permute-start(bf16[2,64,256]{2,1,0:T(8,128)(2,1)S(1)} %hidden_0.1.refs_0_), channel_id=1, source_target_pairs={{0,2},{2,0},{4,6},{6,4},{8,10},{10,8},{12,14},{14,12},{1,3},{3,1},... | collective-permute-start | bytes 196616 | tf_op jit(solution)/shard_map/ppermute | solution.py:237
  46.1 5.6 %collective-permute-start.11 = (bf16[2,64,256]{2,1,0:T(8,128)(2,1)S(1)}, bf16[2,64,256]{2,1,0:T(8,128)(2,1)S(1)}, u32[]{:S(2)}, u32[]{:S(2)}) collective-permute-start(bf16[2,64,256]{2,1,0:T(8,128)(2,1)S(1)} %hidden_1.1.refs_0_), channel_id=1, source_target_pairs={{0,6},{2,4},{4,2},{6,0},{8,14},{10,12},{12,10},{14,8},{1,7},{3,5},... | collective-permute-start | bytes 196616 | tf_op jit(solution)/shard_map/ppermute | solution.py:237
  48.2 4.3 %collective-permute-start.10 = (bf16[2,64,256]{2,1,0:T(8,128)(2,1)S(1)}, bf16[2,64,256]{2,1,0:T(8,128)(2,1)S(1)}, u32[]{:S(2)}, u32[]{:S(2)}) collective-permute-start(bf16[2,64,256]{2,1,0:T(8,128)(2,1)S(1)} %hidden_1.1.refs_0_), channel_id=1, source_target_pairs={{0,4},{2,6},{4,0},{6,2},{8,12},{10,14},{12,8},{14,10},{1,5},{3,7},... | collective-permute-start | bytes 196616 | tf_op jit(solution)/shard_map/ppermute | solution.py:237
  48.2 4.3 %collective-permute-start.9 = (bf16[2,64,256]{2,1,0:T(8,128)(2,1)S(1)}, bf16[2,64,256]{2,1,0:T(8,128)(2,1)S(1)}, u32[]{:S(2)}, u32[]{:S(2)}) collective-permute-start(bf16[2,64,256]{2,1,0:T(8,128)(2,1)S(1)} %hidden_1.1.refs_0_), channel_id=1, source_target_pairs={{0,2},{2,0},{4,6},{6,4},{8,10},{10,8},{12,14},{14,12},{1,3},{3,1},... | collective-permute-start | bytes 196616 | tf_op jit(solution)/shard_map/ppermute | solution.py:237
  49.7 17.8 %copy-start.2 = (bf16[4,4096]{1,0:T(4,128)(2,1)S(1)}, bf16[4,4096]{1,0:T(4,128)(2,1)}, u32[]{:S(2)}) copy-start(bf16[4,4096]{1,0:T(4,128)(2,1)} %tok_ref.1) | copy-start | bytes 98308
  49.7 17.8 %copy-start.3 = (f32[4096]{0:T(1024)S(1)}, f32[4096]{0:T(1024)}, u32[]{:S(2)}) copy-start(f32[4096]{0:T(1024)} %param.19) | copy-start | bytes 49156
  66.1 1.4 %collective-permute-start.16 = (f32[8,4,1024]{2,1,0:T(4,128)S(1)}, f32[8,4,1024]{2,1,0:T(4,128)S(1)}, u32[]{:S(2)}, u32[]{:S(2)}) collective-permute-start(f32[8,4,1024]{2,1,0:T(4,128)S(1)} %group_sum.1.branch_ref), channel_id=1, source_target_pairs={{0,1},{1,0},{2,3},{3,2},{4,5},{5,4},{6,7},{7,6},{8,9},{9,8},{10,11... | collective-permute-start | bytes 393224 | tf_op jit(solution)/shard_map/ppermute | solution.py:237
  (1 other events, 11.0 us)

commit v7 on v6

--- a/solution.py
+++ b/solution.py
@@ -299,8 +299,8 @@
     got = [[swap(send, "fsdp", q) for send, q in zip(sends_0, orders[0])]]
     branch = None
     both = [call(both_kernel, "both_0", [kept[0], *got[0]], [sums, coded(2)])]
-    held = call(hold_kernel, "hold_send", [sends_1[2], unread(both[0][1])], coded(2))
-    got.append([swap(send, "fsdp", q) for send, q in zip((*sends_1[:2], held), orders[1])])
+    held = [call(hold_kernel, f"hold_send_{i}", [sends_1[i], unread(both[0][1])], coded(2)) for i in (1, 2)]
+    got.append([swap(send, "fsdp", q) for send, q in zip((sends_1[0], *held), orders[1])])
     both.append(call(both_kernel, "both_1", [kept[1], *got[1], unread(hbm(down_codes))], [sums, coded(2)]))
     order = (1, 2, 3)
     for p in range(2):

time: 69 us -> 69.7 us (1.010)
  starting transfers between devices: 18.1 us -> 18.9 us
    ppermute x17, starting transfers between devices: 18.1 us -> 18.9 us  [swap(): lax.ppermute(x, axis, [(i, i ^ bit) for i in range(n if axis == 'fsdp' el...]
    pallas_call x15 -> x16, Pallas kernels: 12.2 us -> 12.2 us  [call(): pl.pallas_call(kernel, in_specs=specs, out_specs=jax.tree.map(lambda _: V...]
  transfers between devices with their start and end apart: 17 -> 17, of which waited for: 9 -> 10; matrix products, arithmetic and copies ran while one was open for 0% -> 0% of each run, Pallas kernels for 9% -> 9%
where the time goes in v7:
time: 69.7 us; the launch traced here: 69.5 us
  blocking collectives  27.8 us (40%)
  starting transfers between devices  18.9 us (27%)
  Pallas kernels  12.2 us (18%)
  waiting for transfers between devices  8.99 us (13%)
  between operations  1.5 us (2%)
    ppermute x17, starting transfers between devices, swap(): lax.ppermute(x, axis, [(i, i ^ bit) for i in range(n if axis == 'fsdp' el...  18.9 us
    all_to_all x1, blocking collectives, body_split(): lax.all_to_all(normed, rows_axes, 0, 0, tiled=True)  16 us
    pallas_call x16, Pallas kernels, call(): pl.pallas_call(kernel, in_specs=specs, out_specs=jax.tree.map(lambda _: V...  12.2 us
    all_to_all x1, blocking collectives, body_split(): got = lax.all_to_all(branch, rows_axes, 0, 0, tiled=True)  11.7 us
    ppermute x17, waiting for transfers between devices, swap(): lax.ppermute(x, axis, [(i, i ^ bit) for i in range(n if axis == 'fsdp' el...  8.99 us
  transfers between devices with their start and end apart: 17, of which 10 were waited for; matrix products, arithmetic and copies ran while one was open for 0% of the time, Pallas kernels for 9%

profile of v7, /device:TPU:0, one launch (start us, length us, event | category | flops | bytes accessed | tf_op | source)
XLA Modules:
  0.0 69.5 jit_solution(9214204361677261026)
XLA Ops:
  2.6 1.0 %norm.1 = (bf16[16,4,1024]{2,1,0:T(4,128)(2,1)S(1)}, f32[2,8,64]{2,1,0:T(8,128)S(1)}, f32[8,64]{1,0:T(8,128)S(1)}) custom-call(s32[4]{0:T(128)S(1)} %pad_add_fusion.place_ref, bf16[4,4096]{1,0:T(4,128)(2,1)} %tok_ref.1, bf16[4,4096]{1,0:T(4,128)(2,1)S(1)} %collective-permute-done.core_mate_ref.tok_mate_ref, bf16[8192]{0:T(1024)(128)(2,1)} %gain_ref.1, ...), custom_call_target="tpu_custom_call" | custom-call | tf_op jit(solution)/shard_map/norm/pallas_call | solution.py:213
  3.6 16.0 %all_to_all.10.got_ref = bf16[16,4,1024]{2,1,0:T(4,128)(2,1)S(1)} all-to-all(bf16[16,4,1024]{2,1,0:T(4,128)(2,1)S(1)} %hold.1), channel_id=1, replica_groups=mesh['groups'=2,'fsdp'=8,'tp'=2] {'groups','fsdp'}, dimensions={0} | all-to-all | bytes 262144 | tf_op jit(solution)/shard_map/all_to_all | solution.py:269
  19.7 2.0 %gate_up_send_0.1 = (s16[144,512]{1,0:T(8,128)(2,1)S(1)}, s16[144,512]{1,0:T(8,128)(2,1)S(1)}, s16[144,512]{1,0:T(8,128)(2,1)S(1)}) custom-call(s32[4]{0:T(128)S(1)} %pad_add_fusion.place_ref, f32[2,8,64]{2,1,0:T(8,128)S(1)} %get-tuple-element.20.scl_ref, bf16[64,1024]{1,0:T(8,128)(2,1)S(1)} %rows.1.x_ref._, bf16[1024,8192]{1,0:T(8,128)(2,1)S(1)} %copy-done, ...), custom_call_target="tpu_custom_call" | custom-call | flops 268435456 | bytes 4194304 | tf_op jit(solution)/shard_map/gate_up_send_0/pallas_call | solution.py:213
  21.7 1.2 %collective-permute-start.4 = (s16[144,512]{1,0:T(8,128)(2,1)S(1)}, s16[144,512]{1,0:T(8,128)(2,1)S(1)}, u32[]{:S(2)}, u32[]{:S(2)}) collective-permute-start(s16[144,512]{1,0:T(8,128)(2,1)S(1)} %get-tuple-element.27), channel_id=1, source_target_pairs={{0,2},{2,0},{4,6},{6,4},{8,10},{10,8},{12,14},{14,12},{1,3},{3,1},... | collective-permute-start | bytes 442376 | tf_op jit(solution)/shard_map/ppermute | solution.py:237
  23.0 2.3 %collective-permute-start.3 = (s16[144,512]{1,0:T(8,128)(2,1)S(1)}, s16[144,512]{1,0:T(8,128)(2,1)S(1)}, u32[]{:S(2)}, u32[]{:S(2)}) collective-permute-start(s16[144,512]{1,0:T(8,128)(2,1)S(1)} %get-tuple-element.22._), channel_id=1, source_target_pairs={{0,6},{2,4},{4,2},{6,0},{8,14},{10,12},{12,10},{14,8},{1,7},{3,5},... | collective-permute-start | bytes 442376 | tf_op jit(solution)/shard_map/ppermute | solution.py:237
  25.3 1.5 %gate_up_keep.1 = (f32[2,64,512]{2,1,0:T(8,128)S(1)}, f32[2,64,512]{2,1,0:T(8,128)S(1)}) custom-call(s32[4]{0:T(128)S(1)} %pad_add_fusion.place_ref, f32[2,8,64]{2,1,0:T(8,128)S(1)} %get-tuple-element.20.scl_ref, bf16[64,1024]{1,0:T(8,128)(2,1)S(1)} %rows.1.x_ref._, bf16[1024,8192]{1,0:T(8,128)(2,1)S(1)} %copy-done, bf16[1024,8192]{1,0:T(8,128)(2,1)S(1)} %copy-done.1, ...), custom_call_target="tpu_custom_call" | custom-call | flops 268435456 | bytes 4194304 | tf_op jit(solution)/shard_map/gate_up_keep/pallas_call | solution.py:213
  26.9 2.0 %gate_up_send_1.1 = (s16[144,512]{1,0:T(8,128)(2,1)S(1)}, s16[144,512]{1,0:T(8,128)(2,1)S(1)}, s16[144,512]{1,0:T(8,128)(2,1)S(1)}) custom-call(s32[4]{0:T(128)S(1)} %pad_add_fusion.place_ref, f32[2,8,64]{2,1,0:T(8,128)S(1)} %get-tuple-element.20.scl_ref, bf16[64,1024]{1,0:T(8,128)(2,1)S(1)} %rows.1.x_ref._, bf16[1024,8192]{1,0:T(8,128)(2,1)S(1)} %copy-done, ...), custom_call_target="tpu_custom_call" | custom-call | flops 268435456 | bytes 4194304 | tf_op jit(solution)/shard_map/gate_up_send_1/pallas_call | solution.py:213
  28.9 0.7 %collective-permute-start.2 = (s16[144,512]{1,0:T(8,128)(2,1)S(1)}, s16[144,512]{1,0:T(8,128)(2,1)S(1)}, u32[]{:S(2)}, u32[]{:S(2)}) collective-permute-start(s16[144,512]{1,0:T(8,128)(2,1)S(1)} %get-tuple-element.25), channel_id=1, source_target_pairs={{0,6},{2,4},{4,2},{6,0},{8,14},{10,12},{12,10},{14,8},{1,7},{3,5},... | collective-permute-start | bytes 442376 | tf_op jit(solution)/shard_map/ppermute | solution.py:237
  29.6 1.3 %collective-permute-done.3.refs_0_ = s16[144,512]{1,0:T(8,128)(2,1)S(1)} collective-permute-done((s16[144,512]{1,0:T(8,128)(2,1)S(1)}, s16[144,512]{1,0:T(8,128)(2,1)S(1)}, u32[]{:S(2)}, u32[]{:S(2)}) %collective-permute-start.3) | collective-permute-done | bytes 147488 | tf_op jit(solution)/shard_map/ppermute | solution.py:237
  31.2 1.5 %collective-permute-start.7 = (s16[144,512]{1,0:T(8,128)(2,1)S(1)}, s16[144,512]{1,0:T(8,128)(2,1)S(1)}, u32[]{:S(2)}, u32[]{:S(2)}) collective-permute-start(s16[144,512]{1,0:T(8,128)(2,1)S(1)} %hold_send_2.1), channel_id=1, source_target_pairs={{0,2},{2,0},{4,6},{6,4},{8,10},{10,8},{12,14},{14,12},{1,3},{3,1},... | collective-permute-start | bytes 442376 | tf_op jit(solution)/shard_map/ppermute | solution.py:237
  33.0 2.2 %collective-permute-start.12 = (s16[144,512]{1,0:T(8,128)(2,1)S(1)}, s16[144,512]{1,0:T(8,128)(2,1)S(1)}, u32[]{:S(2)}, u32[]{:S(2)}) collective-permute-start(s16[144,512]{1,0:T(8,128)(2,1)S(1)} %get-tuple-element.29.refs_0_), channel_id=1, source_target_pairs={{0,12},{2,14},{4,8},{6,10},{8,4},{10,6},{12,0},{14,2},{1,13},{3,15... | collective-permute-start | bytes 442376 | tf_op jit(solution)/shard_map/ppermute | solution.py:237
  35.6 1.5 %collective-permute-done.7.refs_2_ = s16[144,512]{1,0:T(8,128)(2,1)S(1)} collective-permute-done((s16[144,512]{1,0:T(8,128)(2,1)S(1)}, s16[144,512]{1,0:T(8,128)(2,1)S(1)}, u32[]{:S(2)}, u32[]{:S(2)}) %collective-permute-start.7) | collective-permute-done | bytes 147488 | tf_op jit(solution)/shard_map/ppermute | solution.py:237
  37.1 2.1 %collective-permute-done.6.refs_1_ = s16[144,512]{1,0:T(8,128)(2,1)S(1)} collective-permute-done((s16[144,512]{1,0:T(8,128)(2,1)S(1)}, s16[144,512]{1,0:T(8,128)(2,1)S(1)}, u32[]{:S(2)}, u32[]{:S(2)}) %collective-permute-start.6) | collective-permute-done | bytes 147488 | tf_op jit(solution)/shard_map/ppermute | solution.py:237
  39.3 1.7 %collective-permute-start.8 = (s16[144,512]{1,0:T(8,128)(2,1)S(1)}, s16[144,512]{1,0:T(8,128)(2,1)S(1)}, u32[]{:S(2)}, u32[]{:S(2)}) collective-permute-start(s16[144,512]{1,0:T(8,128)(2,1)S(1)} %get-tuple-element.32), channel_id=1, source_target_pairs={{0,12},{2,14},{4,8},{6,10},{8,4},{10,6},{12,0},{14,2},{1,13},{3,15... | collective-permute-start | bytes 442376 | tf_op jit(solution)/shard_map/ppermute | solution.py:237
  41.6 3.4 %collective-permute-start.15 = (bf16[2,64,256]{2,1,0:T(8,128)(2,1)S(1)}, bf16[2,64,256]{2,1,0:T(8,128)(2,1)S(1)}, u32[]{:S(2)}, u32[]{:S(2)}) collective-permute-start(bf16[2,64,256]{2,1,0:T(8,128)(2,1)S(1)} %hidden_0.1.refs_0_), channel_id=1, source_target_pairs={{0,6},{2,4},{4,2},{6,0},{8,14},{10,12},{12,10},{14,8},{1,7},{3,5},... | collective-permute-start | bytes 196616 | tf_op jit(solution)/shard_map/ppermute | solution.py:237
  45.0 1.2 %collective-permute-start.13 = (bf16[2,64,256]{2,1,0:T(8,128)(2,1)S(1)}, bf16[2,64,256]{2,1,0:T(8,128)(2,1)S(1)}, u32[]{:S(2)}, u32[]{:S(2)}) collective-permute-start(bf16[2,64,256]{2,1,0:T(8,128)(2,1)S(1)} %hidden_0.1.refs_0_), channel_id=1, source_target_pairs={{0,2},{2,0},{4,6},{6,4},{8,10},{10,8},{12,14},{14,12},{1,3},{3,1},... | collective-permute-start | bytes 196616 | tf_op jit(solution)/shard_map/ppermute | solution.py:237
  46.6 2.3 %collective-permute-start.11 = (bf16[2,64,256]{2,1,0:T(8,128)(2,1)S(1)}, bf16[2,64,256]{2,1,0:T(8,128)(2,1)S(1)}, u32[]{:S(2)}, u32[]{:S(2)}) collective-permute-start(bf16[2,64,256]{2,1,0:T(8,128)(2,1)S(1)} %hidden_1.1.refs_0_), channel_id=1, source_target_pairs={{0,6},{2,4},{4,2},{6,0},{8,14},{10,12},{12,10},{14,8},{1,7},{3,5},... | collective-permute-start | bytes 196616 | tf_op jit(solution)/shard_map/ppermute | solution.py:237
  48.9 1.2 %collective-permute-start.9 = (bf16[2,64,256]{2,1,0:T(8,128)(2,1)S(1)}, bf16[2,64,256]{2,1,0:T(8,128)(2,1)S(1)}, u32[]{:S(2)}, u32[]{:S(2)}) collective-permute-start(bf16[2,64,256]{2,1,0:T(8,128)(2,1)S(1)} %hidden_1.1.refs_0_), channel_id=1, source_target_pairs={{0,2},{2,0},{4,6},{6,4},{8,10},{10,8},{12,14},{14,12},{1,3},{3,1},... | collective-permute-start | bytes 196616 | tf_op jit(solution)/shard_map/ppermute | solution.py:237
  50.2 1.8 %down_0.1.refs_4_ = f32[1024,64]{1,0:T(8,128)S(1)} custom-call(s32[4]{0:T(128)S(1)} %pad_add_fusion.place_ref, f32[8,64]{1,0:T(8,128)S(1)} %get-tuple-element.19.scl_ref, bf16[1024,8192]{1,0:T(8,128)(2,1)S(1)} %bitcast.6, bf16[2,64,256]{2,1,0:T(8,128)(2,1)S(1)} %hidden_0.1.refs_0_, bf16[2,64,256]{2,1,0:T(8,128)(2,1)S(1)} %collective-permute-done.13.refs_1_, ...), custom_call_target="tpu_custom_call" | custom-call | flops 268435456 | bytes 4194304 | tf_op jit(solution)/shard_map/down_0/pallas_call | solution.py:213
  52.0 1.1 %collective-permute-done.10.refs_2_ = bf16[2,64,256]{2,1,0:T(8,128)(2,1)S(1)} collective-permute-done((bf16[2,64,256]{2,1,0:T(8,128)(2,1)S(1)}, bf16[2,64,256]{2,1,0:T(8,128)(2,1)S(1)}, u32[]{:S(2)}, u32[]{:S(2)}) %collective-permute-start.10) | collective-permute-done | bytes 65568 | tf_op jit(solution)/shard_map/ppermute | solution.py:237
  53.2 1.9 %down_1.1 = bf16[16,4,1024]{2,1,0:T(4,128)(2,1)S(1)} custom-call(s32[4]{0:T(128)S(1)} %pad_add_fusion.place_ref, f32[8,64]{1,0:T(8,128)S(1)} %get-tuple-element.19.scl_ref, bf16[1024,8192]{1,0:T(8,128)(2,1)S(1)} %bitcast.6, bf16[2,64,256]{2,1,0:T(8,128)(2,1)S(1)} %hidden_1.1.refs_0_, bf16[2,64,256]{2,1,0:T(8,128)(2,1)S(1)} %collective-permute-done.9.refs_1_, ...), custom_call_target="tpu_custom_call" | custom-call | flops 268435456 | bytes 4194304 | tf_op jit(solution)/shard_map/down_1/pallas_call | solution.py:213
  55.1 11.7 %all_to_all.11.got_ref = bf16[16,4,1024]{2,1,0:T(4,128)(2,1)S(1)} all-to-all(bf16[16,4,1024]{2,1,0:T(4,128)(2,1)S(1)} %down_1.1), channel_id=1, replica_groups=mesh['groups'=2,'fsdp'=8,'tp'=2] {'groups','fsdp'}, dimensions={0} | all-to-all | bytes 262144 | tf_op jit(solution)/shard_map/all_to_all | solution.py:319
  66.9 1.3 %collective-permute-done.16.branch_mate_ref = f32[8,4,1024]{2,1,0:T(4,128)S(1)} collective-permute-done((f32[8,4,1024]{2,1,0:T(4,128)S(1)}, f32[8,4,1024]{2,1,0:T(4,128)S(1)}, u32[]{:S(2)}, u32[]{:S(2)}) %collective-permute-start.16) | collective-permute-done | bytes 131104 | tf_op jit(solution)/shard_map/ppermute | solution.py:237
  68.2 1.2 %final.1 = (bf16[4,4096]{1,0:T(4,128)(2,1)}, f32[1,4]{1,0:T(1,128)}) custom-call(s32[4]{0:T(128)S(1)} %pad_add_fusion.place_ref, bf16[4,4096]{1,0:T(4,128)(2,1)S(1)} %copy-done.2, bf16[4,4096]{1,0:T(4,128)(2,1)S(1)} %collective-permute-done.core_mate_ref.tok_mate_ref, f32[8,4,1024]{2,1,0:T(4,128)S(1)} %group_sum.1.branch_ref, ...), custom_call_target="tpu_custom_call" | custom-call | tf_op jit(solution)/shard_map/final/pallas_call | solution.py:213
  (46 shorter events, 3.5 us)
Async XLA Ops:
  0.6 1.6 %collective-permute-start.1 = (f32[1,4096]{1,0:T(1,128)}, f32[1,4096]{1,0:T(1,128)S(1)}, u32[]{:S(2)}, u32[]{:S(2)}) collective-permute-start(f32[1,4096]{1,0:T(1,128)} %bitcast.7), channel_id=1, source_target_pairs={{0,1},{1,0},{2,3},{3,2},{4,5},{5,4},{6,7},{7,6},{8,9},{9,8},{10,11... | collective-permute-start | bytes 49160 | tf_op jit(solution)/shard_map/ppermute | solution.py:237
  1.1 1.4 %collective-permute-start = (bf16[4,4096]{1,0:T(4,128)(2,1)}, bf16[4,4096]{1,0:T(4,128)(2,1)S(1)}, u32[]{:S(2)}, u32[]{:S(2)}) collective-permute-start(bf16[4,4096]{1,0:T(4,128)(2,1)} %tok_ref.1), channel_id=1, source_target_pairs={{0,1},{1,0},{2,3},{3,2},{4,5},{5,4},{6,7},{7,6},{8,9},{9,8},{10,11... | collective-permute-start | bytes 98312 | tf_op jit(solution)/shard_map/ppermute | solution.py:237
  3.5 16.1 %copy-start = (bf16[1024,8192]{1,0:T(8,128)(2,1)S(1)}, bf16[1024,8192]{1,0:T(8,128)(2,1)}, u32[]{:S(2)}) copy-start(bf16[1024,8192]{1,0:T(8,128)(2,1)} %gate_ref.5) | copy-start | bytes 50331652
  3.5 16.1 %copy-start.1 = (bf16[1024,8192]{1,0:T(8,128)(2,1)S(1)}, bf16[1024,8192]{1,0:T(8,128)(2,1)}, u32[]{:S(2)}) copy-start(bf16[1024,8192]{1,0:T(8,128)(2,1)} %up_ref.5) | copy-start | bytes 50331652
  21.7 7.9 %collective-permute-start.4 = (s16[144,512]{1,0:T(8,128)(2,1)S(1)}, s16[144,512]{1,0:T(8,128)(2,1)S(1)}, u32[]{:S(2)}, u32[]{:S(2)}) collective-permute-start(s16[144,512]{1,0:T(8,128)(2,1)S(1)} %get-tuple-element.27), channel_id=1, source_target_pairs={{0,2},{2,0},{4,6},{6,4},{8,10},{10,8},{12,14},{14,12},{1,3},{3,1},... | collective-permute-start | bytes 442376 | tf_op jit(solution)/shard_map/ppermute | solution.py:237
  22.9 6.7 %collective-permute-start.5 = (s16[144,512]{1,0:T(8,128)(2,1)S(1)}, s16[144,512]{1,0:T(8,128)(2,1)S(1)}, u32[]{:S(2)}, u32[]{:S(2)}) collective-permute-start(s16[144,512]{1,0:T(8,128)(2,1)S(1)} %get-tuple-element.28), channel_id=1, source_target_pairs={{0,4},{2,6},{4,0},{6,2},{8,12},{10,14},{12,8},{14,10},{1,5},{3,7},... | collective-permute-start | bytes 442376 | tf_op jit(solution)/shard_map/ppermute | solution.py:237
  23.0 7.9 %collective-permute-start.3 = (s16[144,512]{1,0:T(8,128)(2,1)S(1)}, s16[144,512]{1,0:T(8,128)(2,1)S(1)}, u32[]{:S(2)}, u32[]{:S(2)}) collective-permute-start(s16[144,512]{1,0:T(8,128)(2,1)S(1)} %get-tuple-element.22._), channel_id=1, source_target_pairs={{0,6},{2,4},{4,2},{6,0},{8,14},{10,12},{12,10},{14,8},{1,7},{3,5},... | collective-permute-start | bytes 442376 | tf_op jit(solution)/shard_map/ppermute | solution.py:237
  26.8 23.3 %slice-start = ((s8[16777216]{0:T(1024)(128)(4,1)}), s8[4194304]{0:T(1024)(128)(4,1)S(1)}, s32[]{:S(2)}) async-start(s8[16777216]{0:T(1024)(128)(4,1)} %bitcast.5), calls=%async_computation.2 | async-start | bytes 8388608
  26.8 23.3 %slice-start.1 = ((s8[16777216]{0:T(1024)(128)(4,1)}), s8[4194304]{0:T(1024)(128)(4,1)S(1)}, s32[]{:S(2)}) async-start(s8[16777216]{0:T(1024)(128)(4,1)} %bitcast.5), calls=%async_computation.3 | async-start | bytes 8388608
  26.9 23.3 %slice-start.2 = ((s8[16777216]{0:T(1024)(128)(4,1)}), s8[4194304]{0:T(1024)(128)(4,1)S(1)}, s32[]{:S(2)}) async-start(s8[16777216]{0:T(1024)(128)(4,1)} %bitcast.5), calls=%async_computation.4 | async-start | bytes 8388608
  28.9 6.7 %collective-permute-start.2 = (s16[144,512]{1,0:T(8,128)(2,1)S(1)}, s16[144,512]{1,0:T(8,128)(2,1)S(1)}, u32[]{:S(2)}, u32[]{:S(2)}) collective-permute-start(s16[144,512]{1,0:T(8,128)(2,1)S(1)} %get-tuple-element.25), channel_id=1, source_target_pairs={{0,6},{2,4},{4,2},{6,0},{8,14},{10,12},{12,10},{14,8},{1,7},{3,5},... | collective-permute-start | bytes 442376 | tf_op jit(solution)/shard_map/ppermute | solution.py:237
  31.2 5.9 %collective-permute-start.7 = (s16[144,512]{1,0:T(8,128)(2,1)S(1)}, s16[144,512]{1,0:T(8,128)(2,1)S(1)}, u32[]{:S(2)}, u32[]{:S(2)}) collective-permute-start(s16[144,512]{1,0:T(8,128)(2,1)S(1)} %hold_send_2.1), channel_id=1, source_target_pairs={{0,2},{2,0},{4,6},{6,4},{8,10},{10,8},{12,14},{14,12},{1,3},{3,1},... | collective-permute-start | bytes 442376 | tf_op jit(solution)/shard_map/ppermute | solution.py:237
  32.7 6.5 %collective-permute-start.6 = (s16[144,512]{1,0:T(8,128)(2,1)S(1)}, s16[144,512]{1,0:T(8,128)(2,1)S(1)}, u32[]{:S(2)}, u32[]{:S(2)}) collective-permute-start(s16[144,512]{1,0:T(8,128)(2,1)S(1)} %hold_send_1.1), channel_id=1, source_target_pairs={{0,4},{2,6},{4,0},{6,2},{8,12},{10,14},{12,8},{14,10},{1,5},{3,7},... | collective-permute-start | bytes 442376 | tf_op jit(solution)/shard_map/ppermute | solution.py:237
  33.0 8.5 %collective-permute-start.12 = (s16[144,512]{1,0:T(8,128)(2,1)S(1)}, s16[144,512]{1,0:T(8,128)(2,1)S(1)}, u32[]{:S(2)}, u32[]{:S(2)}) collective-permute-start(s16[144,512]{1,0:T(8,128)(2,1)S(1)} %get-tuple-element.29.refs_0_), channel_id=1, source_target_pairs={{0,12},{2,14},{4,8},{6,10},{8,4},{10,6},{12,0},{14,2},{1,13},{3,15... | collective-permute-start | bytes 442376 | tf_op jit(solution)/shard_map/ppermute | solution.py:237
  39.3 7.1 %collective-permute-start.8 = (s16[144,512]{1,0:T(8,128)(2,1)S(1)}, s16[144,512]{1,0:T(8,128)(2,1)S(1)}, u32[]{:S(2)}, u32[]{:S(2)}) collective-permute-start(s16[144,512]{1,0:T(8,128)(2,1)S(1)} %get-tuple-element.32), channel_id=1, source_target_pairs={{0,12},{2,14},{4,8},{6,10},{8,4},{10,6},{12,0},{14,2},{1,13},{3,15... | collective-permute-start | bytes 442376 | tf_op jit(solution)/shard_map/ppermute | solution.py:237
  41.6 7.3 %collective-permute-start.15 = (bf16[2,64,256]{2,1,0:T(8,128)(2,1)S(1)}, bf16[2,64,256]{2,1,0:T(8,128)(2,1)S(1)}, u32[]{:S(2)}, u32[]{:S(2)}) collective-permute-start(bf16[2,64,256]{2,1,0:T(8,128)(2,1)S(1)} %hidden_0.1.refs_0_), channel_id=1, source_target_pairs={{0,6},{2,4},{4,2},{6,0},{8,14},{10,12},{12,10},{14,8},{1,7},{3,5},... | collective-permute-start | bytes 196616 | tf_op jit(solution)/shard_map/ppermute | solution.py:237
  45.0 5.1 %collective-permute-start.14 = (bf16[2,64,256]{2,1,0:T(8,128)(2,1)S(1)}, bf16[2,64,256]{2,1,0:T(8,128)(2,1)S(1)}, u32[]{:S(2)}, u32[]{:S(2)}) collective-permute-start(bf16[2,64,256]{2,1,0:T(8,128)(2,1)S(1)} %hidden_0.1.refs_0_), channel_id=1, source_target_pairs={{0,4},{2,6},{4,0},{6,2},{8,12},{10,14},{12,8},{14,10},{1,5},{3,7},... | collective-permute-start | bytes 196616 | tf_op jit(solution)/shard_map/ppermute | solution.py:237
  45.0 5.1 %collective-permute-start.13 = (bf16[2,64,256]{2,1,0:T(8,128)(2,1)S(1)}, bf16[2,64,256]{2,1,0:T(8,128)(2,1)S(1)}, u32[]{:S(2)}, u32[]{:S(2)}) collective-permute-start(bf16[2,64,256]{2,1,0:T(8,128)(2,1)S(1)} %hidden_0.1.refs_0_), channel_id=1, source_target_pairs={{0,2},{2,0},{4,6},{6,4},{8,10},{10,8},{12,14},{14,12},{1,3},{3,1},... | collective-permute-start | bytes 196616 | tf_op jit(solution)/shard_map/ppermute | solution.py:237
  46.6 5.5 %collective-permute-start.11 = (bf16[2,64,256]{2,1,0:T(8,128)(2,1)S(1)}, bf16[2,64,256]{2,1,0:T(8,128)(2,1)S(1)}, u32[]{:S(2)}, u32[]{:S(2)}) collective-permute-start(bf16[2,64,256]{2,1,0:T(8,128)(2,1)S(1)} %hidden_1.1.refs_0_), channel_id=1, source_target_pairs={{0,6},{2,4},{4,2},{6,0},{8,14},{10,12},{12,10},{14,8},{1,7},{3,5},... | collective-permute-start | bytes 196616 | tf_op jit(solution)/shard_map/ppermute | solution.py:237
  48.9 4.3 %collective-permute-start.10 = (bf16[2,64,256]{2,1,0:T(8,128)(2,1)S(1)}, bf16[2,64,256]{2,1,0:T(8,128)(2,1)S(1)}, u32[]{:S(2)}, u32[]{:S(2)}) collective-permute-start(bf16[2,64,256]{2,1,0:T(8,128)(2,1)S(1)} %hidden_1.1.refs_0_), channel_id=1, source_target_pairs={{0,4},{2,6},{4,0},{6,2},{8,12},{10,14},{12,8},{14,10},{1,5},{3,7},... | collective-permute-start | bytes 196616 | tf_op jit(solution)/shard_map/ppermute | solution.py:237
  48.9 4.3 %collective-permute-start.9 = (bf16[2,64,256]{2,1,0:T(8,128)(2,1)S(1)}, bf16[2,64,256]{2,1,0:T(8,128)(2,1)S(1)}, u32[]{:S(2)}, u32[]{:S(2)}) collective-permute-start(bf16[2,64,256]{2,1,0:T(8,128)(2,1)S(1)} %hidden_1.1.refs_0_), channel_id=1, source_target_pairs={{0,2},{2,0},{4,6},{6,4},{8,10},{10,8},{12,14},{14,12},{1,3},{3,1},... | collective-permute-start | bytes 196616 | tf_op jit(solution)/shard_map/ppermute | solution.py:237
  50.2 18.1 %copy-start.2 = (bf16[4,4096]{1,0:T(4,128)(2,1)S(1)}, bf16[4,4096]{1,0:T(4,128)(2,1)}, u32[]{:S(2)}) copy-start(bf16[4,4096]{1,0:T(4,128)(2,1)} %tok_ref.1) | copy-start | bytes 98308
  50.2 18.1 %copy-start.3 = (f32[4096]{0:T(1024)S(1)}, f32[4096]{0:T(1024)}, u32[]{:S(2)}) copy-start(f32[4096]{0:T(1024)} %param.19) | copy-start | bytes 49156
  66.8 1.4 %collective-permute-start.16 = (f32[8,4,1024]{2,1,0:T(4,128)S(1)}, f32[8,4,1024]{2,1,0:T(4,128)S(1)}, u32[]{:S(2)}, u32[]{:S(2)}) collective-permute-start(f32[8,4,1024]{2,1,0:T(4,128)S(1)} %group_sum.1.branch_ref), channel_id=1, source_target_pairs={{0,1},{1,0},{2,3},{3,2},{4,5},{5,4},{6,7},{7,6},{8,9},{9,8},{10,11... | collective-permute-start | bytes 393224 | tf_op jit(solution)/shard_map/ppermute | solution.py:237
  (1 other events, 11.0 us)
